TPU v7x, 512 devices: a whole 4x8x8 slice. The times are simulated.
512 devices in a mesh: vol: 8 (over x, core), chan: 64 (over y, z).
Axes of the slice: x: 4, y: 8, z: 8, core: 2. Of those that a mesh axis runs over, the one named last changes fastest.
Arguments:
- fwd_input: bfloat16 [8, 256, 12288], P('vol', None, 'chan'), may hold values from 0 to 72, as said below
- weight_one: bfloat16 [27, 256, 256], P(None, 'chan'), may hold values from -0.078125 to 0.078125
- gain_one: float32 [256], P('chan'), may hold values from 0.25 to 1.75
- bias_one: float32 [256], P('chan'), may hold values from -0.5 to 0.5
- saved_conv: bfloat16 [8, 256, 12288], P('vol', 'chan'), may hold values from -39 to 39
- cotangent: bfloat16 [8, 256, 12288], P('vol', 'chan'), may hold values from -26 to 26
- saved_input: bfloat16 [8, 256, 12288], P('vol', 'chan'), may hold values from 0 to 72, as said below
- weight_two: bfloat16 [27, 256, 256], P(None, None, 'chan'), may hold values from -0.078125 to 0.078125
- gain_two: float32 [256], P('chan'), may hold values from 0.25 to 1.75
Outputs:
- activation: bfloat16 [8, 256, 12288], P('vol', 'chan')
- input_grad: bfloat16 [8, 256, 12288], P('vol', 'chan')
- weight_grad: float32 [27, 256, 256], P(None, 'vol', 'chan')
- gain_grad: float32 [256], P('chan')
- shift_grad: float32 [256], P('chan')
Inputs may be any that keep to these rules, and one draw needn't show every extreme that they name: `fwd_input`: input activations are never negative. `saved_input`: input activations are never negative.
All inputs are finite; a program needn't handle non-finite values.
Results may differ from a plain program's by a relative error of at most 0.02.
Values may be sent and summed in bfloat16 or wider, within the bound.
No kernel may reach another device: no remote copies, remote signals or barrier semaphores. Data moves between devices by JAX's collectives and lax.ppermute only.
A program may use at most 192 MiB of HBM per device.

v0:
```python
import math

import jax
import jax.numpy as jnp
from jax import lax
from jax.experimental import pallas as pl
from jax.experimental.pallas import tpu as pltpu
from jax.sharding import Mesh
from jax.sharding import PartitionSpec as P

PLANE = 1024
BLOCK = 1536
EDGE = 128
REACH = PLANE + EDGE
SPAN = BLOCK + 2 * REACH
CELLS = 12288
NY = 8
NZ = 8
OWN = 4
GROUP = NY * OWN
CH = 256
ROWS = 27 * GROUP
EPSILON = 1e-05
F32 = jnp.float32
BF16 = jnp.bfloat16

VMEM = pl.BlockSpec(memory_space=pltpu.VMEM)
SMEM = pl.BlockSpec(memory_space=pltpu.SMEM)
PARAMS = pltpu.CompilerParams(vmem_limit_bytes=40 * 1024 * 1024)


def iota(shape, axis):
    return lax.broadcasted_iota(jnp.int32, shape, axis)


def shift(value, amount):
    lanes = value.shape[1]
    return pltpu.roll(value, (-amount) % lanes, 1)


def nt_dot(left, right):
    return lax.dot_general(left, right, (((1,), (1,)), ((), ())), preferred_element_type=F32)


def spread(base, terms, out_ref, sign):
    def rows(group, carry):
        lane = iota((8, BLOCK), 1)
        along_x = lane & 31
        along_y = lax.shift_right_logical(lane + base, 5) & 31
        ends = {1: along_x >= 1, -1: along_x <= 30}
        sides = {1: along_y >= 1, -1: along_y <= 30}
        margin = jnp.zeros((8, EDGE), F32)
        by_plane = {}
        for a in (-1, 0, 1):
            total = None
            for b in (-1, 0, 1):
                line = None
                for c in (-1, 0, 1):
                    index = 9 * (a + 1) + 3 * (b + 1) + (c + 1)
                    term = terms[pl.ds(pl.multiple_of(index * GROUP + group * 8, 8), 8), :]
                    if c != 0:
                        term = shift(jnp.where(ends[sign * c], term, 0.0), sign * c)
                    line = term if line is None else line + term
                if b != 0:
                    line = jnp.where(sides[sign * b], line, 0.0)
                line = jnp.concatenate([margin, line, margin], axis=1)
                if b != 0:
                    line = shift(line, sign * b * 32)
                total = line if total is None else total + line
            by_plane[sign * a] = total
        low, mid, high = by_plane[1], by_plane[0], by_plane[-1]
        pieces = (
            (0, low[:, :1024]),
            (1024, low[:, 1024:] + mid[:, :768]),
            (1792, mid[:, 768:1024]),
            (2048, mid[:, 1024:] + high[:, :768]),
            (2816, high[:, 768:]),
        )
        for start, piece in pieces:
            stop = start + piece.shape[1]
            out_ref[2 * group, :, start:stop] = piece[:OWN].astype(out_ref.dtype)
            out_ref[2 * group + 1, :, start:stop] = piece[OWN:].astype(out_ref.dtype)
        return carry

    lax.fori_loop(0, GROUP // 8, rows, 0)


def forward_kernel(base_ref, weight_ref, cells_ref, out_ref, terms):
    def columns(step, carry):
        part = pl.ds(pl.multiple_of(step * 256, 256), 256)
        terms[:, part] = nt_dot(weight_ref[...], cells_ref[part, :])
        return carry

    lax.fori_loop(0, BLOCK // 256, columns, 0)
    spread(base_ref[0], terms, out_ref, 1)


def natural_rows(grads_ref, natural):
    to, of = iota((CH, CH), 0), iota((CH, CH), 1)
    same = (
        (lax.shift_right_logical(to, 5) == (lax.shift_right_logical(of, 2) & 7))
        & ((lax.shift_right_logical(to, 2) & 7) == lax.shift_right_logical(of, 5))
        & ((to & 3) == (of & 3))
    )
    select = jnp.where(same, 1.0, 0.0).astype(BF16)

    def columns(step, carry):
        part = pl.ds(pl.multiple_of(step * 256, 256), 256)
        natural[:, part] = jnp.dot(
            select, grads_ref[:, part], preferred_element_type=F32
        ).astype(BF16)
        return carry

    lax.fori_loop(0, BLOCK // 256, columns, 0)


def backward_kernel(base_ref, weight_ref, grads_ref, out_ref, natural, terms):
    natural_rows(grads_ref, natural)

    def columns(step, carry):
        part = pl.ds(pl.multiple_of(step * 256, 256), 256)
        terms[:, part] = jnp.dot(
            weight_ref[...], natural[:, part], preferred_element_type=F32
        )
        return carry

    lax.fori_loop(0, BLOCK // 256, columns, 0)
    spread(base_ref[0], terms, out_ref, -1)


def filter_kernel(base_ref, grads_ref, acts_ref, out_ref, natural, copies, product):
    natural_rows(grads_ref, natural)
    base = base_ref[0]

    def rows(group, carry):
        lane = iota((16, SPAN), 1)
        along_x = lane & 31
        along_y = lax.shift_right_logical(lane + (base + 2 * PLANE - REACH), 5) & 31
        first = pl.multiple_of(group * 16, 16)
        acts = acts_ref[pl.ds(first, 16), :].astype(F32)
        ends = {1: along_x <= 30, -1: along_x >= 1}
        sides = {1: along_y <= 30, -1: along_y >= 1}
        for b in (-1, 0, 1):
            for c in (-1, 0, 1):
                moved = acts
                if b != 0 or c != 0:
                    moved = shift(acts, 32 * b + c)
                if c != 0:
                    moved = jnp.where(ends[c], moved, 0.0)
                if b != 0:
                    moved = jnp.where(sides[b], moved, 0.0)
                moved = moved.astype(BF16)
                for a in (-1, 0, 1):
                    index = 9 * (a + 1) + 3 * (b + 1) + (c + 1)
                    start = REACH + PLANE * a
                    copies[pl.ds(index * GROUP + first, 16), :] = moved[:, start : start + BLOCK]
        return carry

    lax.fori_loop(0, GROUP // 16, rows, 0)
    copies[ROWS:, :] = jnp.zeros((1024 - ROWS, BLOCK), BF16)

    def offsets(step, carry):
        part = pl.ds(pl.multiple_of(step * 256, 256), 256)
        product[:, part] = nt_dot(natural[...], copies[part, :]).astype(BF16)
        return carry

    lax.fori_loop(0, 4, offsets, 0)

    def owners(step, carry):
        of = iota((1024, 256), 0)
        to = iota((1024, 256), 1)
        same = (
            (2 * step + lax.shift_right_logical(to, 7)) == (lax.shift_right_logical(of, 2) & 7)
        ) & ((to & 127) == (lax.shift_right_logical(of, 5) * 4 + (of & 3)))
        select = jnp.where(same, 1.0, 0.0).astype(BF16)
        placed = jnp.dot(product[...], select, preferred_element_type=F32).astype(BF16)
        for vol in range(8):
            for half in range(2):
                out_ref[vol, 2 * step + half] = placed[
                    32 * vol : 32 * vol + 32, 128 * half : 128 * half + 128
                ]
        return carry

    lax.fori_loop(0, 4, owners, 0)


def lane_sum(value):
    parts = value[:, :128]
    for start in range(128, value.shape[1], 128):
        parts = parts + value[:, start : start + 128]
    return jnp.broadcast_to(jnp.sum(parts, axis=1, keepdims=True), (value.shape[0], 128))


def prepare_kernel(saved_ref, upstream_ref, acts_ref, sums_ref, packed_ref):
    saved = saved_ref[...].astype(F32)
    upstream = upstream_ref[...].astype(F32)
    sums_ref[0] = lane_sum(saved)
    sums_ref[1] = lane_sum(saved * saved)
    sums_ref[2] = lane_sum(upstream)
    sums_ref[3] = lane_sum(upstream * saved)
    for block in range(NY):
        start = block * BLOCK - REACH
        low, high = max(start, 0), min(start + SPAN, CELLS)
        packed_ref[block, :, low - start : high - start] = acts_ref[:, low:high]
        if low > start:
            packed_ref[block, :, : low - start] = jnp.zeros((OWN, low - start), BF16)
        if high < start + SPAN:
            packed_ref[block, :, high - start :] = jnp.zeros((OWN, start + SPAN - high), BF16)


def grad_kernel(counted, saved_ref, upstream_ref, sums_ref, params_ref, packed_ref, means_ref):
    mean = sums_ref[0] / counted
    var = sums_ref[1] / counted - mean * mean
    inverse = lax.rsqrt(var + EPSILON)
    shift_grad = sums_ref[2] / counted
    gain_grad = (sums_ref[3] / counted - mean * shift_grad) * inverse
    means_ref[0] = gain_grad
    means_ref[1] = shift_grad
    scale = (params_ref[2] * inverse)[:, :1]
    mean, inverse = mean[:, :1], inverse[:, :1]
    shift_grad, gain_grad = shift_grad[:, :1], gain_grad[:, :1]
    for block in range(NY):
        part = slice(block * BLOCK, (block + 1) * BLOCK)
        normed = (saved_ref[:, part].astype(F32) - mean) * inverse
        upstream = upstream_ref[:, part].astype(F32)
        packed_ref[block] = (scale * (upstream - shift_grad - normed * gain_grad)).astype(BF16)


def joined(parts_ref, block):
    whole = parts_ref[block, :, REACH : REACH + BLOCK].astype(F32)
    pieces = [whole[:, :384], whole[:, 384:REACH], whole[:, REACH:]]
    if block > 0:
        before = parts_ref[block - 1, :, REACH + BLOCK :].astype(F32)
        pieces[0] = pieces[0] + before[:, :384]
        pieces[1] = pieces[1] + before[:, 384:]
    if block < NY - 1:
        after = parts_ref[block + 1, :, :REACH].astype(F32)
        pieces[1] = pieces[1] + after[:, : REACH - 384]
        pieces[2] = pieces[2] + after[:, REACH - 384 :]
    return jnp.concatenate(pieces, axis=1)


def join_stats_kernel(parts_ref, out_ref, sums_ref):
    total = jnp.zeros((OWN, 128), F32)
    squares = jnp.zeros((OWN, 128), F32)
    for block in range(NY):
        cells = joined(parts_ref, block)
        out_ref[:, block * BLOCK : (block + 1) * BLOCK] = cells
        total = total + lane_sum(cells)
        squares = squares + lane_sum(cells * cells)
    sums_ref[0] = total
    sums_ref[1] = squares


def join_kernel(parts_ref, out_ref):
    for block in range(NY):
        out_ref[:, block * BLOCK : (block + 1) * BLOCK] = joined(parts_ref, block).astype(BF16)


def relu_kernel(counted, conv_ref, sums_ref, params_ref, out_ref):
    mean = sums_ref[0] / counted
    var = sums_ref[1] / counted - mean * mean
    scale = (params_ref[0] * lax.rsqrt(var + EPSILON))[:, :1]
    mean, bias = mean[:, :1], params_ref[1][:, :1]
    out_ref[...] = jnp.maximum((conv_ref[...] - mean) * scale + bias, 0.0).astype(BF16)


def shaped(shape, dtype):
    return jax.ShapeDtypeStruct(shape, dtype)


def call(kernel, outs, specs, scratch=(), flops=0, moved=0):
    return pl.pallas_call(
        kernel,
        out_shape=outs,
        in_specs=specs,
        out_specs=jax.tree.map(lambda _: VMEM, outs),
        scratch_shapes=list(scratch),
        compiler_params=PARAMS,
        cost_estimate=pl.CostEstimate(flops=flops, bytes_accessed=moved, transcendentals=0),
    )


def shards(
    fwd_input,
    weight_one,
    gain_one,
    bias_one,
    saved_conv,
    cotangent,
    saved_input,
    weight_two,
    gain_two,
):
    counted = lax.axis_size("vol") * CELLS
    matmul = 2 * ROWS * CH * BLOCK
    base = (lax.axis_index("y") * BLOCK).astype(jnp.int32).reshape(1)
    params = jnp.broadcast_to(
        jnp.stack([gain_one, bias_one, gain_two])[:, :, None], (3, OWN, 128)
    )

    cells = lax.all_gather(fwd_input[0].T, "z", axis=0, tiled=True)
    both = jnp.stack([weight_one, jnp.transpose(weight_two, (0, 2, 1))])
    both = lax.all_gather(both, "y", axis=0, tiled=False)
    both = jnp.transpose(both, (1, 2, 0, 3, 4)).reshape(2, ROWS, CH)

    saved, upstream = saved_conv[0], cotangent[0]
    sums_two, acts = call(
        prepare_kernel,
        (shaped((4, OWN, 128), F32), shaped((NY, OWN, SPAN), BF16)),
        [VMEM] * 3,
        moved=600000,
    )(saved, upstream, saved_input[0])
    acts = lax.all_to_all(acts, "y", 0, 0, tiled=True).reshape(GROUP, SPAN)
    sums_two = lax.psum(sums_two, "vol")
    grads, means = call(
        lambda *refs: grad_kernel(counted, *refs),
        (shaped((NY, OWN, BLOCK), BF16), shaped((2, OWN, 128), F32)),
        [VMEM] * 4,
        moved=300000,
    )(saved, upstream, sums_two, params)
    grads = lax.all_to_all(grads, "y", 0, 0, tiled=True).reshape(GROUP, BLOCK)
    grads = lax.all_gather(grads, "z", axis=0, tiled=True)

    cells, sums_two = lax.optimization_barrier((cells, sums_two))
    conv_parts = call(
        forward_kernel,
        shaped((NY, OWN, SPAN), F32),
        [SMEM, VMEM, VMEM],
        [pltpu.VMEM((ROWS, BLOCK), F32)],
        flops=matmul,
        moved=10000000,
    )(base, both[0], cells)
    conv_parts = lax.all_to_all(conv_parts, "y", 0, 0, tiled=True)
    conv_out, sums_one = call(
        join_stats_kernel,
        (shaped((OWN, CELLS), F32), shaped((2, OWN, 128), F32)),
        [VMEM],
        moved=700000,
    )(conv_parts)
    sums_one = lax.psum(sums_one, "vol")
    sums_one, grads = lax.optimization_barrier((sums_one, grads))
    activation = call(
        lambda *refs: relu_kernel(counted, *refs),
        shaped((OWN, CELLS), BF16),
        [VMEM] * 3,
        moved=300000,
    )(conv_out, sums_one, params)

    filter_parts = call(
        filter_kernel,
        shaped((8, NY, GROUP, 128), BF16),
        [SMEM, VMEM, VMEM],
        [
            pltpu.VMEM((CH, BLOCK), BF16),
            pltpu.VMEM((1024, BLOCK), BF16),
            pltpu.VMEM((CH, 1024), BF16),
        ],
        flops=2 * matmul,
        moved=10000000,
    )(base, grads, acts)
    filter_parts = lax.all_to_all(
        filter_parts.reshape(8 * NY, GROUP, 128), ("vol", "y"), 0, 0, tiled=True
    )

    input_parts = call(
        backward_kernel,
        shaped((NY, OWN, SPAN), BF16),
        [SMEM, VMEM, VMEM],
        [pltpu.VMEM((CH, BLOCK), BF16), pltpu.VMEM((ROWS, BLOCK), F32)],
        flops=matmul,
        moved=10000000,
    )(base, both[1], grads)
    input_parts = lax.all_to_all(input_parts, "y", 0, 0, tiled=True)
    input_grad = call(join_kernel, shaped((OWN, CELLS), BF16), [VMEM], moved=350000)(input_parts)

    summed = jnp.sum(filter_parts.astype(F32), axis=0) / math.sqrt(counted)
    weight_grad = jnp.transpose(summed[:, : 27 * OWN].reshape(GROUP, 27, OWN), (1, 0, 2))
    return (activation[None], input_grad[None], weight_grad, means[0, :, 0], means[1, :, 0])


def solution(mesh):
    cut = Mesh(mesh.devices.reshape(mesh.devices.shape[0], NY, NZ), ("vol", "y", "z"))
    chan = ("y", "z")
    return jax.shard_map(
        shards,
        mesh=cut,
        in_specs=(
            P("vol", None, chan),
            P(None, chan, None),
            P(chan),
            P(chan),
            P("vol", chan, None),
            P("vol", chan, None),
            P("vol", chan, None),
            P(None, None, chan),
            P(chan),
        ),
        out_specs=(
            P("vol", chan, None),
            P("vol", chan, None),
            P(None, "vol", chan),
            P(chan),
            P(chan),
        ),
        check_vma=False,
    )
```

profile of v0, /device:TPU:1, one launch (start us, length us, event | category | flops | bytes accessed | tf_op | source)
XLA Modules:
  0.0 205.4 jit_solution(16580516781267540871)
XLA Ops:
  0.6 0.0 copy-start
  0.6 0.9 copy-done
  1.5 0.0 copy-start.2
  1.5 0.9 copy-done.2
  2.4 0.0 copy-start.4
  2.4 0.9 copy-done.4
  3.3 0.0 copy-start.1
  3.3 0.0 copy-start.3
  3.3 0.8 shard_map.128
  4.1 18.8 %psum.14.refs_2_ = f32[4,4,128]{2,1,0:T(4,128)S(1)} all-reduce(f32[4,4,128]{2,1,0:T(4,128)S(1)} %get-tuple-element.14), channel_id=1, replica_groups=mesh['vol'=8,'y'=8,'z'=8] {'vol'}, use_global_device_ids=true, to_apply=%region_0.0 | all-reduce | flops 2048 | bytes 16384 | tf_op jit(solution)/shard_map/psum | solution.py:315
  23.0 0.0 copy-start.8
  23.0 0.0 copy-start.9
  23.0 0.0 copy-start.10
  23.0 0.6 copy-done.8
  23.6 0.0 copy-done.9
  23.7 0.0 copy-done.10
  23.7 0.1 broadcast_in_dim.12.refs_3_.refs_2_
  23.8 0.0 copy-done.1
  23.8 0.0 copy-done.3
  23.8 0.8 shard_map.131
  24.6 0.0 copy-start.6
  24.6 0.0 copy-start.7
  24.6 3.5 %all-to-all-start.1 = ((bf16[8,4,1536]{2,1,0:T(4,128)(2,1)}), bf16[8,4,1536]{2,1,0:T(4,128)(2,1)S(1)}, u32[]{:S(2)}, u32[]{:S(2)}) async-start(bf16[8,4,1536]{2,1,0:T(4,128)(2,1)} %get-tuple-element.18), calls=%async_computation.1 | async-start | bytes 196608 | tf_op jit(solution)/shard_map/all_to_all | solution.py:322
  28.1 0.0 copy-done.6
  28.1 0.0 copy-done.7
  28.1 0.1 pad_maximum_fusion
  28.2 22.6 %all-gather = bf16[16,27,4,256]{3,2,1,0:T(4,128)(2,1)S(1)} all-gather(bf16[2,27,4,256]{3,2,1,0:T(4,128)(2,1)S(1)} %pad_maximum_fusion), channel_id=2, replica_groups=mesh['vol'=8,'y'=8,'z'=8] {'y'}, dimensions={0}, use_global_device_ids=true | all-gather | bytes 995328 | tf_op jit(solution)/shard_map/all_gather | solution.py:304
  50.8 0.0 copy-start.5
  50.8 0.5 copy.19
  51.3 0.4 copy-done.5
  51.7 25.5 %all_gather.14.cells_ref = bf16[1536,256]{1,0:T(8,128)(2,1)S(1)} all-gather(bf16[192,256]{1,0:T(8,128)(2,1)S(1)} %bitcast.31), channel_id=1, replica_groups=mesh['vol'=8,'y'=8,'z'=8] {'z'}, dimensions={0}, use_global_device_ids=true | all-gather | bytes 884736 | tf_op jit(solution)/shard_map/all_gather | solution.py:302
  77.1 0.4 fusion
  77.5 0.1 squeeze.24.weight_ref
  77.7 4.4 %shard_map.129 = f32[8,4,3840]{2,1,0:T(4,128)S(1)} custom-call(s32[1]{0:T(128)} %bitcast.base_ref, bf16[864,256]{1,0:T(8,128)(2,1)S(1)} %squeeze.24.weight_ref, bf16[1536,256]{1,0:T(8,128)(2,1)S(1)} %all_gather.14.cells_ref), custom_call_target="tpu_custom_call" | custom-call | flops 679477248 | bytes 10000000 | tf_op jit(solution)/shard_map/pallas_call | solution.py:326
  82.1 0.0 all-to-all-done.1
  82.1 17.0 %all_to_all.25.parts_ref = f32[8,4,3840]{2,1,0:T(4,128)S(1)} all-to-all(f32[8,4,3840]{2,1,0:T(4,128)S(1)} %shard_map.129), channel_id=1, replica_groups=mesh['vol'=8,'y'=8,'z'=8] {'y'}, dimensions={0} | all-to-all | bytes 983040 | tf_op jit(solution)/shard_map/all_to_all | solution.py:334
  99.1 3.4 %all-to-all-start.3 = ((bf16[8,4,3840]{2,1,0:T(4,128)(2,1)}), bf16[8,4,3840]{2,1,0:T(4,128)(2,1)S(1)}, u32[]{:S(2)}, u32[]{:S(2)}) async-start(bf16[8,4,3840]{2,1,0:T(4,128)(2,1)} %get-tuple-element.21), calls=%async_computation.3 | async-start | bytes 491520 | tf_op jit(solution)/shard_map/all_to_all | solution.py:314
  102.5 0.1 squeeze.29.weight_ref
  102.7 20.6 %all_gather.15.grads_ref = bf16[256,1536]{1,0:T(8,128)(2,1)S(1)} all-gather(bf16[32,1536]{1,0:T(8,128)(2,1)S(1)} %reshape.32), channel_id=1, replica_groups=mesh['vol'=8,'y'=8,'z'=8] {'z'}, dimensions={0}, use_global_device_ids=true | all-gather | bytes 884736 | tf_op jit(solution)/shard_map/all_gather | solution.py:323
  123.2 0.2 shard_map.130
  123.4 34.5 %psum.15.refs_1_ = f32[2,4,128]{2,1,0:T(4,128)S(1)} all-reduce(f32[2,4,128]{2,1,0:T(4,128)S(1)} %get-tuple-element.17), channel_id=1, replica_groups=mesh['vol'=8,'y'=8,'z'=8] {'vol'}, use_global_device_ids=true, to_apply=%region_1.0 | all-reduce | flops 1024 | bytes 8192 | tf_op jit(solution)/shard_map/psum | solution.py:341
  157.8 6.1 %shard_map.133 = bf16[8,4,3840]{2,1,0:T(4,128)(2,1)} custom-call(s32[1]{0:T(128)} %bitcast.base_ref, bf16[864,256]{1,0:T(8,128)(2,1)S(1)} %squeeze.29.weight_ref, bf16[256,1536]{1,0:T(8,128)(2,1)S(1)} %all_gather.15.grads_ref), custom_call_target="tpu_custom_call" | custom-call | flops 679477248 | bytes 10000000 | tf_op jit(solution)/shard_map/pallas_call | solution.py:366
  164.0 0.0 all-to-all-done.3
  164.0 6.8 %all-to-all-start.2 = ((bf16[8,4,3840]{2,1,0:T(4,128)(2,1)}), bf16[8,4,3840]{2,1,0:T(4,128)(2,1)S(1)}, u32[]{:S(2)}, u32[]{:S(2)}) async-start(bf16[8,4,3840]{2,1,0:T(4,128)(2,1)} %shard_map.133), calls=%async_computation.2 | async-start | bytes 491520 | tf_op jit(solution)/shard_map/all_to_all | solution.py:374
  170.8 0.1 reshape.33.acts_ref
  170.8 6.1 %shard_map.135 = bf16[8,8,32,128]{3,2,1,0:T(8,128)(2,1)} custom-call(s32[1]{0:T(128)} %bitcast.base_ref, bf16[256,1536]{1,0:T(8,128)(2,1)S(1)} %all_gather.15.grads_ref, bf16[32,3840]{1,0:T(8,128)(2,1)S(1)} %reshape.33.acts_ref), custom_call_target="tpu_custom_call" | custom-call | flops 1358954496 | bytes 10000000 | tf_op jit(solution)/shard_map/pallas_call | solution.py:350
  176.9 3.9 %all-to-all-done.2.parts_ref = bf16[8,4,3840]{2,1,0:T(4,128)(2,1)S(1)} async-done(((bf16[8,4,3840]{2,1,0:T(4,128)(2,1)}), bf16[8,4,3840]{2,1,0:T(4,128)(2,1)S(1)}, u32[]{:S(2)}, u32[]{:S(2)}) %all-to-all-start.2) | async-done | bytes 245792 | tf_op jit(solution)/shard_map/all_to_all | solution.py:374
  180.8 6.6 %all-to-all-start.4 = ((bf16[64,32,128]{2,1,0:T(8,128)(2,1)}), bf16[64,32,128]{2,1,0:T(8,128)(2,1)S(1)}, u32[]{:S(2)}, u32[]{:S(2)}) async-start(bf16[64,32,128]{2,1,0:T(8,128)(2,1)} %bitcast.16), calls=%async_computation.4 | async-start | bytes 1048576 | tf_op jit(solution)/shard_map/all_to_all | solution.py:362
  187.4 0.7 slice_reduce_fusion
  188.0 0.8 shard_map.132
  188.8 0.7 shard_map.134
  189.5 15.0 %all-to-all-done.4 = bf16[64,32,128]{2,1,0:T(8,128)(2,1)S(1)} async-done(((bf16[64,32,128]{2,1,0:T(8,128)(2,1)}), bf16[64,32,128]{2,1,0:T(8,128)(2,1)S(1)}, u32[]{:S(2)}, u32[]{:S(2)}) %all-to-all-start.4) | async-done | bytes 524320 | tf_op jit(solution)/shard_map/all_to_all | solution.py:362
  204.5 0.1 convert_reduce_fusion
  204.7 0.1 copy.17
  204.8 0.6 reshape.35
  (3 shorter events, 0.0 us)
Async XLA Ops:
  0.6 0.9 copy-start
  1.5 0.9 copy-start.2
  2.4 0.9 copy-start.4
  3.3 20.4 %copy-start.1 = (bf16[1,4,12288]{2,1,0:T(4,128)(2,1)S(1)}, bf16[1,4,12288]{2,1,0:T(4,128)(2,1)}, u32[]{:S(2)}) copy-start(bf16[1,4,12288]{2,1,0:T(4,128)(2,1)} %param.13) | copy-start | bytes 294916
  3.3 20.4 %copy-start.3 = (bf16[1,4,12288]{2,1,0:T(4,128)(2,1)S(1)}, bf16[1,4,12288]{2,1,0:T(4,128)(2,1)}, u32[]{:S(2)}) copy-start(bf16[1,4,12288]{2,1,0:T(4,128)(2,1)} %param.14) | copy-start | bytes 294916
  23.0 0.7 copy-start.8
  23.0 0.7 copy-start.9
  23.0 0.7 copy-start.10
  24.6 3.5 %copy-start.6 = (bf16[27,256,4]{1,2,0:T(4,128)(2,1)S(1)}, bf16[27,256,4]{1,2,0:T(4,128)(2,1)}, u32[]{:S(2)}) copy-start(bf16[27,256,4]{1,2,0:T(4,128)(2,1)} %param.16) | copy-start | bytes 165892
  24.6 3.5 %copy-start.7 = (bf16[27,4,256]{2,1,0:T(4,128)(2,1)S(1)}, bf16[27,4,256]{2,1,0:T(4,128)(2,1)}, u32[]{:S(2)}) copy-start(bf16[27,4,256]{2,1,0:T(4,128)(2,1)} %param.10) | copy-start | bytes 165892
  24.6 57.6 %all-to-all-start.1 = ((bf16[8,4,1536]{2,1,0:T(4,128)(2,1)}), bf16[8,4,1536]{2,1,0:T(4,128)(2,1)S(1)}, u32[]{:S(2)}, u32[]{:S(2)}) async-start(bf16[8,4,1536]{2,1,0:T(4,128)(2,1)} %get-tuple-element.18), calls=%async_computation.1 | async-start | bytes 196608 | tf_op jit(solution)/shard_map/all_to_all | solution.py:322
  50.8 0.9 copy-start.5
  99.1 64.9 %all-to-all-start.3 = ((bf16[8,4,3840]{2,1,0:T(4,128)(2,1)}), bf16[8,4,3840]{2,1,0:T(4,128)(2,1)S(1)}, u32[]{:S(2)}, u32[]{:S(2)}) async-start(bf16[8,4,3840]{2,1,0:T(4,128)(2,1)} %get-tuple-element.21), calls=%async_computation.3 | async-start | bytes 491520 | tf_op jit(solution)/shard_map/all_to_all | solution.py:314
  164.0 16.8 %all-to-all-start.2 = ((bf16[8,4,3840]{2,1,0:T(4,128)(2,1)}), bf16[8,4,3840]{2,1,0:T(4,128)(2,1)S(1)}, u32[]{:S(2)}, u32[]{:S(2)}) async-start(bf16[8,4,3840]{2,1,0:T(4,128)(2,1)} %shard_map.133), calls=%async_computation.2 | async-start | bytes 491520 | tf_op jit(solution)/shard_map/all_to_all | solution.py:374
  180.8 23.8 %all-to-all-start.4 = ((bf16[64,32,128]{2,1,0:T(8,128)(2,1)}), bf16[64,32,128]{2,1,0:T(8,128)(2,1)S(1)}, u32[]{:S(2)}, u32[]{:S(2)}) async-start(bf16[64,32,128]{2,1,0:T(8,128)(2,1)} %bitcast.16), calls=%async_computation.4 | async-start | bytes 1048576 | tf_op jit(solution)/shard_map/all_to_all | solution.py:362
where the time goes:
time: 206 us; the launch traced here: 205 us
  blocking collectives  139 us (67%)
  starting transfers between devices  20.3 us (10%)
  Pallas kernels  19.8 us (10%)
  waiting for transfers between devices  18.9 us (9%)
  local copies, waits for them, and re-layouts  6.41 us (3%)
    psum x1, blocking collectives, shards(): sums_one = lax.psum(sums_one, 'vol')  34.5 us
    all_gather x1, blocking collectives, shards(): cells = lax.all_gather(fwd_input[0].T, 'z', axis=0, tiled=True)  25.5 us
    all_gather x1, blocking collectives, shards(): both = lax.all_gather(both, 'y', axis=0, tiled=False)  22.6 us
    all_gather x1, blocking collectives, shards(): grads = lax.all_gather(grads, 'z', axis=0, tiled=True)  20.6 us
    psum x1, blocking collectives, shards(): sums_two = lax.psum(sums_two, 'vol')  18.8 us
    all_to_all x1, blocking collectives, shards(): conv_parts = lax.all_to_all(conv_parts, 'y', 0, 0, tiled=True)  17 us
    all_to_all x1, waiting for transfers between devices, shards(): lax.all_to_all(filter_parts.reshape(8 * NY, GROUP, 128), ('vol', 'y'), 0,...  15 us
    all_to_all x1, starting transfers between devices, shards(): input_parts = lax.all_to_all(input_parts, 'y', 0, 0, tiled=True)  6.82 us
  transfers between devices with their start and end apart: 4, of which 2 were waited for; matrix products, arithmetic and copies ran while one was open for 1% of the time, Pallas kernels for 9%

commit v1 on v0

--- a/solution.py
+++ b/solution.py
@@ -95,32 +95,11 @@
     spread(base_ref[0], terms, out_ref, 1)
 
 
-def natural_rows(grads_ref, natural):
-    to, of = iota((CH, CH), 0), iota((CH, CH), 1)
-    same = (
-        (lax.shift_right_logical(to, 5) == (lax.shift_right_logical(of, 2) & 7))
-        & ((lax.shift_right_logical(to, 2) & 7) == lax.shift_right_logical(of, 5))
-        & ((to & 3) == (of & 3))
-    )
-    select = jnp.where(same, 1.0, 0.0).astype(BF16)
-
-    def columns(step, carry):
-        part = pl.ds(pl.multiple_of(step * 256, 256), 256)
-        natural[:, part] = jnp.dot(
-            select, grads_ref[:, part], preferred_element_type=F32
-        ).astype(BF16)
-        return carry
-
-    lax.fori_loop(0, BLOCK // 256, columns, 0)
-
-
-def backward_kernel(base_ref, weight_ref, grads_ref, out_ref, natural, terms):
-    natural_rows(grads_ref, natural)
-
+def backward_kernel(base_ref, weight_ref, grads_ref, out_ref, terms):
     def columns(step, carry):
         part = pl.ds(pl.multiple_of(step * 256, 256), 256)
         terms[:, part] = jnp.dot(
-            weight_ref[...], natural[:, part], preferred_element_type=F32
+            weight_ref[...], grads_ref[:, part], preferred_element_type=F32
         )
         return carry
 
@@ -128,8 +107,7 @@
     spread(base_ref[0], terms, out_ref, -1)
 
 
-def filter_kernel(base_ref, grads_ref, acts_ref, out_ref, natural, copies, product):
-    natural_rows(grads_ref, natural)
+def filter_kernel(base_ref, grads_ref, acts_ref, out_ref, copies, product):
     base = base_ref[0]
 
     def rows(group, carry):
@@ -161,7 +139,7 @@
 
     def offsets(step, carry):
         part = pl.ds(pl.multiple_of(step * 256, 256), 256)
-        product[:, part] = nt_dot(natural[...], copies[part, :]).astype(BF16)
+        product[:, part] = nt_dot(grads_ref[...], copies[part, :]).astype(BF16)
         return carry
 
     lax.fori_loop(0, 4, offsets, 0)
@@ -191,13 +169,52 @@
     return jnp.broadcast_to(jnp.sum(parts, axis=1, keepdims=True), (value.shape[0], 128))
 
 
-def prepare_kernel(saved_ref, upstream_ref, acts_ref, sums_ref, packed_ref):
+def in_lanes(values):
+    lane = iota((OWN, 128), 1)
+    row = jnp.zeros((OWN, 128), F32)
+    for index, value in enumerate(values):
+        row = jnp.where(lane == index, value, row)
+    return row
+
+
+def from_lanes(sums_ref, count):
+    total = sums_ref[0]
+    for vol in range(1, sums_ref.shape[0]):
+        total = total + sums_ref[vol]
+    lane = iota((OWN, 128), 1)
+    return [
+        jnp.sum(jnp.where(lane == index, total, 0.0), axis=1, keepdims=True)
+        for index in range(count)
+    ]
+
+
+def to_volumes(sums_ref, values):
+    row = in_lanes(values)
+    for vol in range(sums_ref.shape[0]):
+        sums_ref[vol] = row
+
+
+def sums_kernel(saved_hbm, upstream_hbm, sums_ref, saved_ref, upstream_ref, arrived):
+    first = pltpu.make_async_copy(saved_hbm, saved_ref, arrived.at[0])
+    second = pltpu.make_async_copy(upstream_hbm, upstream_ref, arrived.at[1])
+    first.start()
+    second.start()
+    first.wait()
+    second.wait()
     saved = saved_ref[...].astype(F32)
     upstream = upstream_ref[...].astype(F32)
-    sums_ref[0] = lane_sum(saved)
-    sums_ref[1] = lane_sum(saved * saved)
-    sums_ref[2] = lane_sum(upstream)
-    sums_ref[3] = lane_sum(upstream * saved)
+    to_volumes(
+        sums_ref,
+        [
+            lane_sum(saved),
+            lane_sum(saved * saved),
+            lane_sum(upstream),
+            lane_sum(upstream * saved),
+        ],
+    )
+
+
+def pack_kernel(acts_ref, packed_ref):
     for block in range(NY):
         start = block * BLOCK - REACH
         low, high = max(start, 0), min(start + SPAN, CELLS)
@@ -209,21 +226,21 @@
 
 
 def grad_kernel(counted, saved_ref, upstream_ref, sums_ref, params_ref, packed_ref, means_ref):
-    mean = sums_ref[0] / counted
-    var = sums_ref[1] / counted - mean * mean
+    saved_sum, square_sum, upstream_sum, product_sum = from_lanes(sums_ref, 4)
+    mean = saved_sum / counted
+    var = square_sum / counted - mean * mean
     inverse = lax.rsqrt(var + EPSILON)
-    shift_grad = sums_ref[2] / counted
-    gain_grad = (sums_ref[3] / counted - mean * shift_grad) * inverse
-    means_ref[0] = gain_grad
-    means_ref[1] = shift_grad
-    scale = (params_ref[2] * inverse)[:, :1]
-    mean, inverse = mean[:, :1], inverse[:, :1]
-    shift_grad, gain_grad = shift_grad[:, :1], gain_grad[:, :1]
+    shift_grad = upstream_sum / counted
+    gain_grad = (product_sum / counted - mean * shift_grad) * inverse
+    means_ref[...] = in_lanes([gain_grad, shift_grad])
+    scale = params_ref[2][:, :1] * inverse
     for block in range(NY):
         part = slice(block * BLOCK, (block + 1) * BLOCK)
         normed = (saved_ref[:, part].astype(F32) - mean) * inverse
         upstream = upstream_ref[:, part].astype(F32)
-        packed_ref[block] = (scale * (upstream - shift_grad - normed * gain_grad)).astype(BF16)
+        grads = (scale * (upstream - shift_grad - normed * gain_grad)).astype(BF16)
+        for to in range(NZ):
+            packed_ref[block * NZ + to] = grads
 
 
 def joined(parts_ref, block):
@@ -248,8 +265,7 @@
         out_ref[:, block * BLOCK : (block + 1) * BLOCK] = cells
         total = total + lane_sum(cells)
         squares = squares + lane_sum(cells * cells)
-    sums_ref[0] = total
-    sums_ref[1] = squares
+    to_volumes(sums_ref, [total, squares])
 
 
 def join_kernel(parts_ref, out_ref):
@@ -258,10 +274,11 @@
 
 
 def relu_kernel(counted, conv_ref, sums_ref, params_ref, out_ref):
-    mean = sums_ref[0] / counted
-    var = sums_ref[1] / counted - mean * mean
-    scale = (params_ref[0] * lax.rsqrt(var + EPSILON))[:, :1]
-    mean, bias = mean[:, :1], params_ref[1][:, :1]
+    first_sum, square_sum = from_lanes(sums_ref, 2)
+    mean = first_sum / counted
+    var = square_sum / counted - mean * mean
+    scale = params_ref[0][:, :1] * lax.rsqrt(var + EPSILON)
+    bias = params_ref[1][:, :1]
     out_ref[...] = jnp.maximum((conv_ref[...] - mean) * scale + bias, 0.0).astype(BF16)
 
 
@@ -269,7 +286,7 @@
     return jax.ShapeDtypeStruct(shape, dtype)
 
 
-def call(kernel, outs, specs, scratch=(), flops=0, moved=0):
+def call(kernel, outs, specs, scratch=()):
     return pl.pallas_call(
         kernel,
         out_shape=outs,
@@ -277,8 +294,16 @@
         out_specs=jax.tree.map(lambda _: VMEM, outs),
         scratch_shapes=list(scratch),
         compiler_params=PARAMS,
-        cost_estimate=pl.CostEstimate(flops=flops, bytes_accessed=moved, transcendentals=0),
+        cost_estimate=pl.CostEstimate(flops=1000, bytes_accessed=1000, transcendentals=0),
     )
+
+
+def exchange(value, axes):
+    return lax.all_to_all(value, axes, 0, 0, tiled=True)
+
+
+def to_all(value, axis):
+    return exchange(jnp.broadcast_to(value[None], (lax.axis_size(axis),) + value.shape), axis)
 
 
 def shards(
@@ -292,91 +317,87 @@
     weight_two,
     gain_two,
 ):
-    counted = lax.axis_size("vol") * CELLS
-    matmul = 2 * ROWS * CH * BLOCK
+    volumes = lax.axis_size("vol")
+    counted = volumes * CELLS
     base = (lax.axis_index("y") * BLOCK).astype(jnp.int32).reshape(1)
     params = jnp.broadcast_to(
         jnp.stack([gain_one, bias_one, gain_two])[:, :, None], (3, OWN, 128)
     )
-
-    cells = lax.all_gather(fwd_input[0].T, "z", axis=0, tiled=True)
-    both = jnp.stack([weight_one, jnp.transpose(weight_two, (0, 2, 1))])
-    both = lax.all_gather(both, "y", axis=0, tiled=False)
-    both = jnp.transpose(both, (1, 2, 0, 3, 4)).reshape(2, ROWS, CH)
-
     saved, upstream = saved_conv[0], cotangent[0]
-    sums_two, acts = call(
-        prepare_kernel,
-        (shaped((4, OWN, 128), F32), shaped((NY, OWN, SPAN), BF16)),
-        [VMEM] * 3,
-        moved=600000,
-    )(saved, upstream, saved_input[0])
-    acts = lax.all_to_all(acts, "y", 0, 0, tiled=True).reshape(GROUP, SPAN)
-    sums_two = lax.psum(sums_two, "vol")
-    grads, means = call(
+
+    sums_two = call(
+        sums_kernel,
+        shaped((volumes, OWN, 128), F32),
+        [pl.BlockSpec(memory_space=pl.ANY)] * 2,
+        [
+            pltpu.VMEM((OWN, CELLS), BF16),
+            pltpu.VMEM((OWN, CELLS), BF16),
+            pltpu.SemaphoreType.DMA((2,)),
+        ],
+    )(saved, upstream)
+    weight_one, sums_two = lax.optimization_barrier((weight_one, sums_two))
+    sums_two = exchange(sums_two, "vol")
+
+    cells = to_all(fwd_input[0].T, "z").reshape(BLOCK, CH)
+    rows = jnp.concatenate(
+        [jnp.transpose(weight_one, (1, 0, 2)), jnp.transpose(weight_two, (2, 0, 1))]
+    )
+    row = lax.dynamic_index_in_dim(rows, lax.axis_index("vol"), 0, keepdims=False)
+    rows = to_all(to_all(row, "y"), "vol")
+    weights = [
+        jnp.transpose(rows[first : first + OWN], (2, 1, 0, 3)).reshape(ROWS, CH)
+        for first in (0, OWN)
+    ]
+    acts = call(pack_kernel, shaped((NY, OWN, SPAN), BF16), [VMEM])(saved_input[0])
+    acts = exchange(acts, "y").reshape(GROUP, SPAN)
+
+    packed, means = call(
         lambda *refs: grad_kernel(counted, *refs),
-        (shaped((NY, OWN, BLOCK), BF16), shaped((2, OWN, 128), F32)),
+        (shaped((NY * NZ, OWN, BLOCK), BF16), shaped((OWN, 128), F32)),
         [VMEM] * 4,
-        moved=300000,
     )(saved, upstream, sums_two, params)
-    grads = lax.all_to_all(grads, "y", 0, 0, tiled=True).reshape(GROUP, BLOCK)
-    grads = lax.all_gather(grads, "z", axis=0, tiled=True)
-
-    cells, sums_two = lax.optimization_barrier((cells, sums_two))
+    grads = exchange(packed, ("y", "z")).reshape(CH, BLOCK)
+
+    cells, means = lax.optimization_barrier((cells, means))
     conv_parts = call(
         forward_kernel,
         shaped((NY, OWN, SPAN), F32),
         [SMEM, VMEM, VMEM],
         [pltpu.VMEM((ROWS, BLOCK), F32)],
-        flops=matmul,
-        moved=10000000,
-    )(base, both[0], cells)
-    conv_parts = lax.all_to_all(conv_parts, "y", 0, 0, tiled=True)
-    conv_out, sums_one = call(
-        join_stats_kernel,
-        (shaped((OWN, CELLS), F32), shaped((2, OWN, 128), F32)),
-        [VMEM],
-        moved=700000,
-    )(conv_parts)
-    sums_one = lax.psum(sums_one, "vol")
-    sums_one, grads = lax.optimization_barrier((sums_one, grads))
-    activation = call(
-        lambda *refs: relu_kernel(counted, *refs),
-        shaped((OWN, CELLS), BF16),
-        [VMEM] * 3,
-        moved=300000,
-    )(conv_out, sums_one, params)
-
+    )(base, weights[0], cells)
+    grads, conv_parts = lax.optimization_barrier((grads, conv_parts))
+    conv_parts = exchange(conv_parts, "y")
     filter_parts = call(
         filter_kernel,
         shaped((8, NY, GROUP, 128), BF16),
         [SMEM, VMEM, VMEM],
-        [
-            pltpu.VMEM((CH, BLOCK), BF16),
-            pltpu.VMEM((1024, BLOCK), BF16),
-            pltpu.VMEM((CH, 1024), BF16),
-        ],
-        flops=2 * matmul,
-        moved=10000000,
+        [pltpu.VMEM((1024, BLOCK), BF16), pltpu.VMEM((CH, 1024), BF16)],
     )(base, grads, acts)
-    filter_parts = lax.all_to_all(
-        filter_parts.reshape(8 * NY, GROUP, 128), ("vol", "y"), 0, 0, tiled=True
-    )
-
+    weight, filter_parts = lax.optimization_barrier((weights[1], filter_parts))
+    filter_parts = exchange(filter_parts.reshape(8 * NY, GROUP, 128), ("vol", "y"))
     input_parts = call(
         backward_kernel,
         shaped((NY, OWN, SPAN), BF16),
         [SMEM, VMEM, VMEM],
-        [pltpu.VMEM((CH, BLOCK), BF16), pltpu.VMEM((ROWS, BLOCK), F32)],
-        flops=matmul,
-        moved=10000000,
-    )(base, both[1], grads)
-    input_parts = lax.all_to_all(input_parts, "y", 0, 0, tiled=True)
-    input_grad = call(join_kernel, shaped((OWN, CELLS), BF16), [VMEM], moved=350000)(input_parts)
+        [pltpu.VMEM((ROWS, BLOCK), F32)],
+    )(base, weight, grads)
+    conv_parts, input_parts = lax.optimization_barrier((conv_parts, input_parts))
+    input_parts = exchange(input_parts, "y")
+
+    conv_out, sums_one = call(
+        join_stats_kernel,
+        (shaped((OWN, CELLS), F32), shaped((volumes, OWN, 128), F32)),
+        [VMEM],
+    )(conv_parts)
+    sums_one = exchange(sums_one, "vol")
+    activation = call(
+        lambda *refs: relu_kernel(counted, *refs), shaped((OWN, CELLS), BF16), [VMEM] * 3
+    )(conv_out, sums_one, params)
+    input_grad = call(join_kernel, shaped((OWN, CELLS), BF16), [VMEM])(input_parts)
 
     summed = jnp.sum(filter_parts.astype(F32), axis=0) / math.sqrt(counted)
     weight_grad = jnp.transpose(summed[:, : 27 * OWN].reshape(GROUP, 27, OWN), (1, 0, 2))
-    return (activation[None], input_grad[None], weight_grad, means[0, :, 0], means[1, :, 0])
+    return (activation[None], input_grad[None], weight_grad, means[:, 0], means[:, 1])
 
 
 def solution(mesh):

time: 206 us -> 191 us (0.927)
  blocking collectives: 139 us -> 64.7 us
  waiting for transfers between devices: 18.9 us -> 61.3 us
  starting transfers between devices: 20.3 us -> 35.3 us
  local copies, waits for them, and re-layouts: 6.41 us -> 8.55 us
    all_gather x3 -> x0, blocking collectives: 68.7 us -> none  [the longest x1 25.5 us: shards(): cells = lax.all_gather(fwd_input[0].T, 'z', axis=0, tiled=True)]
    psum x2 -> x0, blocking collectives: 53.3 us -> none  [the longest x1 34.5 us: shards(): sums_one = lax.psum(sums_one, 'vol')]
    all_to_all x1 -> x4, blocking collectives: 17 us -> 64.7 us  [exchange(): return lax.all_to_all(value, axes, 0, 0, tiled=True)]
    all_to_all x4 -> x6, waiting for transfers between devices: 18.9 us -> 61.3 us  [exchange(): return lax.all_to_all(value, axes, 0, 0, tiled=True)]
    all_to_all x4 -> x6, starting transfers between devices: 20.3 us -> 35.3 us  [exchange(): return lax.all_to_all(value, axes, 0, 0, tiled=True)]
    unnamed x22 -> x25, local copies, waits for them, and re-layouts: 3.76 us -> 4.21 us
  transfers between devices with their start and end apart: 4 -> 6, of which waited for: 2 -> 6; matrix products, arithmetic and copies ran while one was open for 1% -> 2% of each run, Pallas kernels for 9% -> 9%
where the time goes in v1:
time: 191 us; the launch traced here: 190 us
  blocking collectives  64.7 us (34%)
  waiting for transfers between devices  61.3 us (32%)
  starting transfers between devices  35.3 us (18%)
  Pallas kernels  18.9 us (10%)
  local copies, waits for them, and re-layouts  8.55 us (4%)
    all_to_all x4, blocking collectives, exchange(): return lax.all_to_all(value, axes, 0, 0, tiled=True)  64.7 us
    all_to_all x6, waiting for transfers between devices, exchange(): return lax.all_to_all(value, axes, 0, 0, tiled=True)  61.3 us
    all_to_all x6, starting transfers between devices, exchange(): return lax.all_to_all(value, axes, 0, 0, tiled=True)  35.3 us
    pallas_call x1, Pallas kernels, shards(): call(forward_kernel, shaped((NY, OWN, SPAN), F32), [SMEM, VMEM, VMEM], [p...  5.21 us
    pallas_call x1, Pallas kernels, shards(): call(backward_kernel, shaped((NY, OWN, SPAN), BF16), [SMEM, VMEM, VMEM],...  4.88 us
    unnamed x25, local copies, waits for them, and re-layouts  4.21 us
    pallas_call x1, Pallas kernels, shards(): call(filter_kernel, shaped((8, NY, GROUP, 128), BF16), [SMEM, VMEM, VMEM]...  4.16 us
  transfers between devices with their start and end apart: 6, of which 6 were waited for; matrix products, arithmetic and copies ran while one was open for 2% of the time, Pallas kernels for 9%

profile of v1, /device:TPU:1, one launch (start us, length us, event | category | flops | bytes accessed | tf_op | source)
XLA Modules:
  0.0 189.7 jit_solution(16631766985840096023)
XLA Ops:
  0.6 0.0 copy-start
  0.6 0.9 copy-done
  1.5 0.0 copy-start.2
  1.5 0.9 copy-done.2
  2.4 0.0 copy-start.7
  2.4 1.1 shard_map.128
  3.5 0.0 copy-done.7
  3.5 0.0 copy-start.8
  3.6 0.8 copy-done.8
  4.4 15.4 %all_to_all.50 = bf16[8,27,256]{2,1,0:T(8,128)(2,1)S(1)} all-to-all(bf16[8,27,256]{2,1,0:T(8,128)(2,1)S(1)} %broadcast_in_dim.16), channel_id=1, replica_groups=mesh['vol'=8,'y'=8,'z'=8] {'y'}, dimensions={0} | all-to-all | bytes 221184 | tf_op jit(solution)/shard_map/all_to_all | solution.py:302
  19.8 6.4 %all-to-all-start = ((f32[8,4,128]{2,1,0:T(4,128)}), f32[8,4,128]{2,1,0:T(4,128)S(1)}, u32[]{:S(2)}, u32[]{:S(2)}) async-start(f32[8,4,128]{2,1,0:T(4,128)} %shard_map.128), calls=%async_computation | async-start | bytes 32768 | tf_op jit(solution)/shard_map/all_to_all | solution.py:302
  26.2 0.1 copy.18
  26.3 4.6 %all-to-all-done.refs_2_ = f32[8,4,128]{2,1,0:T(4,128)S(1)} async-done(((f32[8,4,128]{2,1,0:T(4,128)}), f32[8,4,128]{2,1,0:T(4,128)S(1)}, u32[]{:S(2)}, u32[]{:S(2)}) %all-to-all-start) | async-done | bytes 16416 | tf_op jit(solution)/shard_map/all_to_all | solution.py:302
  30.9 0.1 broadcast_in_dim.17
  30.9 0.0 copy-start.6
  30.9 16.7 %all_to_all.51 = bf16[8,8,27,256]{3,1,2,0:T(8,128)(2,1)S(1)} all-to-all(bf16[8,8,27,256]{3,1,2,0:T(8,128)(2,1)S(1)} %broadcast_in_dim.17), channel_id=1, replica_groups=mesh['vol'=8,'y'=8,'z'=8] {'vol'}, dimensions={0} | all-to-all | bytes 1769472 | tf_op jit(solution)/shard_map/all_to_all | solution.py:302
  47.6 0.0 copy-done.6
  47.7 1.0 broadcast_in_dim.36
  48.6 0.0 copy-start.1
  48.6 0.0 copy-start.3
  48.6 10.2 %all-to-all-start.4 = ((bf16[8,192,256]{2,1,0:T(8,128)(2,1)}), bf16[8,192,256]{2,1,0:T(8,128)(2,1)S(1)}, u32[]{:S(2)}, u32[]{:S(2)}) async-start(bf16[8,192,256]{2,1,0:T(8,128)(2,1)} %broadcast_in_dim.36), calls=%async_computation.4 | async-start | bytes 1572864 | tf_op jit(solution)/shard_map/all_to_all | solution.py:302
  58.8 0.0 copy-start.9
  58.8 0.0 copy-start.10
  58.8 0.0 copy-start.11
  58.8 0.6 copy-done.9
  59.4 0.0 copy-done.10
  59.5 0.0 copy-done.11
  59.5 0.1 broadcast_in_dim.14.refs_3_.refs_2_
  59.6 0.0 copy-done.1
  59.6 0.0 copy-done.3
  59.6 1.1 shard_map.129
  60.7 21.7 %all-to-all-done.4 = bf16[8,192,256]{2,1,0:T(8,128)(2,1)S(1)} async-done(((bf16[8,192,256]{2,1,0:T(8,128)(2,1)}), bf16[8,192,256]{2,1,0:T(8,128)(2,1)S(1)}, u32[]{:S(2)}, u32[]{:S(2)}) %all-to-all-start.4) | async-done | bytes 786464 | tf_op jit(solution)/shard_map/all_to_all | solution.py:302
  82.4 0.0 copy-start.4
  82.4 4.8 %all-to-all-start.1 = ((bf16[64,4,1536]{2,1,0:T(4,128)(2,1)}), bf16[64,4,1536]{2,1,0:T(4,128)(2,1)S(1)}, u32[]{:S(2)}, u32[]{:S(2)}) async-start(bf16[64,4,1536]{2,1,0:T(4,128)(2,1)} %get-tuple-element.20), calls=%async_computation.1 | async-start | bytes 1572864 | tf_op jit(solution)/shard_map/all_to_all | solution.py:302
  87.1 0.0 copy-done.4
  87.2 0.7 shard_map.131
  87.9 21.2 %all-to-all-done.1 = bf16[64,4,1536]{2,1,0:T(4,128)(2,1)S(1)} async-done(((bf16[64,4,1536]{2,1,0:T(4,128)(2,1)}), bf16[64,4,1536]{2,1,0:T(4,128)(2,1)S(1)}, u32[]{:S(2)}, u32[]{:S(2)}) %all-to-all-start.1) | async-done | bytes 786464 | tf_op jit(solution)/shard_map/all_to_all | solution.py:302
  109.1 5.6 %all-to-all-start.6 = ((bf16[8,4,3840]{2,1,0:T(4,128)(2,1)}), bf16[8,4,3840]{2,1,0:T(4,128)(2,1)S(1)}, u32[]{:S(2)}, u32[]{:S(2)}) async-start(bf16[8,4,3840]{2,1,0:T(4,128)(2,1)} %shard_map.131), calls=%async_computation.6 | async-start | bytes 491520 | tf_op jit(solution)/shard_map/all_to_all | solution.py:302
  114.7 0.8 slice_bitcast_fusion
  115.6 0.2 copy.19
  115.8 0.1 reshape.39.weight_ref
  115.9 5.2 %shard_map.130 = f32[8,4,3840]{2,1,0:T(4,128)} custom-call(s32[1]{0:T(128)} %bitcast.5.base_ref, bf16[864,256]{1,0:T(8,128)(2,1)S(1)} %reshape.39.weight_ref, bf16[1536,256]{1,0:T(8,128)(2,1)S(1)} %bitcast.29), custom_call_target="tpu_custom_call" | custom-call | flops 1000 | bytes 1000 | tf_op jit(solution)/shard_map/pallas_call | solution.py:362
  121.1 0.2 reshape.37.grads_ref
  121.3 2.7 %all-to-all-done.6 = bf16[8,4,3840]{2,1,0:T(4,128)(2,1)S(1)} async-done(((bf16[8,4,3840]{2,1,0:T(4,128)(2,1)}), bf16[8,4,3840]{2,1,0:T(4,128)(2,1)S(1)}, u32[]{:S(2)}, u32[]{:S(2)}) %all-to-all-start.6) | async-done | bytes 245792 | tf_op jit(solution)/shard_map/all_to_all | solution.py:302
  124.0 4.0 %all-to-all-start.5 = ((f32[8,4,3840]{2,1,0:T(4,128)}), f32[8,4,3840]{2,1,0:T(4,128)S(1)}, u32[]{:S(2)}, u32[]{:S(2)}) async-start(f32[8,4,3840]{2,1,0:T(4,128)} %shard_map.130), calls=%async_computation.5 | async-start | bytes 983040 | tf_op jit(solution)/shard_map/all_to_all | solution.py:302
  128.0 0.0 copy-start.5
  128.0 0.1 reshape.42.acts_ref
  128.0 0.9 copy-done.5
  129.0 0.2 copy.20
  129.2 0.1 reshape.41.weight_ref
  129.3 4.2 %shard_map.132 = bf16[8,8,32,128]{3,2,1,0:T(8,128)(2,1)S(1)} custom-call(s32[1]{0:T(128)} %bitcast.5.base_ref, bf16[256,1536]{1,0:T(8,128)(2,1)S(1)} %reshape.37.grads_ref, bf16[32,3840]{1,0:T(8,128)(2,1)S(1)} %reshape.42.acts_ref), custom_call_target="tpu_custom_call" | custom-call | flops 1000 | bytes 1000 | tf_op jit(solution)/shard_map/pallas_call | solution.py:370
  133.5 4.9 %shard_map.133 = bf16[8,4,3840]{2,1,0:T(4,128)(2,1)} custom-call(s32[1]{0:T(128)} %bitcast.5.base_ref, bf16[864,256]{1,0:T(8,128)(2,1)S(1)} %reshape.41.weight_ref, bf16[256,1536]{1,0:T(8,128)(2,1)S(1)} %reshape.37.grads_ref), custom_call_target="tpu_custom_call" | custom-call | flops 1000 | bytes 1000 | tf_op jit(solution)/shard_map/pallas_call | solution.py:378
  138.4 3.2 %all-to-all-done.5.parts_ref = f32[8,4,3840]{2,1,0:T(4,128)S(1)} async-done(((f32[8,4,3840]{2,1,0:T(4,128)}), f32[8,4,3840]{2,1,0:T(4,128)S(1)}, u32[]{:S(2)}, u32[]{:S(2)}) %all-to-all-start.5) | async-done | bytes 491552 | tf_op jit(solution)/shard_map/all_to_all | solution.py:302
  141.6 0.2 shard_map.134
  141.8 11.1 %all_to_all.52.refs_1_ = f32[8,4,128]{2,1,0:T(4,128)S(1)} all-to-all(f32[8,4,128]{2,1,0:T(4,128)S(1)} %get-tuple-element.29), channel_id=1, replica_groups=mesh['vol'=8,'y'=8,'z'=8] {'vol'}, dimensions={0} | all-to-all | bytes 32768 | tf_op jit(solution)/shard_map/all_to_all | solution.py:302
  152.9 21.5 %all_to_all.53 = bf16[64,32,128]{2,1,0:T(8,128)(2,1)S(1)} all-to-all(bf16[64,32,128]{2,1,0:T(8,128)(2,1)S(1)} %bitcast.30), channel_id=1, replica_groups=mesh['vol'=8,'y'=8,'z'=8] {'vol','y'}, dimensions={0} | all-to-all | bytes 1048576 | tf_op jit(solution)/shard_map/all_to_all | solution.py:302
  174.4 4.3 %all-to-all-start.8 = ((bf16[8,4,3840]{2,1,0:T(4,128)(2,1)}), bf16[8,4,3840]{2,1,0:T(4,128)(2,1)S(1)}, u32[]{:S(2)}, u32[]{:S(2)}) async-start(bf16[8,4,3840]{2,1,0:T(4,128)(2,1)} %shard_map.133), calls=%async_computation.8 | async-start | bytes 491520 | tf_op jit(solution)/shard_map/all_to_all | solution.py:302
  178.7 0.7 slice_reduce_fusion
  179.4 0.9 shard_map.135
  180.2 0.1 convert_reduce_fusion
  180.3 0.1 copy.21
  180.4 0.6 reshape.44
  181.1 7.9 %all-to-all-done.8.parts_ref = bf16[8,4,3840]{2,1,0:T(4,128)(2,1)S(1)} async-done(((bf16[8,4,3840]{2,1,0:T(4,128)(2,1)}), bf16[8,4,3840]{2,1,0:T(4,128)(2,1)S(1)}, u32[]{:S(2)}, u32[]{:S(2)}) %all-to-all-start.8) | async-done | bytes 245792 | tf_op jit(solution)/shard_map/all_to_all | solution.py:302
  189.0 0.7 shard_map.136
  (6 shorter events, 0.1 us)
Async XLA Ops:
  0.6 0.9 copy-start
  1.5 0.9 copy-start.2
  2.4 1.1 copy-start.7
  3.5 0.8 copy-start.8
  19.8 11.1 %all-to-all-start = ((f32[8,4,128]{2,1,0:T(4,128)}), f32[8,4,128]{2,1,0:T(4,128)S(1)}, u32[]{:S(2)}, u32[]{:S(2)}) async-start(f32[8,4,128]{2,1,0:T(4,128)} %shard_map.128), calls=%async_computation | async-start | bytes 32768 | tf_op jit(solution)/shard_map/all_to_all | solution.py:302
  30.9 16.7 %copy-start.6 = (bf16[1,256,192]{1,2,0:T(8,128)(2,1)S(1)}, bf16[1,256,192]{1,2,0:T(8,128)(2,1)}, u32[]{:S(2)}) copy-start(bf16[1,256,192]{1,2,0:T(8,128)(2,1)} %param.9) | copy-start | bytes 294916
  48.6 10.9 %copy-start.1 = (bf16[1,4,12288]{2,1,0:T(4,128)(2,1)S(1)}, bf16[1,4,12288]{2,1,0:T(4,128)(2,1)}, u32[]{:S(2)}) copy-start(bf16[1,4,12288]{2,1,0:T(4,128)(2,1)} %param.13) | copy-start | bytes 294916
  48.6 10.9 %copy-start.3 = (bf16[1,4,12288]{2,1,0:T(4,128)(2,1)S(1)}, bf16[1,4,12288]{2,1,0:T(4,128)(2,1)}, u32[]{:S(2)}) copy-start(bf16[1,4,12288]{2,1,0:T(4,128)(2,1)} %param.14) | copy-start | bytes 294916
  48.6 33.7 %all-to-all-start.4 = ((bf16[8,192,256]{2,1,0:T(8,128)(2,1)}), bf16[8,192,256]{2,1,0:T(8,128)(2,1)S(1)}, u32[]{:S(2)}, u32[]{:S(2)}) async-start(bf16[8,192,256]{2,1,0:T(8,128)(2,1)} %broadcast_in_dim.36), calls=%async_computation.4 | async-start | bytes 1572864 | tf_op jit(solution)/shard_map/all_to_all | solution.py:302
  58.8 0.7 copy-start.9
  58.8 0.7 copy-start.10
  58.8 0.7 copy-start.11
  82.4 4.8 %copy-start.4 = (bf16[1,4,12288]{2,1,0:T(4,128)(2,1)S(1)}, bf16[1,4,12288]{2,1,0:T(4,128)(2,1)}, u32[]{:S(2)}) copy-start(bf16[1,4,12288]{2,1,0:T(4,128)(2,1)} %param.15) | copy-start | bytes 294916
  82.4 26.7 %all-to-all-start.1 = ((bf16[64,4,1536]{2,1,0:T(4,128)(2,1)}), bf16[64,4,1536]{2,1,0:T(4,128)(2,1)S(1)}, u32[]{:S(2)}, u32[]{:S(2)}) async-start(bf16[64,4,1536]{2,1,0:T(4,128)(2,1)} %get-tuple-element.20), calls=%async_computation.1 | async-start | bytes 1572864 | tf_op jit(solution)/shard_map/all_to_all | solution.py:302
  109.1 14.9 %all-to-all-start.6 = ((bf16[8,4,3840]{2,1,0:T(4,128)(2,1)}), bf16[8,4,3840]{2,1,0:T(4,128)(2,1)S(1)}, u32[]{:S(2)}, u32[]{:S(2)}) async-start(bf16[8,4,3840]{2,1,0:T(4,128)(2,1)} %shard_map.131), calls=%async_computation.6 | async-start | bytes 491520 | tf_op jit(solution)/shard_map/all_to_all | solution.py:302
  124.0 17.6 %all-to-all-start.5 = ((f32[8,4,3840]{2,1,0:T(4,128)}), f32[8,4,3840]{2,1,0:T(4,128)S(1)}, u32[]{:S(2)}, u32[]{:S(2)}) async-start(f32[8,4,3840]{2,1,0:T(4,128)} %shard_map.130), calls=%async_computation.5 | async-start | bytes 983040 | tf_op jit(solution)/shard_map/all_to_all | solution.py:302
  128.0 1.0 copy-start.5
  174.4 14.6 %all-to-all-start.8 = ((bf16[8,4,3840]{2,1,0:T(4,128)(2,1)}), bf16[8,4,3840]{2,1,0:T(4,128)(2,1)S(1)}, u32[]{:S(2)}, u32[]{:S(2)}) async-start(bf16[8,4,3840]{2,1,0:T(4,128)(2,1)} %shard_map.133), calls=%async_computation.8 | async-start | bytes 491520 | tf_op jit(solution)/shard_map/all_to_all | solution.py:302

commit v2 on v1

--- a/solution.py
+++ b/solution.py
@@ -20,6 +20,7 @@
 GROUP = NY * OWN
 CH = 256
 ROWS = 27 * GROUP
+RING = (0, 1, -1, 2, -2, 3, -3, 4)
 EPSILON = 1e-05
 F32 = jnp.float32
 BF16 = jnp.bfloat16
@@ -42,7 +43,7 @@
     return lax.dot_general(left, right, (((1,), (1,)), ((), ())), preferred_element_type=F32)
 
 
-def spread(base, terms, out_ref, sign):
+def spread(base, terms, held, out_refs, sign):
     def rows(group, carry):
         lane = iota((8, BLOCK), 1)
         along_x = lane & 31
@@ -78,24 +79,35 @@
         )
         for start, piece in pieces:
             stop = start + piece.shape[1]
-            out_ref[2 * group, :, start:stop] = piece[:OWN].astype(out_ref.dtype)
-            out_ref[2 * group + 1, :, start:stop] = piece[OWN:].astype(out_ref.dtype)
+            held[2 * group, :, start:stop] = piece[:OWN]
+            held[2 * group + 1, :, start:stop] = piece[OWN:]
         return carry
 
     lax.fori_loop(0, GROUP // 8, rows, 0)
-
-
-def forward_kernel(base_ref, weight_ref, cells_ref, out_ref, terms):
+    for hop, out_ref in enumerate(out_refs):
+        out_ref[...] = held[hop].astype(out_ref.dtype)
+
+
+def forward_kernel(place_ref, weight_ref, *refs):
+    parts, out_refs = refs[:NZ], refs[NZ : NZ + NY]
+    cells, terms, held = refs[NZ + NY :]
+    for hop, part in zip(RING, parts):
+        source = (place_ref[1] - hop) & (NZ - 1)
+        rows = BLOCK // NZ
+        cells[pl.ds(pl.multiple_of(source * rows, rows), rows), :] = part[...]
+
     def columns(step, carry):
         part = pl.ds(pl.multiple_of(step * 256, 256), 256)
-        terms[:, part] = nt_dot(weight_ref[...], cells_ref[part, :])
+        terms[:, part] = nt_dot(weight_ref[...], cells[part, :])
         return carry
 
     lax.fori_loop(0, BLOCK // 256, columns, 0)
-    spread(base_ref[0], terms, out_ref, 1)
-
-
-def backward_kernel(base_ref, weight_ref, grads_ref, out_ref, terms):
+    spread(place_ref[0] * BLOCK, terms, held, out_refs, 1)
+
+
+def backward_kernel(place_ref, weight_ref, grads_ref, *refs):
+    out_refs, (terms, held) = refs[:NY], refs[NY:]
+
     def columns(step, carry):
         part = pl.ds(pl.multiple_of(step * 256, 256), 256)
         terms[:, part] = jnp.dot(
@@ -104,18 +116,21 @@
         return carry
 
     lax.fori_loop(0, BLOCK // 256, columns, 0)
-    spread(base_ref[0], terms, out_ref, -1)
-
-
-def filter_kernel(base_ref, grads_ref, acts_ref, out_ref, copies, product):
-    base = base_ref[0]
+    spread(place_ref[0] * BLOCK, terms, held, out_refs, -1)
+
+
+def filter_kernel(place_ref, grads_ref, *refs):
+    parts, (out_ref, acts_all, copies, product) = refs[:NY], refs[NY:]
+    base = place_ref[0] * BLOCK
+    for hop, part in enumerate(parts):
+        acts_all[OWN * hop : OWN * hop + OWN, :] = part[...].astype(F32)
 
     def rows(group, carry):
         lane = iota((16, SPAN), 1)
         along_x = lane & 31
         along_y = lax.shift_right_logical(lane + (base + 2 * PLANE - REACH), 5) & 31
         first = pl.multiple_of(group * 16, 16)
-        acts = acts_ref[pl.ds(first, 16), :].astype(F32)
+        acts = acts_all[pl.ds(first, 16), :]
         ends = {1: along_x <= 30, -1: along_x >= 1}
         sides = {1: along_y <= 30, -1: along_y >= 1}
         for b in (-1, 0, 1):
@@ -154,7 +169,8 @@
         placed = jnp.dot(product[...], select, preferred_element_type=F32).astype(BF16)
         for vol in range(8):
             for half in range(2):
-                out_ref[vol, 2 * step + half] = placed[
+                owner = (place_ref[0] - (2 * step + half)) & (NY - 1)
+                out_ref[vol, owner] = placed[
                     32 * vol : 32 * vol + 32, 128 * half : 128 * half + 128
                 ]
         return carry
@@ -177,10 +193,10 @@
     return row
 
 
-def from_lanes(sums_ref, count):
-    total = sums_ref[0]
-    for vol in range(1, sums_ref.shape[0]):
-        total = total + sums_ref[vol]
+def from_lanes(sums, count):
+    total = sums[0][...]
+    for row in sums[1:]:
+        total = total + row[...]
     lane = iota((OWN, 128), 1)
     return [
         jnp.sum(jnp.where(lane == index, total, 0.0), axis=1, keepdims=True)
@@ -214,19 +230,35 @@
     )
 
 
-def pack_kernel(acts_ref, packed_ref):
-    for block in range(NY):
-        start = block * BLOCK - REACH
-        low, high = max(start, 0), min(start + SPAN, CELLS)
-        packed_ref[block, :, low - start : high - start] = acts_ref[:, low:high]
-        if low > start:
-            packed_ref[block, :, : low - start] = jnp.zeros((OWN, low - start), BF16)
-        if high < start + SPAN:
-            packed_ref[block, :, high - start :] = jnp.zeros((OWN, start + SPAN - high), BF16)
+def pack_kernel(place_ref, acts_ref, *refs):
+    out_refs, (padded,) = refs[:NY], refs[NY:]
+    padded[:, :REACH] = jnp.zeros((OWN, REACH), F32)
+    padded[:, REACH : REACH + CELLS] = acts_ref[...].astype(F32)
+    padded[:, REACH + CELLS :] = jnp.zeros((OWN, REACH), F32)
+    for hop, out_ref in enumerate(out_refs):
+        block = (place_ref[0] + hop) & (NY - 1)
+        part = padded[:, pl.ds(pl.multiple_of(block * BLOCK, BLOCK), SPAN)]
+        out_ref[...] = part.astype(BF16)
+
+
+def arrange_kernel(place_ref, *refs):
+    parts, (first_ref, second_ref, held) = refs[:8], refs[8:]
+    for hop, part in enumerate(parts):
+        held[(place_ref[2] - hop) & 7] = part[...]
+    to, of = iota((ROWS, 1024), 0), iota((ROWS, 1024), 1)
+    same = (
+        (lax.shift_right_logical(to, 5) == (of & 31))
+        & ((lax.shift_right_logical(to, 2) & 7) == (lax.shift_right_logical(of, 5) & 7))
+        & ((to & 3) == lax.shift_right_logical(of, 8))
+    )
+    select = jnp.where(same, 1.0, 0.0).astype(BF16)
+    for start, out_ref in ((0, first_ref), (OWN, second_ref)):
+        rows = held[start : start + OWN].reshape(1024, CH)
+        out_ref[...] = jnp.dot(select, rows, preferred_element_type=F32).astype(BF16)
 
 
 def grad_kernel(counted, saved_ref, upstream_ref, sums_ref, params_ref, packed_ref, means_ref):
-    saved_sum, square_sum, upstream_sum, product_sum = from_lanes(sums_ref, 4)
+    saved_sum, square_sum, upstream_sum, product_sum = from_lanes([sums_ref.at[vol] for vol in range(sums_ref.shape[0])], 4)
     mean = saved_sum / counted
     var = square_sum / counted - mean * mean
     inverse = lax.rsqrt(var + EPSILON)
@@ -257,7 +289,14 @@
     return jnp.concatenate(pieces, axis=1)
 
 
-def join_stats_kernel(parts_ref, out_ref, sums_ref):
+def place_blocks(place_ref, parts, held):
+    for hop, part in enumerate(parts):
+        held[(place_ref[0] + hop) & (NY - 1)] = part[...].astype(F32)
+
+
+def join_stats_kernel(place_ref, *refs):
+    parts, (out_ref, sums_ref, parts_ref) = refs[:NY], refs[NY:]
+    place_blocks(place_ref, parts, parts_ref)
     total = jnp.zeros((OWN, 128), F32)
     squares = jnp.zeros((OWN, 128), F32)
     for block in range(NY):
@@ -265,16 +304,19 @@
         out_ref[:, block * BLOCK : (block + 1) * BLOCK] = cells
         total = total + lane_sum(cells)
         squares = squares + lane_sum(cells * cells)
-    to_volumes(sums_ref, [total, squares])
-
-
-def join_kernel(parts_ref, out_ref):
+    sums_ref[...] = in_lanes([total, squares])
+
+
+def join_kernel(place_ref, *refs):
+    parts, (out_ref, parts_ref) = refs[:NY], refs[NY:]
+    place_blocks(place_ref, parts, parts_ref)
     for block in range(NY):
         out_ref[:, block * BLOCK : (block + 1) * BLOCK] = joined(parts_ref, block).astype(BF16)
 
 
-def relu_kernel(counted, conv_ref, sums_ref, params_ref, out_ref):
-    first_sum, square_sum = from_lanes(sums_ref, 2)
+def relu_kernel(counted, conv_ref, params_ref, *refs):
+    sums, out_ref = refs[:-1], refs[-1]
+    first_sum, square_sum = from_lanes(sums, 2)
     mean = first_sum / counted
     var = square_sum / counted - mean * mean
     scale = params_ref[0][:, :1] * lax.rsqrt(var + EPSILON)
@@ -302,8 +344,24 @@
     return lax.all_to_all(value, axes, 0, 0, tiled=True)
 
 
-def to_all(value, axis):
-    return exchange(jnp.broadcast_to(value[None], (lax.axis_size(axis),) + value.shape), axis)
+def hop_to(value, axis, hop):
+    size = lax.axis_size(axis)
+    return lax.ppermute(value, axis, [(at, (at + hop) % size) for at in range(size)])
+
+
+def by_hop(values, axis, sign=1):
+    return [
+        value if hop == 0 else hop_to(value, axis, sign * hop) for hop, value in enumerate(values)
+    ]
+
+
+def round_ring(value, axis):
+    held = {0: value}
+    for hop in range(1, NZ // 2 + 1):
+        held[hop] = hop_to(held[hop - 1], axis, 1)
+        if hop < NZ // 2:
+            held[-hop] = hop_to(held[1 - hop], axis, -1)
+    return [held[hop] for hop in RING]
 
 
 def shards(
@@ -319,7 +377,7 @@
 ):
     volumes = lax.axis_size("vol")
     counted = volumes * CELLS
-    base = (lax.axis_index("y") * BLOCK).astype(jnp.int32).reshape(1)
+    place = jnp.stack([lax.axis_index(name) for name in ("y", "z", "vol")]).astype(jnp.int32)
     params = jnp.broadcast_to(
         jnp.stack([gain_one, bias_one, gain_two])[:, :, None], (3, OWN, 128)
     )
@@ -335,21 +393,31 @@
             pltpu.SemaphoreType.DMA((2,)),
         ],
     )(saved, upstream)
-    weight_one, sums_two = lax.optimization_barrier((weight_one, sums_two))
+    weight_one, weight_two, fwd_input, sums_two = lax.optimization_barrier(
+        (weight_one, weight_two, fwd_input, sums_two)
+    )
     sums_two = exchange(sums_two, "vol")
 
-    cells = to_all(fwd_input[0].T, "z").reshape(BLOCK, CH)
+    cells = round_ring(fwd_input[0].T, "z")
     rows = jnp.concatenate(
         [jnp.transpose(weight_one, (1, 0, 2)), jnp.transpose(weight_two, (2, 0, 1))]
     )
     row = lax.dynamic_index_in_dim(rows, lax.axis_index("vol"), 0, keepdims=False)
-    rows = to_all(to_all(row, "y"), "vol")
-    weights = [
-        jnp.transpose(rows[first : first + OWN], (2, 1, 0, 3)).reshape(ROWS, CH)
-        for first in (0, OWN)
-    ]
-    acts = call(pack_kernel, shaped((NY, OWN, SPAN), BF16), [VMEM])(saved_input[0])
-    acts = exchange(acts, "y").reshape(GROUP, SPAN)
+    row = jnp.pad(row, ((0, 5), (0, 0)))
+    rows = jnp.stack(by_hop([row] * NY, "y"))
+    weights = call(
+        arrange_kernel,
+        (shaped((ROWS, CH), BF16), shaped((ROWS, CH), BF16)),
+        [SMEM] + [VMEM] * 8,
+        [pltpu.VMEM((8, NY, 32, CH), BF16)],
+    )(place, *by_hop([rows] * 8, "vol"))
+    acts = call(
+        pack_kernel,
+        [shaped((OWN, SPAN), BF16)] * NY,
+        [SMEM, VMEM],
+        [pltpu.VMEM((OWN, CELLS + 2 * REACH), F32)],
+    )(place, saved_input[0])
+    acts = by_hop(acts, "y")
 
     packed, means = call(
         lambda *refs: grad_kernel(counted, *refs),
@@ -361,39 +429,53 @@
     cells, means = lax.optimization_barrier((cells, means))
     conv_parts = call(
         forward_kernel,
-        shaped((NY, OWN, SPAN), F32),
-        [SMEM, VMEM, VMEM],
-        [pltpu.VMEM((ROWS, BLOCK), F32)],
-    )(base, weights[0], cells)
+        [shaped((OWN, SPAN), F32)] * NY,
+        [SMEM] + [VMEM] * (1 + NZ),
+        [
+            pltpu.VMEM((BLOCK, CH), BF16),
+            pltpu.VMEM((ROWS, BLOCK), F32),
+            pltpu.VMEM((NY, OWN, SPAN), F32),
+        ],
+    )(place, weights[0], *cells)
     grads, conv_parts = lax.optimization_barrier((grads, conv_parts))
-    conv_parts = exchange(conv_parts, "y")
+    conv_parts = by_hop(conv_parts, "y", -1)
     filter_parts = call(
         filter_kernel,
         shaped((8, NY, GROUP, 128), BF16),
-        [SMEM, VMEM, VMEM],
-        [pltpu.VMEM((1024, BLOCK), BF16), pltpu.VMEM((CH, 1024), BF16)],
-    )(base, grads, acts)
+        [SMEM] + [VMEM] * (1 + NY),
+        [
+            pltpu.VMEM((GROUP, SPAN), F32),
+            pltpu.VMEM((1024, BLOCK), BF16),
+            pltpu.VMEM((CH, 1024), BF16),
+        ],
+    )(place, grads, *acts)
     weight, filter_parts = lax.optimization_barrier((weights[1], filter_parts))
     filter_parts = exchange(filter_parts.reshape(8 * NY, GROUP, 128), ("vol", "y"))
     input_parts = call(
         backward_kernel,
-        shaped((NY, OWN, SPAN), BF16),
+        [shaped((OWN, SPAN), BF16)] * NY,
         [SMEM, VMEM, VMEM],
-        [pltpu.VMEM((ROWS, BLOCK), F32)],
-    )(base, weight, grads)
+        [pltpu.VMEM((ROWS, BLOCK), F32), pltpu.VMEM((NY, OWN, SPAN), F32)],
+    )(place, weight, grads)
     conv_parts, input_parts = lax.optimization_barrier((conv_parts, input_parts))
-    input_parts = exchange(input_parts, "y")
+    input_parts = by_hop(input_parts, "y", -1)
 
     conv_out, sums_one = call(
         join_stats_kernel,
-        (shaped((OWN, CELLS), F32), shaped((volumes, OWN, 128), F32)),
-        [VMEM],
-    )(conv_parts)
-    sums_one = exchange(sums_one, "vol")
+        (shaped((OWN, CELLS), F32), shaped((OWN, 128), F32)),
+        [SMEM] + [VMEM] * NY,
+        [pltpu.VMEM((NY, OWN, SPAN), F32)],
+    )(place, *conv_parts)
+    sums_one = by_hop([sums_one] * 8, "vol")
     activation = call(
-        lambda *refs: relu_kernel(counted, *refs), shaped((OWN, CELLS), BF16), [VMEM] * 3
-    )(conv_out, sums_one, params)
-    input_grad = call(join_kernel, shaped((OWN, CELLS), BF16), [VMEM])(input_parts)
+        lambda *refs: relu_kernel(counted, *refs), shaped((OWN, CELLS), BF16), [VMEM] * 10
+    )(conv_out, params, *sums_one)
+    input_grad = call(
+        join_kernel,
+        shaped((OWN, CELLS), BF16),
+        [SMEM] + [VMEM] * NY,
+        [pltpu.VMEM((NY, OWN, SPAN), F32)],
+    )(place, *input_parts)
 
     summed = jnp.sum(filter_parts.astype(F32), axis=0) / math.sqrt(counted)
     weight_grad = jnp.transpose(summed[:, : 27 * OWN].reshape(GROUP, 27, OWN), (1, 0, 2))

time: 191 us -> 244 us (1.28)
  starting transfers between devices: 35.3 us -> 199 us
  blocking collectives: 64.7 us -> 0 us
  waiting for transfers between devices: 61.3 us -> 13.4 us
  Pallas kernels: 18.9 us -> 23.1 us
  local copies, waits for them, and re-layouts: 8.55 us -> 5.02 us
    ppermute x0 -> x49, starting transfers between devices: none -> 170 us  [hop_to(): lax.ppermute(value, axis, [(at, (at + hop) % size) for at in range(size)])]
    all_to_all x4 -> x0, blocking collectives: 64.7 us -> none  [exchange(): return lax.all_to_all(value, axes, 0, 0, tiled=True)]
    all_to_all x6 -> x3, waiting for transfers between devices: 61.3 us -> 3.94 us  [exchange(): return lax.all_to_all(value, axes, 0, 0, tiled=True)]
    ppermute x0 -> x49, waiting for transfers between devices: none -> 9.47 us  [hop_to(): lax.ppermute(value, axis, [(at, (at + hop) % size) for at in range(size)])]
    all_to_all x6 -> x3, starting transfers between devices: 35.3 us -> 29.5 us  [exchange(): return lax.all_to_all(value, axes, 0, 0, tiled=True)]
    pallas_call x6 -> x7, Pallas kernels: 15.8 us -> 20 us  [the longest x1 5.6 us: shards(): call(filter_kernel, shaped((8, NY, GROUP, 128), BF16), [SMEM] + [VMEM] *...]
  transfers between devices with their start and end apart: 6 -> 52, of which waited for: 6 -> 6; matrix products, arithmetic and copies ran while one was open for 2% -> 0% of each run, Pallas kernels for 9% -> 7%
where the time goes in v2:
time: 244 us; the launch traced here: 242 us
  starting transfers between devices  199 us (82%)
  Pallas kernels  23.1 us (9%)
  waiting for transfers between devices  13.4 us (5%)
  local copies, waits for them, and re-layouts  5.02 us (2%)
    ppermute x49, starting transfers between devices, hop_to(): lax.ppermute(value, axis, [(at, (at + hop) % size) for at in range(size)])  170 us
    all_to_all x3, starting transfers between devices, exchange(): return lax.all_to_all(value, axes, 0, 0, tiled=True)  29.5 us
    ppermute x49, waiting for transfers between devices, hop_to(): lax.ppermute(value, axis, [(at, (at + hop) % size) for at in range(size)])  9.47 us
    pallas_call x1, Pallas kernels, shards(): call(filter_kernel, shaped((8, NY, GROUP, 128), BF16), [SMEM] + [VMEM] *...  5.6 us
    pallas_call x1, Pallas kernels, shards(): call(forward_kernel, [shaped((OWN, SPAN), F32)] * NY, [SMEM] + [VMEM] * (...  5.08 us
    pallas_call x1, Pallas kernels, shards(): call(backward_kernel, [shaped((OWN, SPAN), BF16)] * NY, [SMEM, VMEM, VMEM...  4.97 us
  transfers between devices with their start and end apart: 52, of which 6 were waited for; matrix products, arithmetic and copies ran while one was open for 0% of the time, Pallas kernels for 7%

profile of v2, /device:TPU:1, one launch (start us, length us, event | category | flops | bytes accessed | tf_op | source)
XLA Modules:
  0.0 242.5 jit_solution(3423362363316877085)
XLA Ops:
  1.5 0.9 copy-done.2
  2.4 1.1 shard_map.128
  4.4 4.2 %collective-permute-start = (bf16[32,256]{1,0:T(8,128)(2,1)S(1)}, bf16[32,256]{1,0:T(8,128)(2,1)S(1)}, u32[]{:S(2)}, u32[]{:S(2)}) collective-permute-start(bf16[32,256]{1,0:T(8,128)(2,1)S(1)} %pad.4), channel_id=1, source_target_pairs={{0,8},{8,16},{16,24},{24,32},{32,40},{40,48},{48,56},{56,0},{1,9},... | collective-permute-start | bytes 49160 | tf_op jit(solution)/shard_map/ppermute | solution.py:349
  8.6 4.2 %collective-permute-start.1 = (bf16[32,256]{1,0:T(8,128)(2,1)S(1)}, bf16[32,256]{1,0:T(8,128)(2,1)S(1)}, u32[]{:S(2)}, u32[]{:S(2)}) collective-permute-start(bf16[32,256]{1,0:T(8,128)(2,1)S(1)} %pad.4), channel_id=1, source_target_pairs={{0,16},{8,24},{16,32},{24,40},{32,48},{40,56},{48,0},{56,8},{1,17}... | collective-permute-start | bytes 49160 | tf_op jit(solution)/shard_map/ppermute | solution.py:349
  12.8 4.6 %collective-permute-start.2 = (bf16[32,256]{1,0:T(8,128)(2,1)S(1)}, bf16[32,256]{1,0:T(8,128)(2,1)S(1)}, u32[]{:S(2)}, u32[]{:S(2)}) collective-permute-start(bf16[32,256]{1,0:T(8,128)(2,1)S(1)} %pad.4), channel_id=1, source_target_pairs={{0,24},{8,32},{16,40},{24,48},{32,56},{40,0},{48,8},{56,16},{1,25}... | collective-permute-start | bytes 49160 | tf_op jit(solution)/shard_map/ppermute | solution.py:349
  17.5 3.5 %collective-permute-start.3 = (bf16[32,256]{1,0:T(8,128)(2,1)S(1)}, bf16[32,256]{1,0:T(8,128)(2,1)S(1)}, u32[]{:S(2)}, u32[]{:S(2)}) collective-permute-start(bf16[32,256]{1,0:T(8,128)(2,1)S(1)} %pad.4), channel_id=1, source_target_pairs={{0,32},{8,40},{16,48},{24,56},{32,0},{40,8},{48,16},{56,24},{1,33}... | collective-permute-start | bytes 49160 | tf_op jit(solution)/shard_map/ppermute | solution.py:349
  21.0 4.9 %collective-permute-start.4 = (bf16[32,256]{1,0:T(8,128)(2,1)S(1)}, bf16[32,256]{1,0:T(8,128)(2,1)S(1)}, u32[]{:S(2)}, u32[]{:S(2)}) collective-permute-start(bf16[32,256]{1,0:T(8,128)(2,1)S(1)} %pad.4), channel_id=1, source_target_pairs={{0,40},{8,48},{16,56},{24,0},{32,8},{40,16},{48,24},{56,32},{1,41}... | collective-permute-start | bytes 49160 | tf_op jit(solution)/shard_map/ppermute | solution.py:349
  25.9 6.4 %all-to-all-start = ((f32[8,4,128]{2,1,0:T(4,128)}), f32[8,4,128]{2,1,0:T(4,128)S(1)}, u32[]{:S(2)}, u32[]{:S(2)}) async-start(f32[8,4,128]{2,1,0:T(4,128)} %shard_map.128), calls=%async_computation | async-start | bytes 32768 | tf_op jit(solution)/shard_map/all_to_all | solution.py:344
  33.0 3.9 %all-to-all-done.refs_2_ = f32[8,4,128]{2,1,0:T(4,128)S(1)} async-done(((f32[8,4,128]{2,1,0:T(4,128)}), f32[8,4,128]{2,1,0:T(4,128)S(1)}, u32[]{:S(2)}, u32[]{:S(2)}) %all-to-all-start) | async-done | bytes 16416 | tf_op jit(solution)/shard_map/all_to_all | solution.py:344
  37.0 1.2 shard_map.129
  38.2 14.7 %all-to-all-start.1 = ((bf16[64,4,1536]{2,1,0:T(4,128)(2,1)}), bf16[64,4,1536]{2,1,0:T(4,128)(2,1)S(1)}, u32[]{:S(2)}, u32[]{:S(2)}) async-start(bf16[64,4,1536]{2,1,0:T(4,128)(2,1)} %get-tuple-element.76), calls=%async_computation.1 | async-start | bytes 1572864 | tf_op jit(solution)/shard_map/all_to_all | solution.py:344
  52.9 5.2 %collective-permute-start.5 = (bf16[32,256]{1,0:T(8,128)(2,1)S(1)}, bf16[32,256]{1,0:T(8,128)(2,1)S(1)}, u32[]{:S(2)}, u32[]{:S(2)}) collective-permute-start(bf16[32,256]{1,0:T(8,128)(2,1)S(1)} %pad.4), channel_id=1, source_target_pairs={{0,48},{8,56},{16,0},{24,8},{32,16},{40,24},{48,32},{56,40},{1,49}... | collective-permute-start | bytes 49160 | tf_op jit(solution)/shard_map/ppermute | solution.py:349
  58.2 3.2 %collective-permute-start.6 = (bf16[32,256]{1,0:T(8,128)(2,1)S(1)}, bf16[32,256]{1,0:T(8,128)(2,1)S(1)}, u32[]{:S(2)}, u32[]{:S(2)}) collective-permute-start(bf16[32,256]{1,0:T(8,128)(2,1)S(1)} %pad.4), channel_id=1, source_target_pairs={{0,56},{8,0},{16,8},{24,16},{32,24},{40,32},{48,40},{56,48},{1,57}... | collective-permute-start | bytes 49160 | tf_op jit(solution)/shard_map/ppermute | solution.py:349
  61.4 3.1 %collective-permute-start.14 = (bf16[192,256]{1,0:T(8,128)(2,1)S(1)}, bf16[192,256]{1,0:T(8,128)(2,1)S(1)}, u32[]{:S(2)}, u32[]{:S(2)}) collective-permute-start(bf16[192,256]{1,0:T(8,128)(2,1)S(1)} %bitcast.46), channel_id=1, source_target_pairs={{0,1},{1,2},{2,3},{3,4},{4,5},{5,6},{6,7},{7,0},{8,9},{9,10},{10,1... | collective-permute-start | bytes 294920 | tf_op jit(solution)/shard_map/ppermute | solution.py:349
  64.5 3.4 %collective-permute-start.15 = (bf16[192,256]{1,0:T(8,128)(2,1)S(1)}, bf16[192,256]{1,0:T(8,128)(2,1)S(1)}, u32[]{:S(2)}, u32[]{:S(2)}) collective-permute-start(bf16[192,256]{1,0:T(8,128)(2,1)S(1)} %bitcast.47), channel_id=1, source_target_pairs={{0,7},{1,0},{2,1},{3,2},{4,3},{5,4},{6,5},{7,6},{8,15},{9,8},{10,9... | collective-permute-start | bytes 294920 | tf_op jit(solution)/shard_map/ppermute | solution.py:349
  68.0 2.3 collective-permute-done.5
  70.6 2.9 %collective-permute-start.7 = (bf16[8,32,256]{2,1,0:T(8,128)(2,1)S(1)}, bf16[8,32,256]{2,1,0:T(8,128)(2,1)S(1)}, u32[]{:S(2)}, u32[]{:S(2)}) collective-permute-start(bf16[8,32,256]{2,1,0:T(8,128)(2,1)S(1)} %constant_dynamic-update-slice_fusion.refs_0_), channel_id=1, source_target_pairs={{0,64},{64,128},{128,192},{192,256},{256,320},{320,384},{384,448},... | collective-permute-start | bytes 393224 | tf_op jit(solution)/shard_map/ppermute | solution.py:349
  73.5 3.9 %collective-permute-done.14.refs_1_ = bf16[192,256]{1,0:T(8,128)(2,1)S(1)} collective-permute-done((bf16[192,256]{1,0:T(8,128)(2,1)S(1)}, bf16[192,256]{1,0:T(8,128)(2,1)S(1)}, u32[]{:S(2)}, u32[]{:S(2)}) %collective-permute-start.14) | collective-permute-done | bytes 98336 | tf_op jit(solution)/shard_map/ppermute | solution.py:349
  77.4 1.9 collective-permute-start.16
  80.0 2.6 %collective-permute-start.28 = (bf16[4,3840]{1,0:T(4,128)(2,1)S(1)}, bf16[4,3840]{1,0:T(4,128)(2,1)S(1)}, u32[]{:S(2)}, u32[]{:S(2)}) collective-permute-start(bf16[4,3840]{1,0:T(4,128)(2,1)S(1)} %get-tuple-element.109), channel_id=1, source_target_pairs={{0,8},{8,16},{16,24},{24,32},{32,40},{40,48},{48,56},{56,0},{1,9},... | collective-permute-start | bytes 92168 | tf_op jit(solution)/shard_map/ppermute | solution.py:349
  82.6 4.0 %collective-permute-start.29 = (bf16[4,3840]{1,0:T(4,128)(2,1)S(1)}, bf16[4,3840]{1,0:T(4,128)(2,1)S(1)}, u32[]{:S(2)}, u32[]{:S(2)}) collective-permute-start(bf16[4,3840]{1,0:T(4,128)(2,1)S(1)} %get-tuple-element.110), channel_id=1, source_target_pairs={{0,16},{8,24},{16,32},{24,40},{32,48},{40,56},{48,0},{56,8},{1,17}... | collective-permute-start | bytes 92168 | tf_op jit(solution)/shard_map/ppermute | solution.py:349
  86.7 2.2 collective-permute-start.8
  89.4 4.5 %collective-permute-start.9 = (bf16[8,32,256]{2,1,0:T(8,128)(2,1)S(1)}, bf16[8,32,256]{2,1,0:T(8,128)(2,1)S(1)}, u32[]{:S(2)}, u32[]{:S(2)}) collective-permute-start(bf16[8,32,256]{2,1,0:T(8,128)(2,1)S(1)} %constant_dynamic-update-slice_fusion.refs_0_), channel_id=1, source_target_pairs={{0,192},{64,256},{128,320},{192,384},{256,448},{320,0},{384,64},{4... | collective-permute-start | bytes 393224 | tf_op jit(solution)/shard_map/ppermute | solution.py:349
  93.9 4.0 %collective-permute-start.10 = (bf16[8,32,256]{2,1,0:T(8,128)(2,1)S(1)}, bf16[8,32,256]{2,1,0:T(8,128)(2,1)S(1)}, u32[]{:S(2)}, u32[]{:S(2)}) collective-permute-start(bf16[8,32,256]{2,1,0:T(8,128)(2,1)S(1)} %constant_dynamic-update-slice_fusion.refs_0_), channel_id=1, source_target_pairs={{0,256},{64,320},{128,384},{192,448},{256,0},{320,64},{384,128},{4... | collective-permute-start | bytes 393224 | tf_op jit(solution)/shard_map/ppermute | solution.py:349
  97.9 4.9 %collective-permute-start.17 = (bf16[192,256]{1,0:T(8,128)(2,1)S(1)}, bf16[192,256]{1,0:T(8,128)(2,1)S(1)}, u32[]{:S(2)}, u32[]{:S(2)}) collective-permute-start(bf16[192,256]{1,0:T(8,128)(2,1)S(1)} %collective-permute-done.15.refs_2_), channel_id=1, source_target_pairs={{0,7},{1,0},{2,1},{3,2},{4,3},{5,4},{6,5},{7,6},{8,15},{9,8},{10,9... | collective-permute-start | bytes 294920 | tf_op jit(solution)/shard_map/ppermute | solution.py:349
  102.8 1.9 collective-permute-start.18
  104.7 2.2 collective-permute-start.11
  106.9 3.1 %collective-permute-start.12 = (bf16[8,32,256]{2,1,0:T(8,128)(2,1)S(1)}, bf16[8,32,256]{2,1,0:T(8,128)(2,1)S(1)}, u32[]{:S(2)}, u32[]{:S(2)}) collective-permute-start(bf16[8,32,256]{2,1,0:T(8,128)(2,1)S(1)} %constant_dynamic-update-slice_fusion.refs_0_), channel_id=1, source_target_pairs={{0,384},{64,448},{128,0},{192,64},{256,128},{320,192},{384,256},{4... | collective-permute-start | bytes 393224 | tf_op jit(solution)/shard_map/ppermute | solution.py:349
  110.1 1.9 collective-permute-start.13
  111.9 4.6 %collective-permute-start.19 = (bf16[192,256]{1,0:T(8,128)(2,1)S(1)}, bf16[192,256]{1,0:T(8,128)(2,1)S(1)}, u32[]{:S(2)}, u32[]{:S(2)}) collective-permute-start(bf16[192,256]{1,0:T(8,128)(2,1)S(1)} %collective-permute-done.17.refs_4_), channel_id=1, source_target_pairs={{0,7},{1,0},{2,1},{3,2},{4,3},{5,4},{6,5},{7,6},{8,15},{9,8},{10,9... | collective-permute-start | bytes 294920 | tf_op jit(solution)/shard_map/ppermute | solution.py:349
  116.5 1.9 collective-permute-start.20
  118.5 3.8 %collective-permute-start.30 = (bf16[4,3840]{1,0:T(4,128)(2,1)S(1)}, bf16[4,3840]{1,0:T(4,128)(2,1)S(1)}, u32[]{:S(2)}, u32[]{:S(2)}) collective-permute-start(bf16[4,3840]{1,0:T(4,128)(2,1)S(1)} %get-tuple-element.111), channel_id=1, source_target_pairs={{0,24},{8,32},{16,40},{24,48},{32,56},{40,0},{48,8},{56,16},{1,25}... | collective-permute-start | bytes 92168 | tf_op jit(solution)/shard_map/ppermute | solution.py:349
  122.3 3.8 %collective-permute-start.31 = (bf16[4,3840]{1,0:T(4,128)(2,1)S(1)}, bf16[4,3840]{1,0:T(4,128)(2,1)S(1)}, u32[]{:S(2)}, u32[]{:S(2)}) collective-permute-start(bf16[4,3840]{1,0:T(4,128)(2,1)S(1)} %get-tuple-element.112), channel_id=1, source_target_pairs={{0,32},{8,40},{16,48},{24,56},{32,0},{40,8},{48,16},{56,24},{1,33}... | collective-permute-start | bytes 92168 | tf_op jit(solution)/shard_map/ppermute | solution.py:349
  126.1 6.2 %collective-permute-start.32 = (bf16[4,3840]{1,0:T(4,128)(2,1)S(1)}, bf16[4,3840]{1,0:T(4,128)(2,1)S(1)}, u32[]{:S(2)}, u32[]{:S(2)}) collective-permute-start(bf16[4,3840]{1,0:T(4,128)(2,1)S(1)} %get-tuple-element.113), channel_id=1, source_target_pairs={{0,40},{8,48},{16,56},{24,0},{32,8},{40,16},{48,24},{56,32},{1,41}... | collective-permute-start | bytes 92168 | tf_op jit(solution)/shard_map/ppermute | solution.py:349
  132.3 2.9 %collective-permute-start.33 = (bf16[4,3840]{1,0:T(4,128)(2,1)S(1)}, bf16[4,3840]{1,0:T(4,128)(2,1)S(1)}, u32[]{:S(2)}, u32[]{:S(2)}) collective-permute-start(bf16[4,3840]{1,0:T(4,128)(2,1)S(1)} %get-tuple-element.114), channel_id=1, source_target_pairs={{0,48},{8,56},{16,0},{24,8},{32,16},{40,24},{48,32},{56,40},{1,49}... | collective-permute-start | bytes 92168 | tf_op jit(solution)/shard_map/ppermute | solution.py:349
  135.2 2.0 collective-permute-start.34
  137.2 1.7 shard_map.130
  138.9 5.1 %shard_map.131 = (f32[4,3840]{1,0:T(4,128)S(1)}, f32[4,3840]{1,0:T(4,128)S(1)}, f32[4,3840]{1,0:T(4,128)S(1)}, f32[4,3840]{1,0:T(4,128)S(1)}, f32[4,3840]{1,0:T(...) custom-call(s32[3]{0:T(128)S(1)} %pad_add_fusion.place_ref, ...), custom_call_target="tpu_custom_call" | custom-call | flops 1000 | bytes 1000 | tf_op jit(solution)/shard_map/pallas_call | solution.py:430
  144.2 5.6 %shard_map.133 = bf16[8,8,32,128]{3,2,1,0:T(8,128)(2,1)} custom-call(s32[3]{0:T(128)S(1)} %pad_add_fusion.place_ref, bf16[256,1536]{1,0:T(8,128)(2,1)S(1)} %reshape.20.grads_ref, bf16[4,3840]{1,0:T(4,128)(2,1)S(1)} %get-tuple-element.108.refs_0_, bf16[4,3840]{1,0:T(4,128)(2,1)S(1)} %collective-permute-done.28.refs_1_, ...), custom_call_target="tpu_custom_call" | custom-call | flops 1000 | bytes 1000 | tf_op jit(solution)/shard_map/pallas_call | solution.py:442
  149.8 8.3 %all-to-all-start.2 = ((bf16[64,32,128]{2,1,0:T(8,128)(2,1)}), bf16[64,32,128]{2,1,0:T(8,128)(2,1)S(1)}, u32[]{:S(2)}, u32[]{:S(2)}) async-start(bf16[64,32,128]{2,1,0:T(8,128)(2,1)} %bitcast.25), calls=%async_computation.2 | async-start | bytes 1048576 | tf_op jit(solution)/shard_map/all_to_all | solution.py:344
  158.2 4.5 %collective-permute-start.21 = (f32[4,3840]{1,0:T(4,128)S(1)}, f32[4,3840]{1,0:T(4,128)S(1)}, u32[]{:S(2)}, u32[]{:S(2)}) collective-permute-start(f32[4,3840]{1,0:T(4,128)S(1)} %get-tuple-element.99), channel_id=1, source_target_pairs={{0,56},{8,0},{16,8},{24,16},{32,24},{40,32},{48,40},{56,48},{1,57}... | collective-permute-start | bytes 184328 | tf_op jit(solution)/shard_map/ppermute | solution.py:349
  162.7 4.0 %collective-permute-start.22 = (f32[4,3840]{1,0:T(4,128)S(1)}, f32[4,3840]{1,0:T(4,128)S(1)}, u32[]{:S(2)}, u32[]{:S(2)}) collective-permute-start(f32[4,3840]{1,0:T(4,128)S(1)} %get-tuple-element.100), channel_id=1, source_target_pairs={{0,48},{8,56},{16,0},{24,8},{32,16},{40,24},{48,32},{56,40},{1,49}... | collective-permute-start | bytes 184328 | tf_op jit(solution)/shard_map/ppermute | solution.py:349
  166.7 3.1 %collective-permute-start.23 = (f32[4,3840]{1,0:T(4,128)S(1)}, f32[4,3840]{1,0:T(4,128)S(1)}, u32[]{:S(2)}, u32[]{:S(2)}) collective-permute-start(f32[4,3840]{1,0:T(4,128)S(1)} %get-tuple-element.101), channel_id=1, source_target_pairs={{0,40},{8,48},{16,56},{24,0},{32,8},{40,16},{48,24},{56,32},{1,41}... | collective-permute-start | bytes 184328 | tf_op jit(solution)/shard_map/ppermute | solution.py:349
  169.8 5.2 %collective-permute-start.24 = (f32[4,3840]{1,0:T(4,128)S(1)}, f32[4,3840]{1,0:T(4,128)S(1)}, u32[]{:S(2)}, u32[]{:S(2)}) collective-permute-start(f32[4,3840]{1,0:T(4,128)S(1)} %get-tuple-element.102), channel_id=1, source_target_pairs={{0,32},{8,40},{16,48},{24,56},{32,0},{40,8},{48,16},{56,24},{1,33}... | collective-permute-start | bytes 184328 | tf_op jit(solution)/shard_map/ppermute | solution.py:349
  175.0 1.9 collective-permute-start.25
  176.9 5.2 %collective-permute-start.26 = (f32[4,3840]{1,0:T(4,128)S(1)}, f32[4,3840]{1,0:T(4,128)S(1)}, u32[]{:S(2)}, u32[]{:S(2)}) collective-permute-start(f32[4,3840]{1,0:T(4,128)S(1)} %get-tuple-element.104), channel_id=1, source_target_pairs={{0,16},{8,24},{16,32},{24,40},{32,48},{40,56},{48,0},{56,8},{1,17}... | collective-permute-start | bytes 184328 | tf_op jit(solution)/shard_map/ppermute | solution.py:349
  182.1 3.1 %collective-permute-start.27 = (f32[4,3840]{1,0:T(4,128)S(1)}, f32[4,3840]{1,0:T(4,128)S(1)}, u32[]{:S(2)}, u32[]{:S(2)}) collective-permute-start(f32[4,3840]{1,0:T(4,128)S(1)} %get-tuple-element.105), channel_id=1, source_target_pairs={{0,8},{8,16},{16,24},{24,32},{32,40},{40,48},{48,56},{56,0},{1,9},... | collective-permute-start | bytes 184328 | tf_op jit(solution)/shard_map/ppermute | solution.py:349
  185.2 5.0 %shard_map.134 = (bf16[4,3840]{1,0:T(4,128)(2,1)S(1)}, bf16[4,3840]{1,0:T(4,128)(2,1)S(1)}, bf16[4,3840]{1,0:T(4,128)(2,1)S(1)}, bf16[4,3840]{1,0:T(4,128)(2,1)S...) custom-call(s32[3]{0:T(128)S(1)} %pad_add_fusion.place_ref, ...), custom_call_target="tpu_custom_call" | custom-call | flops 1000 | bytes 1000 | tf_op jit(solution)/shard_map/pallas_call | solution.py:454
  190.2 3.4 %collective-permute-start.42 = (bf16[4,3840]{1,0:T(4,128)(2,1)S(1)}, bf16[4,3840]{1,0:T(4,128)(2,1)S(1)}, u32[]{:S(2)}, u32[]{:S(2)}) collective-permute-start(bf16[4,3840]{1,0:T(4,128)(2,1)S(1)} %get-tuple-element.136), channel_id=1, source_target_pairs={{0,56},{8,0},{16,8},{24,16},{32,24},{40,32},{48,40},{56,48},{1,57}... | collective-permute-start | bytes 92168 | tf_op jit(solution)/shard_map/ppermute | solution.py:349
  193.7 1.9 collective-permute-start.43
  196.3 3.7 %collective-permute-start.35 = (f32[4,128]{1,0:T(4,128)S(1)}, f32[4,128]{1,0:T(4,128)S(1)}, u32[]{:S(2)}, u32[]{:S(2)}) collective-permute-start(f32[4,128]{1,0:T(4,128)S(1)} %get-tuple-element.134.refs_2_), channel_id=1, source_target_pairs={{0,64},{64,128},{128,192},{192,256},{256,320},{320,384},{384,448},... | collective-permute-start | bytes 6152 | tf_op jit(solution)/shard_map/ppermute | solution.py:349
  200.0 3.2 %collective-permute-start.36 = (f32[4,128]{1,0:T(4,128)S(1)}, f32[4,128]{1,0:T(4,128)S(1)}, u32[]{:S(2)}, u32[]{:S(2)}) collective-permute-start(f32[4,128]{1,0:T(4,128)S(1)} %get-tuple-element.134.refs_2_), channel_id=1, source_target_pairs={{0,128},{64,192},{128,256},{192,320},{256,384},{320,448},{384,0},{... | collective-permute-start | bytes 6152 | tf_op jit(solution)/shard_map/ppermute | solution.py:349
  203.2 3.5 %collective-permute-start.37 = (f32[4,128]{1,0:T(4,128)S(1)}, f32[4,128]{1,0:T(4,128)S(1)}, u32[]{:S(2)}, u32[]{:S(2)}) collective-permute-start(f32[4,128]{1,0:T(4,128)S(1)} %get-tuple-element.134.refs_2_), channel_id=1, source_target_pairs={{0,192},{64,256},{128,320},{192,384},{256,448},{320,0},{384,64},{4... | collective-permute-start | bytes 6152 | tf_op jit(solution)/shard_map/ppermute | solution.py:349
  206.7 2.3 collective-permute-start.38
  209.0 3.9 %collective-permute-start.39 = (f32[4,128]{1,0:T(4,128)S(1)}, f32[4,128]{1,0:T(4,128)S(1)}, u32[]{:S(2)}, u32[]{:S(2)}) collective-permute-start(f32[4,128]{1,0:T(4,128)S(1)} %get-tuple-element.134.refs_2_), channel_id=1, source_target_pairs={{0,320},{64,384},{128,448},{192,0},{256,64},{320,128},{384,192},{4... | collective-permute-start | bytes 6152 | tf_op jit(solution)/shard_map/ppermute | solution.py:349
  213.0 2.7 %collective-permute-start.40 = (f32[4,128]{1,0:T(4,128)S(1)}, f32[4,128]{1,0:T(4,128)S(1)}, u32[]{:S(2)}, u32[]{:S(2)}) collective-permute-start(f32[4,128]{1,0:T(4,128)S(1)} %get-tuple-element.134.refs_2_), channel_id=1, source_target_pairs={{0,384},{64,448},{128,0},{192,64},{256,128},{320,192},{384,256},{4... | collective-permute-start | bytes 6152 | tf_op jit(solution)/shard_map/ppermute | solution.py:349
  215.7 1.5 collective-permute-start.41
  217.2 5.8 %collective-permute-start.44 = (bf16[4,3840]{1,0:T(4,128)(2,1)S(1)}, bf16[4,3840]{1,0:T(4,128)(2,1)S(1)}, u32[]{:S(2)}, u32[]{:S(2)}) collective-permute-start(bf16[4,3840]{1,0:T(4,128)(2,1)S(1)} %get-tuple-element.138), channel_id=1, source_target_pairs={{0,40},{8,48},{16,56},{24,0},{32,8},{40,16},{48,24},{56,32},{1,41}... | collective-permute-start | bytes 92168 | tf_op jit(solution)/shard_map/ppermute | solution.py:349
  223.0 4.0 %collective-permute-start.45 = (bf16[4,3840]{1,0:T(4,128)(2,1)S(1)}, bf16[4,3840]{1,0:T(4,128)(2,1)S(1)}, u32[]{:S(2)}, u32[]{:S(2)}) collective-permute-start(bf16[4,3840]{1,0:T(4,128)(2,1)S(1)} %get-tuple-element.139), channel_id=1, source_target_pairs={{0,32},{8,40},{16,48},{24,56},{32,0},{40,8},{48,16},{56,24},{1,33}... | collective-permute-start | bytes 92168 | tf_op jit(solution)/shard_map/ppermute | solution.py:349
  227.0 2.8 %collective-permute-start.46 = (bf16[4,3840]{1,0:T(4,128)(2,1)S(1)}, bf16[4,3840]{1,0:T(4,128)(2,1)S(1)}, u32[]{:S(2)}, u32[]{:S(2)}) collective-permute-start(bf16[4,3840]{1,0:T(4,128)(2,1)S(1)} %get-tuple-element.140), channel_id=1, source_target_pairs={{0,24},{8,32},{16,40},{24,48},{32,56},{40,0},{48,8},{56,16},{1,25}... | collective-permute-start | bytes 92168 | tf_op jit(solution)/shard_map/ppermute | solution.py:349
  229.8 4.7 %collective-permute-start.47 = (bf16[4,3840]{1,0:T(4,128)(2,1)S(1)}, bf16[4,3840]{1,0:T(4,128)(2,1)S(1)}, u32[]{:S(2)}, u32[]{:S(2)}) collective-permute-start(bf16[4,3840]{1,0:T(4,128)(2,1)S(1)} %get-tuple-element.141), channel_id=1, source_target_pairs={{0,16},{8,24},{16,32},{24,40},{32,48},{40,56},{48,0},{56,8},{1,17}... | collective-permute-start | bytes 92168 | tf_op jit(solution)/shard_map/ppermute | solution.py:349
  234.5 1.9 collective-permute-start.48
  238.0 2.3 collective-permute-done.48.refs_7_
  240.3 1.3 shard_map.137
  (93 shorter events, 7.5 us)
Async XLA Ops:
  0.6 0.9 copy-start
  1.5 0.9 copy-start.2
  2.4 1.1 copy-start.6
  3.5 0.8 copy-start.7
  4.4 32.7 %copy-start.3 = (bf16[1,4,12288]{2,1,0:T(4,128)(2,1)S(1)}, bf16[1,4,12288]{2,1,0:T(4,128)(2,1)}, u32[]{:S(2)}) copy-start(bf16[1,4,12288]{2,1,0:T(4,128)(2,1)} %param.14) | copy-start | bytes 294916
  4.4 32.6 %copy-start.1 = (bf16[1,4,12288]{2,1,0:T(4,128)(2,1)S(1)}, bf16[1,4,12288]{2,1,0:T(4,128)(2,1)}, u32[]{:S(2)}) copy-start(bf16[1,4,12288]{2,1,0:T(4,128)(2,1)} %param.13) | copy-start | bytes 294916
  4.4 48.5 %collective-permute-start = (bf16[32,256]{1,0:T(8,128)(2,1)S(1)}, bf16[32,256]{1,0:T(8,128)(2,1)S(1)}, u32[]{:S(2)}, u32[]{:S(2)}) collective-permute-start(bf16[32,256]{1,0:T(8,128)(2,1)S(1)} %pad.4), channel_id=1, source_target_pairs={{0,8},{8,16},{16,24},{24,32},{32,40},{40,48},{48,56},{56,0},{1,9},... | collective-permute-start | bytes 49160 | tf_op jit(solution)/shard_map/ppermute | solution.py:349
  8.6 49.6 %collective-permute-start.1 = (bf16[32,256]{1,0:T(8,128)(2,1)S(1)}, bf16[32,256]{1,0:T(8,128)(2,1)S(1)}, u32[]{:S(2)}, u32[]{:S(2)}) collective-permute-start(bf16[32,256]{1,0:T(8,128)(2,1)S(1)} %pad.4), channel_id=1, source_target_pairs={{0,16},{8,24},{16,32},{24,40},{32,48},{40,56},{48,0},{56,8},{1,17}... | collective-permute-start | bytes 49160 | tf_op jit(solution)/shard_map/ppermute | solution.py:349
  12.8 48.6 %collective-permute-start.2 = (bf16[32,256]{1,0:T(8,128)(2,1)S(1)}, bf16[32,256]{1,0:T(8,128)(2,1)S(1)}, u32[]{:S(2)}, u32[]{:S(2)}) collective-permute-start(bf16[32,256]{1,0:T(8,128)(2,1)S(1)} %pad.4), channel_id=1, source_target_pairs={{0,24},{8,32},{16,40},{24,48},{32,56},{40,0},{48,8},{56,16},{1,25}... | collective-permute-start | bytes 49160 | tf_op jit(solution)/shard_map/ppermute | solution.py:349
  17.5 47.1 %collective-permute-start.3 = (bf16[32,256]{1,0:T(8,128)(2,1)S(1)}, bf16[32,256]{1,0:T(8,128)(2,1)S(1)}, u32[]{:S(2)}, u32[]{:S(2)}) collective-permute-start(bf16[32,256]{1,0:T(8,128)(2,1)S(1)} %pad.4), channel_id=1, source_target_pairs={{0,32},{8,40},{16,48},{24,56},{32,0},{40,8},{48,16},{56,24},{1,33}... | collective-permute-start | bytes 49160 | tf_op jit(solution)/shard_map/ppermute | solution.py:349
  21.0 46.9 %collective-permute-start.4 = (bf16[32,256]{1,0:T(8,128)(2,1)S(1)}, bf16[32,256]{1,0:T(8,128)(2,1)S(1)}, u32[]{:S(2)}, u32[]{:S(2)}) collective-permute-start(bf16[32,256]{1,0:T(8,128)(2,1)S(1)} %pad.4), channel_id=1, source_target_pairs={{0,40},{8,48},{16,56},{24,0},{32,8},{40,16},{48,24},{56,32},{1,41}... | collective-permute-start | bytes 49160 | tf_op jit(solution)/shard_map/ppermute | solution.py:349
  25.9 11.0 %all-to-all-start = ((f32[8,4,128]{2,1,0:T(4,128)}), f32[8,4,128]{2,1,0:T(4,128)S(1)}, u32[]{:S(2)}, u32[]{:S(2)}) async-start(f32[8,4,128]{2,1,0:T(4,128)} %shard_map.128), calls=%async_computation | async-start | bytes 32768 | tf_op jit(solution)/shard_map/all_to_all | solution.py:344
  32.3 0.7 copy-start.8
  32.3 0.7 copy-start.9
  32.3 0.7 copy-start.10
  38.2 23.2 %copy-start.4 = (bf16[1,256,192]{1,2,0:T(8,128)(2,1)S(1)}, bf16[1,256,192]{1,2,0:T(8,128)(2,1)}, u32[]{:S(2)}) copy-start(bf16[1,256,192]{1,2,0:T(8,128)(2,1)} %param.9) | copy-start | bytes 294916
  38.2 105.8 %all-to-all-start.1 = ((bf16[64,4,1536]{2,1,0:T(4,128)(2,1)}), bf16[64,4,1536]{2,1,0:T(4,128)(2,1)S(1)}, u32[]{:S(2)}, u32[]{:S(2)}) async-start(bf16[64,4,1536]{2,1,0:T(4,128)(2,1)} %get-tuple-element.76), calls=%async_computation.1 | async-start | bytes 1572864 | tf_op jit(solution)/shard_map/all_to_all | solution.py:344
  52.9 17.3 %collective-permute-start.5 = (bf16[32,256]{1,0:T(8,128)(2,1)S(1)}, bf16[32,256]{1,0:T(8,128)(2,1)S(1)}, u32[]{:S(2)}, u32[]{:S(2)}) collective-permute-start(bf16[32,256]{1,0:T(8,128)(2,1)S(1)} %pad.4), channel_id=1, source_target_pairs={{0,48},{8,56},{16,0},{24,8},{32,16},{40,24},{48,32},{56,40},{1,49}... | collective-permute-start | bytes 49160 | tf_op jit(solution)/shard_map/ppermute | solution.py:349
  58.2 21.2 %copy-start.5 = (bf16[1,4,12288]{2,1,0:T(4,128)(2,1)S(1)}, bf16[1,4,12288]{2,1,0:T(4,128)(2,1)}, u32[]{:S(2)}) copy-start(bf16[1,4,12288]{2,1,0:T(4,128)(2,1)} %param.15) | copy-start | bytes 294916
  58.2 12.4 %collective-permute-start.6 = (bf16[32,256]{1,0:T(8,128)(2,1)S(1)}, bf16[32,256]{1,0:T(8,128)(2,1)S(1)}, u32[]{:S(2)}, u32[]{:S(2)}) collective-permute-start(bf16[32,256]{1,0:T(8,128)(2,1)S(1)} %pad.4), channel_id=1, source_target_pairs={{0,56},{8,0},{16,8},{24,16},{32,24},{40,32},{48,40},{56,48},{1,57}... | collective-permute-start | bytes 49160 | tf_op jit(solution)/shard_map/ppermute | solution.py:349
  61.4 16.0 %collective-permute-start.14 = (bf16[192,256]{1,0:T(8,128)(2,1)S(1)}, bf16[192,256]{1,0:T(8,128)(2,1)S(1)}, u32[]{:S(2)}, u32[]{:S(2)}) collective-permute-start(bf16[192,256]{1,0:T(8,128)(2,1)S(1)} %bitcast.46), channel_id=1, source_target_pairs={{0,1},{1,2},{2,3},{3,4},{4,5},{5,6},{6,7},{7,0},{8,9},{9,10},{10,1... | collective-permute-start | bytes 294920 | tf_op jit(solution)/shard_map/ppermute | solution.py:349
  64.5 29.3 %collective-permute-start.15 = (bf16[192,256]{1,0:T(8,128)(2,1)S(1)}, bf16[192,256]{1,0:T(8,128)(2,1)S(1)}, u32[]{:S(2)}, u32[]{:S(2)}) collective-permute-start(bf16[192,256]{1,0:T(8,128)(2,1)S(1)} %bitcast.47), channel_id=1, source_target_pairs={{0,7},{1,0},{2,1},{3,2},{4,3},{5,4},{6,5},{7,6},{8,15},{9,8},{10,9... | collective-permute-start | bytes 294920 | tf_op jit(solution)/shard_map/ppermute | solution.py:349
  70.6 27.3 %collective-permute-start.7 = (bf16[8,32,256]{2,1,0:T(8,128)(2,1)S(1)}, bf16[8,32,256]{2,1,0:T(8,128)(2,1)S(1)}, u32[]{:S(2)}, u32[]{:S(2)}) collective-permute-start(bf16[8,32,256]{2,1,0:T(8,128)(2,1)S(1)} %constant_dynamic-update-slice_fusion.refs_0_), channel_id=1, source_target_pairs={{0,64},{64,128},{128,192},{192,256},{256,320},{320,384},{384,448},... | collective-permute-start | bytes 393224 | tf_op jit(solution)/shard_map/ppermute | solution.py:349
  77.4 25.4 %collective-permute-start.16 = (bf16[192,256]{1,0:T(8,128)(2,1)S(1)}, bf16[192,256]{1,0:T(8,128)(2,1)S(1)}, u32[]{:S(2)}, u32[]{:S(2)}) collective-permute-start(bf16[192,256]{1,0:T(8,128)(2,1)S(1)} %collective-permute-done.14.refs_1_), channel_id=1, source_target_pairs={{0,1},{1,2},{2,3},{3,4},{4,5},{5,6},{6,7},{7,0},{8,9},{9,10},{10,1... | collective-permute-start | bytes 294920 | tf_op jit(solution)/shard_map/ppermute | solution.py:349
  80.0 6.7 %collective-permute-start.28 = (bf16[4,3840]{1,0:T(4,128)(2,1)S(1)}, bf16[4,3840]{1,0:T(4,128)(2,1)S(1)}, u32[]{:S(2)}, u32[]{:S(2)}) collective-permute-start(bf16[4,3840]{1,0:T(4,128)(2,1)S(1)} %get-tuple-element.109), channel_id=1, source_target_pairs={{0,8},{8,16},{16,24},{24,32},{32,40},{40,48},{48,56},{56,0},{1,9},... | collective-permute-start | bytes 92168 | tf_op jit(solution)/shard_map/ppermute | solution.py:349
  82.6 6.7 %collective-permute-start.29 = (bf16[4,3840]{1,0:T(4,128)(2,1)S(1)}, bf16[4,3840]{1,0:T(4,128)(2,1)S(1)}, u32[]{:S(2)}, u32[]{:S(2)}) collective-permute-start(bf16[4,3840]{1,0:T(4,128)(2,1)S(1)} %get-tuple-element.110), channel_id=1, source_target_pairs={{0,16},{8,24},{16,32},{24,40},{32,48},{40,56},{48,0},{56,8},{1,17}... | collective-permute-start | bytes 92168 | tf_op jit(solution)/shard_map/ppermute | solution.py:349
  86.7 18.0 %collective-permute-start.8 = (bf16[8,32,256]{2,1,0:T(8,128)(2,1)S(1)}, bf16[8,32,256]{2,1,0:T(8,128)(2,1)S(1)}, u32[]{:S(2)}, u32[]{:S(2)}) collective-permute-start(bf16[8,32,256]{2,1,0:T(8,128)(2,1)S(1)} %constant_dynamic-update-slice_fusion.refs_0_), channel_id=1, source_target_pairs={{0,128},{64,192},{128,256},{192,320},{256,384},{320,448},{384,0},{... | collective-permute-start | bytes 393224 | tf_op jit(solution)/shard_map/ppermute | solution.py:349
  89.4 17.5 %collective-permute-start.9 = (bf16[8,32,256]{2,1,0:T(8,128)(2,1)S(1)}, bf16[8,32,256]{2,1,0:T(8,128)(2,1)S(1)}, u32[]{:S(2)}, u32[]{:S(2)}) collective-permute-start(bf16[8,32,256]{2,1,0:T(8,128)(2,1)S(1)} %constant_dynamic-update-slice_fusion.refs_0_), channel_id=1, source_target_pairs={{0,192},{64,256},{128,320},{192,384},{256,448},{320,0},{384,64},{4... | collective-permute-start | bytes 393224 | tf_op jit(solution)/shard_map/ppermute | solution.py:349
  93.9 16.2 %collective-permute-start.10 = (bf16[8,32,256]{2,1,0:T(8,128)(2,1)S(1)}, bf16[8,32,256]{2,1,0:T(8,128)(2,1)S(1)}, u32[]{:S(2)}, u32[]{:S(2)}) collective-permute-start(bf16[8,32,256]{2,1,0:T(8,128)(2,1)S(1)} %constant_dynamic-update-slice_fusion.refs_0_), channel_id=1, source_target_pairs={{0,256},{64,320},{128,384},{192,448},{256,0},{320,64},{384,128},{4... | collective-permute-start | bytes 393224 | tf_op jit(solution)/shard_map/ppermute | solution.py:349
  97.9 14.0 %collective-permute-start.17 = (bf16[192,256]{1,0:T(8,128)(2,1)S(1)}, bf16[192,256]{1,0:T(8,128)(2,1)S(1)}, u32[]{:S(2)}, u32[]{:S(2)}) collective-permute-start(bf16[192,256]{1,0:T(8,128)(2,1)S(1)} %collective-permute-done.15.refs_2_), channel_id=1, source_target_pairs={{0,7},{1,0},{2,1},{3,2},{4,3},{5,4},{6,5},{7,6},{8,15},{9,8},{10,9... | collective-permute-start | bytes 294920 | tf_op jit(solution)/shard_map/ppermute | solution.py:349
  102.8 13.7 %collective-permute-start.18 = (bf16[192,256]{1,0:T(8,128)(2,1)S(1)}, bf16[192,256]{1,0:T(8,128)(2,1)S(1)}, u32[]{:S(2)}, u32[]{:S(2)}) collective-permute-start(bf16[192,256]{1,0:T(8,128)(2,1)S(1)} %collective-permute-done.16.refs_3_), channel_id=1, source_target_pairs={{0,1},{1,2},{2,3},{3,4},{4,5},{5,6},{6,7},{7,0},{8,9},{9,10},{10,1... | collective-permute-start | bytes 294920 | tf_op jit(solution)/shard_map/ppermute | solution.py:349
  104.7 13.7 %collective-permute-start.11 = (bf16[8,32,256]{2,1,0:T(8,128)(2,1)S(1)}, bf16[8,32,256]{2,1,0:T(8,128)(2,1)S(1)}, u32[]{:S(2)}, u32[]{:S(2)}) collective-permute-start(bf16[8,32,256]{2,1,0:T(8,128)(2,1)S(1)} %constant_dynamic-update-slice_fusion.refs_0_), channel_id=1, source_target_pairs={{0,320},{64,384},{128,448},{192,0},{256,64},{320,128},{384,192},{4... | collective-permute-start | bytes 393224 | tf_op jit(solution)/shard_map/ppermute | solution.py:349
  106.9 15.4 %collective-permute-start.12 = (bf16[8,32,256]{2,1,0:T(8,128)(2,1)S(1)}, bf16[8,32,256]{2,1,0:T(8,128)(2,1)S(1)}, u32[]{:S(2)}, u32[]{:S(2)}) collective-permute-start(bf16[8,32,256]{2,1,0:T(8,128)(2,1)S(1)} %constant_dynamic-update-slice_fusion.refs_0_), channel_id=1, source_target_pairs={{0,384},{64,448},{128,0},{192,64},{256,128},{320,192},{384,256},{4... | collective-permute-start | bytes 393224 | tf_op jit(solution)/shard_map/ppermute | solution.py:349
  110.1 16.0 %collective-permute-start.13 = (bf16[8,32,256]{2,1,0:T(8,128)(2,1)S(1)}, bf16[8,32,256]{2,1,0:T(8,128)(2,1)S(1)}, u32[]{:S(2)}, u32[]{:S(2)}) collective-permute-start(bf16[8,32,256]{2,1,0:T(8,128)(2,1)S(1)} %constant_dynamic-update-slice_fusion.refs_0_), channel_id=1, source_target_pairs={{0,448},{64,0},{128,64},{192,128},{256,192},{320,256},{384,320},{4... | collective-permute-start | bytes 393224 | tf_op jit(solution)/shard_map/ppermute | solution.py:349
  111.9 20.3 %collective-permute-start.19 = (bf16[192,256]{1,0:T(8,128)(2,1)S(1)}, bf16[192,256]{1,0:T(8,128)(2,1)S(1)}, u32[]{:S(2)}, u32[]{:S(2)}) collective-permute-start(bf16[192,256]{1,0:T(8,128)(2,1)S(1)} %collective-permute-done.17.refs_4_), channel_id=1, source_target_pairs={{0,7},{1,0},{2,1},{3,2},{4,3},{5,4},{6,5},{7,6},{8,15},{9,8},{10,9... | collective-permute-start | bytes 294920 | tf_op jit(solution)/shard_map/ppermute | solution.py:349
  116.5 18.7 %collective-permute-start.20 = (bf16[192,256]{1,0:T(8,128)(2,1)S(1)}, bf16[192,256]{1,0:T(8,128)(2,1)S(1)}, u32[]{:S(2)}, u32[]{:S(2)}) collective-permute-start(bf16[192,256]{1,0:T(8,128)(2,1)S(1)} %collective-permute-done.18.refs_5_), channel_id=1, source_target_pairs={{0,1},{1,2},{2,3},{3,4},{4,5},{5,6},{6,7},{7,0},{8,9},{9,10},{10,1... | collective-permute-start | bytes 294920 | tf_op jit(solution)/shard_map/ppermute | solution.py:349
  118.5 25.7 %collective-permute-start.30 = (bf16[4,3840]{1,0:T(4,128)(2,1)S(1)}, bf16[4,3840]{1,0:T(4,128)(2,1)S(1)}, u32[]{:S(2)}, u32[]{:S(2)}) collective-permute-start(bf16[4,3840]{1,0:T(4,128)(2,1)S(1)} %get-tuple-element.111), channel_id=1, source_target_pairs={{0,24},{8,32},{16,40},{24,48},{32,56},{40,0},{48,8},{56,16},{1,25}... | collective-permute-start | bytes 92168 | tf_op jit(solution)/shard_map/ppermute | solution.py:349
  122.3 21.9 %collective-permute-start.31 = (bf16[4,3840]{1,0:T(4,128)(2,1)S(1)}, bf16[4,3840]{1,0:T(4,128)(2,1)S(1)}, u32[]{:S(2)}, u32[]{:S(2)}) collective-permute-start(bf16[4,3840]{1,0:T(4,128)(2,1)S(1)} %get-tuple-element.112), channel_id=1, source_target_pairs={{0,32},{8,40},{16,48},{24,56},{32,0},{40,8},{48,16},{56,24},{1,33}... | collective-permute-start | bytes 92168 | tf_op jit(solution)/shard_map/ppermute | solution.py:349
  126.1 18.2 %collective-permute-start.32 = (bf16[4,3840]{1,0:T(4,128)(2,1)S(1)}, bf16[4,3840]{1,0:T(4,128)(2,1)S(1)}, u32[]{:S(2)}, u32[]{:S(2)}) collective-permute-start(bf16[4,3840]{1,0:T(4,128)(2,1)S(1)} %get-tuple-element.113), channel_id=1, source_target_pairs={{0,40},{8,48},{16,56},{24,0},{32,8},{40,16},{48,24},{56,32},{1,41}... | collective-permute-start | bytes 92168 | tf_op jit(solution)/shard_map/ppermute | solution.py:349
  132.3 12.0 %collective-permute-start.33 = (bf16[4,3840]{1,0:T(4,128)(2,1)S(1)}, bf16[4,3840]{1,0:T(4,128)(2,1)S(1)}, u32[]{:S(2)}, u32[]{:S(2)}) collective-permute-start(bf16[4,3840]{1,0:T(4,128)(2,1)S(1)} %get-tuple-element.114), channel_id=1, source_target_pairs={{0,48},{8,56},{16,0},{24,8},{32,16},{40,24},{48,32},{56,40},{1,49}... | collective-permute-start | bytes 92168 | tf_op jit(solution)/shard_map/ppermute | solution.py:349
  135.2 9.1 %collective-permute-start.34 = (bf16[4,3840]{1,0:T(4,128)(2,1)S(1)}, bf16[4,3840]{1,0:T(4,128)(2,1)S(1)}, u32[]{:S(2)}, u32[]{:S(2)}) collective-permute-start(bf16[4,3840]{1,0:T(4,128)(2,1)S(1)} %get-tuple-element.115), channel_id=1, source_target_pairs={{0,56},{8,0},{16,8},{24,16},{32,24},{40,32},{48,40},{56,48},{1,57}... | collective-permute-start | bytes 92168 | tf_op jit(solution)/shard_map/ppermute | solution.py:349
  149.8 91.8 %all-to-all-start.2 = ((bf16[64,32,128]{2,1,0:T(8,128)(2,1)}), bf16[64,32,128]{2,1,0:T(8,128)(2,1)S(1)}, u32[]{:S(2)}, u32[]{:S(2)}) async-start(bf16[64,32,128]{2,1,0:T(8,128)(2,1)} %bitcast.25), calls=%async_computation.2 | async-start | bytes 1048576 | tf_op jit(solution)/shard_map/all_to_all | solution.py:344
  158.2 18.7 %collective-permute-start.21 = (f32[4,3840]{1,0:T(4,128)S(1)}, f32[4,3840]{1,0:T(4,128)S(1)}, u32[]{:S(2)}, u32[]{:S(2)}) collective-permute-start(f32[4,3840]{1,0:T(4,128)S(1)} %get-tuple-element.99), channel_id=1, source_target_pairs={{0,56},{8,0},{16,8},{24,16},{32,24},{40,32},{48,40},{56,48},{1,57}... | collective-permute-start | bytes 184328 | tf_op jit(solution)/shard_map/ppermute | solution.py:349
  162.7 19.4 %collective-permute-start.22 = (f32[4,3840]{1,0:T(4,128)S(1)}, f32[4,3840]{1,0:T(4,128)S(1)}, u32[]{:S(2)}, u32[]{:S(2)}) collective-permute-start(f32[4,3840]{1,0:T(4,128)S(1)} %get-tuple-element.100), channel_id=1, source_target_pairs={{0,48},{8,56},{16,0},{24,8},{32,16},{40,24},{48,32},{56,40},{1,49}... | collective-permute-start | bytes 184328 | tf_op jit(solution)/shard_map/ppermute | solution.py:349
  166.7 23.5 %collective-permute-start.23 = (f32[4,3840]{1,0:T(4,128)S(1)}, f32[4,3840]{1,0:T(4,128)S(1)}, u32[]{:S(2)}, u32[]{:S(2)}) collective-permute-start(f32[4,3840]{1,0:T(4,128)S(1)} %get-tuple-element.101), channel_id=1, source_target_pairs={{0,40},{8,48},{16,56},{24,0},{32,8},{40,16},{48,24},{56,32},{1,41}... | collective-permute-start | bytes 184328 | tf_op jit(solution)/shard_map/ppermute | solution.py:349
  169.8 20.4 %collective-permute-start.24 = (f32[4,3840]{1,0:T(4,128)S(1)}, f32[4,3840]{1,0:T(4,128)S(1)}, u32[]{:S(2)}, u32[]{:S(2)}) collective-permute-start(f32[4,3840]{1,0:T(4,128)S(1)} %get-tuple-element.102), channel_id=1, source_target_pairs={{0,32},{8,40},{16,48},{24,56},{32,0},{40,8},{48,16},{56,24},{1,33}... | collective-permute-start | bytes 184328 | tf_op jit(solution)/shard_map/ppermute | solution.py:349
  175.0 15.2 %collective-permute-start.25 = (f32[4,3840]{1,0:T(4,128)S(1)}, f32[4,3840]{1,0:T(4,128)S(1)}, u32[]{:S(2)}, u32[]{:S(2)}) collective-permute-start(f32[4,3840]{1,0:T(4,128)S(1)} %get-tuple-element.103), channel_id=1, source_target_pairs={{0,24},{8,32},{16,40},{24,48},{32,56},{40,0},{48,8},{56,16},{1,25}... | collective-permute-start | bytes 184328 | tf_op jit(solution)/shard_map/ppermute | solution.py:349
  176.9 13.3 %collective-permute-start.26 = (f32[4,3840]{1,0:T(4,128)S(1)}, f32[4,3840]{1,0:T(4,128)S(1)}, u32[]{:S(2)}, u32[]{:S(2)}) collective-permute-start(f32[4,3840]{1,0:T(4,128)S(1)} %get-tuple-element.104), channel_id=1, source_target_pairs={{0,16},{8,24},{16,32},{24,40},{32,48},{40,56},{48,0},{56,8},{1,17}... | collective-permute-start | bytes 184328 | tf_op jit(solution)/shard_map/ppermute | solution.py:349
  182.1 8.1 %collective-permute-start.27 = (f32[4,3840]{1,0:T(4,128)S(1)}, f32[4,3840]{1,0:T(4,128)S(1)}, u32[]{:S(2)}, u32[]{:S(2)}) collective-permute-start(f32[4,3840]{1,0:T(4,128)S(1)} %get-tuple-element.105), channel_id=1, source_target_pairs={{0,8},{8,16},{16,24},{24,32},{32,40},{40,48},{48,56},{56,0},{1,9},... | collective-permute-start | bytes 184328 | tf_op jit(solution)/shard_map/ppermute | solution.py:349
  190.2 39.6 %collective-permute-start.42 = (bf16[4,3840]{1,0:T(4,128)(2,1)S(1)}, bf16[4,3840]{1,0:T(4,128)(2,1)S(1)}, u32[]{:S(2)}, u32[]{:S(2)}) collective-permute-start(bf16[4,3840]{1,0:T(4,128)(2,1)S(1)} %get-tuple-element.136), channel_id=1, source_target_pairs={{0,56},{8,0},{16,8},{24,16},{32,24},{40,32},{48,40},{56,48},{1,57}... | collective-permute-start | bytes 92168 | tf_op jit(solution)/shard_map/ppermute | solution.py:349
  193.7 40.8 %collective-permute-start.43 = (bf16[4,3840]{1,0:T(4,128)(2,1)S(1)}, bf16[4,3840]{1,0:T(4,128)(2,1)S(1)}, u32[]{:S(2)}, u32[]{:S(2)}) collective-permute-start(bf16[4,3840]{1,0:T(4,128)(2,1)S(1)} %get-tuple-element.137), channel_id=1, source_target_pairs={{0,48},{8,56},{16,0},{24,8},{32,16},{40,24},{48,32},{56,40},{1,49}... | collective-permute-start | bytes 92168 | tf_op jit(solution)/shard_map/ppermute | solution.py:349
  196.3 10.4 %collective-permute-start.35 = (f32[4,128]{1,0:T(4,128)S(1)}, f32[4,128]{1,0:T(4,128)S(1)}, u32[]{:S(2)}, u32[]{:S(2)}) collective-permute-start(f32[4,128]{1,0:T(4,128)S(1)} %get-tuple-element.134.refs_2_), channel_id=1, source_target_pairs={{0,64},{64,128},{128,192},{192,256},{256,320},{320,384},{384,448},... | collective-permute-start | bytes 6152 | tf_op jit(solution)/shard_map/ppermute | solution.py:349
  200.0 9.0 %collective-permute-start.36 = (f32[4,128]{1,0:T(4,128)S(1)}, f32[4,128]{1,0:T(4,128)S(1)}, u32[]{:S(2)}, u32[]{:S(2)}) collective-permute-start(f32[4,128]{1,0:T(4,128)S(1)} %get-tuple-element.134.refs_2_), channel_id=1, source_target_pairs={{0,128},{64,192},{128,256},{192,320},{256,384},{320,448},{384,0},{... | collective-permute-start | bytes 6152 | tf_op jit(solution)/shard_map/ppermute | solution.py:349
  203.2 9.8 %collective-permute-start.37 = (f32[4,128]{1,0:T(4,128)S(1)}, f32[4,128]{1,0:T(4,128)S(1)}, u32[]{:S(2)}, u32[]{:S(2)}) collective-permute-start(f32[4,128]{1,0:T(4,128)S(1)} %get-tuple-element.134.refs_2_), channel_id=1, source_target_pairs={{0,192},{64,256},{128,320},{192,384},{256,448},{320,0},{384,64},{4... | collective-permute-start | bytes 6152 | tf_op jit(solution)/shard_map/ppermute | solution.py:349
  206.7 9.0 %collective-permute-start.38 = (f32[4,128]{1,0:T(4,128)S(1)}, f32[4,128]{1,0:T(4,128)S(1)}, u32[]{:S(2)}, u32[]{:S(2)}) collective-permute-start(f32[4,128]{1,0:T(4,128)S(1)} %get-tuple-element.134.refs_2_), channel_id=1, source_target_pairs={{0,256},{64,320},{128,384},{192,448},{256,0},{320,64},{384,128},{4... | collective-permute-start | bytes 6152 | tf_op jit(solution)/shard_map/ppermute | solution.py:349
  209.0 8.2 %collective-permute-start.39 = (f32[4,128]{1,0:T(4,128)S(1)}, f32[4,128]{1,0:T(4,128)S(1)}, u32[]{:S(2)}, u32[]{:S(2)}) collective-permute-start(f32[4,128]{1,0:T(4,128)S(1)} %get-tuple-element.134.refs_2_), channel_id=1, source_target_pairs={{0,320},{64,384},{128,448},{192,0},{256,64},{320,128},{384,192},{4... | collective-permute-start | bytes 6152 | tf_op jit(solution)/shard_map/ppermute | solution.py:349
  213.0 10.0 %collective-permute-start.40 = (f32[4,128]{1,0:T(4,128)S(1)}, f32[4,128]{1,0:T(4,128)S(1)}, u32[]{:S(2)}, u32[]{:S(2)}) collective-permute-start(f32[4,128]{1,0:T(4,128)S(1)} %get-tuple-element.134.refs_2_), channel_id=1, source_target_pairs={{0,384},{64,448},{128,0},{192,64},{256,128},{320,192},{384,256},{4... | collective-permute-start | bytes 6152 | tf_op jit(solution)/shard_map/ppermute | solution.py:349
  215.7 11.3 %collective-permute-start.41 = (f32[4,128]{1,0:T(4,128)S(1)}, f32[4,128]{1,0:T(4,128)S(1)}, u32[]{:S(2)}, u32[]{:S(2)}) collective-permute-start(f32[4,128]{1,0:T(4,128)S(1)} %get-tuple-element.134.refs_2_), channel_id=1, source_target_pairs={{0,448},{64,0},{128,64},{192,128},{256,192},{320,256},{384,320},{4... | collective-permute-start | bytes 6152 | tf_op jit(solution)/shard_map/ppermute | solution.py:349
  217.2 20.7 %collective-permute-start.44 = (bf16[4,3840]{1,0:T(4,128)(2,1)S(1)}, bf16[4,3840]{1,0:T(4,128)(2,1)S(1)}, u32[]{:S(2)}, u32[]{:S(2)}) collective-permute-start(bf16[4,3840]{1,0:T(4,128)(2,1)S(1)} %get-tuple-element.138), channel_id=1, source_target_pairs={{0,40},{8,48},{16,56},{24,0},{32,8},{40,16},{48,24},{56,32},{1,41}... | collective-permute-start | bytes 92168 | tf_op jit(solution)/shard_map/ppermute | solution.py:349
  223.0 15.0 %collective-permute-start.45 = (bf16[4,3840]{1,0:T(4,128)(2,1)S(1)}, bf16[4,3840]{1,0:T(4,128)(2,1)S(1)}, u32[]{:S(2)}, u32[]{:S(2)}) collective-permute-start(bf16[4,3840]{1,0:T(4,128)(2,1)S(1)} %get-tuple-element.139), channel_id=1, source_target_pairs={{0,32},{8,40},{16,48},{24,56},{32,0},{40,8},{48,16},{56,24},{1,33}... | collective-permute-start | bytes 92168 | tf_op jit(solution)/shard_map/ppermute | solution.py:349
  227.0 11.0 %collective-permute-start.46 = (bf16[4,3840]{1,0:T(4,128)(2,1)S(1)}, bf16[4,3840]{1,0:T(4,128)(2,1)S(1)}, u32[]{:S(2)}, u32[]{:S(2)}) collective-permute-start(bf16[4,3840]{1,0:T(4,128)(2,1)S(1)} %get-tuple-element.140), channel_id=1, source_target_pairs={{0,24},{8,32},{16,40},{24,48},{32,56},{40,0},{48,8},{56,16},{1,25}... | collective-permute-start | bytes 92168 | tf_op jit(solution)/shard_map/ppermute | solution.py:349
  229.8 8.2 %collective-permute-start.47 = (bf16[4,3840]{1,0:T(4,128)(2,1)S(1)}, bf16[4,3840]{1,0:T(4,128)(2,1)S(1)}, u32[]{:S(2)}, u32[]{:S(2)}) collective-permute-start(bf16[4,3840]{1,0:T(4,128)(2,1)S(1)} %get-tuple-element.141), channel_id=1, source_target_pairs={{0,16},{8,24},{16,32},{24,40},{32,48},{40,56},{48,0},{56,8},{1,17}... | collective-permute-start | bytes 92168 | tf_op jit(solution)/shard_map/ppermute | solution.py:349
  234.5 5.8 %collective-permute-start.48 = (bf16[4,3840]{1,0:T(4,128)(2,1)S(1)}, bf16[4,3840]{1,0:T(4,128)(2,1)S(1)}, u32[]{:S(2)}, u32[]{:S(2)}) collective-permute-start(bf16[4,3840]{1,0:T(4,128)(2,1)S(1)} %get-tuple-element.142), channel_id=1, source_target_pairs={{0,8},{8,16},{16,24},{24,32},{32,40},{40,48},{48,56},{56,0},{1,9},... | collective-permute-start | bytes 92168 | tf_op jit(solution)/shard_map/ppermute | solution.py:349

commit v3 on v1

--- a/solution.py
+++ b/solution.py
@@ -14,6 +14,7 @@
 REACH = PLANE + EDGE
 SPAN = BLOCK + 2 * REACH
 CELLS = 12288
+HALF = 6144
 NY = 8
 NZ = 8
 OWN = 4
@@ -85,14 +86,41 @@
     lax.fori_loop(0, GROUP // 8, rows, 0)
 
 
-def forward_kernel(base_ref, weight_ref, cells_ref, out_ref, terms):
+def forward_kernel(weight_ref, cells_ref, own_ref, other_ref, terms, held):
     def columns(step, carry):
         part = pl.ds(pl.multiple_of(step * 256, 256), 256)
         terms[:, part] = nt_dot(weight_ref[...], cells_ref[part, :])
         return carry
 
-    lax.fori_loop(0, BLOCK // 256, columns, 0)
-    spread(base_ref[0], terms, out_ref, 1)
+    lax.fori_loop(0, HALF // 256, columns, 0)
+    held[...] = jnp.zeros_like(held)
+
+    def plane(at, carry):
+        lane = iota((8, PLANE), 1)
+        along_x, along_y = lane & 31, lax.shift_right_logical(lane, 5)
+        ends = {1: along_x >= 1, -1: along_x <= 30}
+        sides = {1: along_y >= 1, -1: along_y <= 30}
+        part = pl.ds(pl.multiple_of(at * PLANE, PLANE), PLANE)
+        for a in (-1, 0, 1):
+            total = None
+            for b in (-1, 0, 1):
+                line = None
+                for c in (-1, 0, 1):
+                    index = 9 * (a + 1) + 3 * (b + 1) + (c + 1)
+                    term = terms[8 * index : 8 * index + 8, part]
+                    if c != 0:
+                        term = shift(jnp.where(ends[c], term, 0.0), c)
+                    line = term if line is None else line + term
+                if b != 0:
+                    line = shift(jnp.where(sides[b], line, 0.0), 32 * b)
+                total = line if total is None else total + line
+            goal = pl.ds(pl.multiple_of((at + 1 - a) * PLANE, PLANE), PLANE)
+            held[:, goal] += total
+        return carry
+
+    lax.fori_loop(0, HALF // PLANE, plane, 0)
+    own_ref[...] = held[:OWN]
+    other_ref[...] = held[OWN:]
 
 
 def backward_kernel(base_ref, weight_ref, grads_ref, out_ref, terms):
@@ -178,9 +206,7 @@
 
 
 def from_lanes(sums_ref, count):
-    total = sums_ref[0]
-    for vol in range(1, sums_ref.shape[0]):
-        total = total + sums_ref[vol]
+    total = sums_ref[...]
     lane = iota((OWN, 128), 1)
     return [
         jnp.sum(jnp.where(lane == index, total, 0.0), axis=1, keepdims=True)
@@ -188,29 +214,28 @@
     ]
 
 
-def to_volumes(sums_ref, values):
-    row = in_lanes(values)
-    for vol in range(sums_ref.shape[0]):
-        sums_ref[vol] = row
+def fetch(pairs, arrived):
+    copies = [
+        pltpu.make_async_copy(source, goal, arrived.at[index])
+        for index, (source, goal) in enumerate(pairs)
+    ]
+    for copy in copies:
+        copy.start()
+    for copy in copies:
+        copy.wait()
 
 
 def sums_kernel(saved_hbm, upstream_hbm, sums_ref, saved_ref, upstream_ref, arrived):
-    first = pltpu.make_async_copy(saved_hbm, saved_ref, arrived.at[0])
-    second = pltpu.make_async_copy(upstream_hbm, upstream_ref, arrived.at[1])
-    first.start()
-    second.start()
-    first.wait()
-    second.wait()
+    fetch(((saved_hbm, saved_ref), (upstream_hbm, upstream_ref)), arrived)
     saved = saved_ref[...].astype(F32)
     upstream = upstream_ref[...].astype(F32)
-    to_volumes(
-        sums_ref,
+    sums_ref[...] = in_lanes(
         [
             lane_sum(saved),
             lane_sum(saved * saved),
             lane_sum(upstream),
             lane_sum(upstream * saved),
-        ],
+        ]
     )
 
 
@@ -225,7 +250,19 @@
             packed_ref[block, :, high - start :] = jnp.zeros((OWN, start + SPAN - high), BF16)
 
 
-def grad_kernel(counted, saved_ref, upstream_ref, sums_ref, params_ref, packed_ref, means_ref):
+def grad_kernel(
+    counted,
+    saved_hbm,
+    upstream_hbm,
+    sums_ref,
+    params_ref,
+    packed_ref,
+    means_ref,
+    saved_ref,
+    upstream_ref,
+    arrived,
+):
+    fetch(((saved_hbm, saved_ref), (upstream_hbm, upstream_ref)), arrived)
     saved_sum, square_sum, upstream_sum, product_sum = from_lanes(sums_ref, 4)
     mean = saved_sum / counted
     var = square_sum / counted - mean * mean
@@ -257,15 +294,15 @@
     return jnp.concatenate(pieces, axis=1)
 
 
-def join_stats_kernel(parts_ref, out_ref, sums_ref):
-    total = jnp.zeros((OWN, 128), F32)
-    squares = jnp.zeros((OWN, 128), F32)
-    for block in range(NY):
-        cells = joined(parts_ref, block)
-        out_ref[:, block * BLOCK : (block + 1) * BLOCK] = cells
-        total = total + lane_sum(cells)
-        squares = squares + lane_sum(cells * cells)
-    to_volumes(sums_ref, [total, squares])
+def join_stats_kernel(half_ref, own_ref, other_ref, out_ref, sums_ref, held):
+    held[...] = jnp.zeros_like(held)
+    mine = half_ref[0] * HALF
+    span = HALF + 2 * PLANE
+    held[:, pl.ds(pl.multiple_of(mine, PLANE), span)] += own_ref[...]
+    held[:, pl.ds(pl.multiple_of(HALF - mine, PLANE), span)] += other_ref[...]
+    cells = held[:, PLANE : PLANE + CELLS]
+    out_ref[...] = cells
+    sums_ref[...] = in_lanes([lane_sum(cells), lane_sum(cells * cells)])
 
 
 def join_kernel(parts_ref, out_ref):
@@ -300,10 +337,6 @@
 
 def exchange(value, axes):
     return lax.all_to_all(value, axes, 0, 0, tiled=True)
-
-
-def to_all(value, axis):
-    return exchange(jnp.broadcast_to(value[None], (lax.axis_size(axis),) + value.shape), axis)
 
 
 def shards(
@@ -317,79 +350,78 @@
     weight_two,
     gain_two,
 ):
-    volumes = lax.axis_size("vol")
-    counted = volumes * CELLS
-    base = (lax.axis_index("y") * BLOCK).astype(jnp.int32).reshape(1)
+    y_axes = ("y_half", "y_rest")
+    counted = lax.axis_size("vol") * CELLS
+    half = lax.axis_index("y_half").astype(jnp.int32).reshape(1)
+    base = (lax.axis_index(y_axes) * BLOCK).astype(jnp.int32).reshape(1)
     params = jnp.broadcast_to(
         jnp.stack([gain_one, bias_one, gain_two])[:, :, None], (3, OWN, 128)
     )
     saved, upstream = saved_conv[0], cotangent[0]
-
-    sums_two = call(
-        sums_kernel,
-        shaped((volumes, OWN, 128), F32),
-        [pl.BlockSpec(memory_space=pl.ANY)] * 2,
-        [
-            pltpu.VMEM((OWN, CELLS), BF16),
-            pltpu.VMEM((OWN, CELLS), BF16),
-            pltpu.SemaphoreType.DMA((2,)),
-        ],
-    )(saved, upstream)
-    weight_one, sums_two = lax.optimization_barrier((weight_one, sums_two))
-    sums_two = exchange(sums_two, "vol")
-
-    cells = to_all(fwd_input[0].T, "z").reshape(BLOCK, CH)
-    rows = jnp.concatenate(
-        [jnp.transpose(weight_one, (1, 0, 2)), jnp.transpose(weight_two, (2, 0, 1))]
-    )
-    row = lax.dynamic_index_in_dim(rows, lax.axis_index("vol"), 0, keepdims=False)
-    rows = to_all(to_all(row, "y"), "vol")
-    weights = [
-        jnp.transpose(rows[first : first + OWN], (2, 1, 0, 3)).reshape(ROWS, CH)
-        for first in (0, OWN)
+    fetched = [
+        pltpu.VMEM((OWN, CELLS), BF16),
+        pltpu.VMEM((OWN, CELLS), BF16),
+        pltpu.SemaphoreType.DMA((2,)),
     ]
+    hbm = pl.BlockSpec(memory_space=pl.ANY)
+
+    cells = lax.all_gather(fwd_input[0].T, ("y_rest", "z"), axis=0, tiled=True)
+
+    sums_two = call(sums_kernel, shaped((OWN, 128), F32), [hbm] * 2, fetched)(saved, upstream)
     acts = call(pack_kernel, shaped((NY, OWN, SPAN), BF16), [VMEM])(saved_input[0])
-    acts = exchange(acts, "y").reshape(GROUP, SPAN)
+    acts = exchange(acts, y_axes)
+    sums_two = lax.psum(sums_two, "vol")
+    acts, sums_two = lax.optimization_barrier((acts, sums_two))
+    acts = acts.reshape(GROUP, SPAN)
 
     packed, means = call(
         lambda *refs: grad_kernel(counted, *refs),
         (shaped((NY * NZ, OWN, BLOCK), BF16), shaped((OWN, 128), F32)),
-        [VMEM] * 4,
+        [hbm] * 2 + [VMEM] * 2,
+        fetched,
     )(saved, upstream, sums_two, params)
-    grads = exchange(packed, ("y", "z")).reshape(CH, BLOCK)
-
-    cells, means = lax.optimization_barrier((cells, means))
-    conv_parts = call(
-        forward_kernel,
-        shaped((NY, OWN, SPAN), F32),
-        [SMEM, VMEM, VMEM],
-        [pltpu.VMEM((ROWS, BLOCK), F32)],
-    )(base, weights[0], cells)
-    grads, conv_parts = lax.optimization_barrier((grads, conv_parts))
-    conv_parts = exchange(conv_parts, "y")
+
+    weight_one, weight_two, packed = lax.optimization_barrier((weight_one, weight_two, packed))
+    grads = exchange(packed, (*y_axes, "z"))
+    second = lax.all_gather(jnp.transpose(weight_two, (0, 2, 1)), y_axes, axis=0, tiled=False)
+    across = lax.ppermute(weight_one, "y_half", [(0, 1), (1, 0)])
+    first = jnp.concatenate([weight_one, across], axis=1).reshape(27 * 2 * OWN, CH)
+    second = jnp.transpose(second, (1, 0, 2, 3)).reshape(ROWS, CH)
+    grads, first, second = lax.optimization_barrier((grads, first, second))
+    grads = grads.reshape(CH, BLOCK)
+
     filter_parts = call(
         filter_kernel,
         shaped((8, NY, GROUP, 128), BF16),
         [SMEM, VMEM, VMEM],
         [pltpu.VMEM((1024, BLOCK), BF16), pltpu.VMEM((CH, 1024), BF16)],
     )(base, grads, acts)
-    weight, filter_parts = lax.optimization_barrier((weights[1], filter_parts))
-    filter_parts = exchange(filter_parts.reshape(8 * NY, GROUP, 128), ("vol", "y"))
+    second, filter_parts, cells = lax.optimization_barrier((second, filter_parts, cells))
+    filter_parts = exchange(filter_parts.reshape(8 * NY, GROUP, 128), ("vol", *y_axes))
     input_parts = call(
         backward_kernel,
         shaped((NY, OWN, SPAN), BF16),
         [SMEM, VMEM, VMEM],
         [pltpu.VMEM((ROWS, BLOCK), F32)],
-    )(base, weight, grads)
-    conv_parts, input_parts = lax.optimization_barrier((conv_parts, input_parts))
-    input_parts = exchange(input_parts, "y")
-
+    )(base, second, grads)
+    first, input_parts = lax.optimization_barrier((first, input_parts))
+    input_parts = exchange(input_parts, y_axes)
+
+    span = HALF + 2 * PLANE
+    own, other = call(
+        forward_kernel,
+        (shaped((OWN, span), F32), shaped((OWN, span), F32)),
+        [VMEM, VMEM],
+        [pltpu.VMEM((27 * 2 * OWN, HALF), F32), pltpu.VMEM((2 * OWN, span), F32)],
+    )(first, cells)
+    other = lax.ppermute(other, "y_half", [(0, 1), (1, 0)])
     conv_out, sums_one = call(
         join_stats_kernel,
-        (shaped((OWN, CELLS), F32), shaped((volumes, OWN, 128), F32)),
-        [VMEM],
-    )(conv_parts)
-    sums_one = exchange(sums_one, "vol")
+        (shaped((OWN, CELLS), F32), shaped((OWN, 128), F32)),
+        [SMEM, VMEM, VMEM],
+        [pltpu.VMEM((OWN, CELLS + 2 * PLANE), F32)],
+    )(half, own, other)
+    sums_one = lax.psum(sums_one, "vol")
     activation = call(
         lambda *refs: relu_kernel(counted, *refs), shaped((OWN, CELLS), BF16), [VMEM] * 3
     )(conv_out, sums_one, params)
@@ -401,8 +433,9 @@
 
 
 def solution(mesh):
-    cut = Mesh(mesh.devices.reshape(mesh.devices.shape[0], NY, NZ), ("vol", "y", "z"))
-    chan = ("y", "z")
+    names = ("vol", "y_half", "y_rest", "z")
+    cut = Mesh(mesh.devices.reshape(mesh.devices.shape[0], 2, NY // 2, NZ), names)
+    chan = names[1:]
     return jax.shard_map(
         shards,
         mesh=cut,

time: 191 us -> 261 us (1.37); the launches traced: 190 us -> 256 us
  starting transfers between devices: 35.3 us -> 64.2 us
  between operations: 0.82 us -> 14.2 us
  blocking collectives: 64.7 us -> 77.4 us
  waiting for transfers between devices: 61.3 us -> 69.5 us
    all_gather x0 -> x1, waiting for transfers between devices: none -> 66.3 us  [shards(): cells = lax.all_gather(fwd_input[0].T, ('y_rest', 'z'), axis=0, tiled=True)]
    all_to_all x6 -> x3, waiting for transfers between devices: 61.3 us -> 0.01 us  [exchange(): return lax.all_to_all(value, axes, 0, 0, tiled=True)]
    all_to_all x4 -> x1, blocking collectives: 64.7 us -> 16 us  [exchange(): return lax.all_to_all(value, axes, 0, 0, tiled=True)]
    all_gather x0 -> x1, blocking collectives: none -> 33.3 us  [shards(): lax.all_gather(jnp.transpose(weight_two, (0, 2, 1)), y_axes, axis=0, tile...]
    psum x0 -> x2, blocking collectives: none -> 28.1 us  [the longest x1 14.7 us: shards(): sums_two = lax.psum(sums_two, 'vol')]
    all_to_all x6 -> x3, starting transfers between devices: 35.3 us -> 50.1 us  [exchange(): return lax.all_to_all(value, axes, 0, 0, tiled=True)]
    ppermute x0 -> x2, starting transfers between devices: none -> 14.1 us  [the longest x1 7.2 us: shards(): other = lax.ppermute(other, 'y_half', [(0, 1), (1, 0)])]
    unnamed x25 -> x14, local copies, waits for them, and re-layouts: 4.21 us -> 6.34 us
  transfers between devices with their start and end apart: 6 -> 6, of which waited for: 6 -> 2; matrix products, arithmetic and copies ran while one was open for 2% -> 1% of each run, Pallas kernels for 9% -> 7%
where the time goes in v3:
time: 261 us; the launch traced here: 256 us
  blocking collectives  77.4 us (30%)
  waiting for transfers between devices  69.5 us (27%)
  starting transfers between devices  64.2 us (25%)
  Pallas kernels  21.5 us (8%)
  between operations  14.2 us (5%)
  local copies, waits for them, and re-layouts  8.43 us (3%)
    all_gather x1, waiting for transfers between devices, shards(): cells = lax.all_gather(fwd_input[0].T, ('y_rest', 'z'), axis=0, tiled=True)  66.3 us
    all_to_all x3, starting transfers between devices, exchange(): return lax.all_to_all(value, axes, 0, 0, tiled=True)  50.1 us
    all_gather x1, blocking collectives, shards(): lax.all_gather(jnp.transpose(weight_two, (0, 2, 1)), y_axes, axis=0, tile...  33.3 us
    all_to_all x1, blocking collectives, exchange(): return lax.all_to_all(value, axes, 0, 0, tiled=True)  16 us
    psum x1, blocking collectives, shards(): sums_two = lax.psum(sums_two, 'vol')  14.7 us
    psum x1, blocking collectives, shards(): sums_one = lax.psum(sums_one, 'vol')  13.4 us
    pallas_call x1, Pallas kernels, shards(): call(forward_kernel, (shaped((OWN, span), F32), shaped((OWN, span), F32))...  8.11 us
    ppermute x1, starting transfers between devices, shards(): other = lax.ppermute(other, 'y_half', [(0, 1), (1, 0)])  7.2 us
  transfers between devices with their start and end apart: 6, of which 2 were waited for; matrix products, arithmetic and copies ran while one was open for 1% of the time, Pallas kernels for 7%

profile of v3, /device:TPU:1, one launch (start us, length us, event | category | flops | bytes accessed | tf_op | source)
XLA Modules:
  0.0 256.1 jit_solution(6365670401247215400)
XLA Ops:
  7.2 0.0 copy-start.6
  7.2 0.0 all-gather.3.cloned.1.call-start
  7.2 0.7 all-gather.3.cloned.1.call-update
  7.9 0.0 copy-start.5
  7.9 0.9 copy-done.5
  8.8 0.7 shard_map.128
  9.5 7.7 %all-to-all-start = ((bf16[8,4,3840]{2,1,0:T(4,128)(2,1)}), bf16[8,4,3840]{2,1,0:T(4,128)(2,1)S(1)}, u32[]{:S(2)}, u32[]{:S(2)}) async-start(bf16[8,4,3840]{2,1,0:T(4,128)(2,1)} %shard_map.128), calls=%async_computation | async-start | bytes 491520 | tf_op jit(solution)/shard_map/all_to_all | solution.py:339
  17.2 0.0 copy-start.1
  17.2 0.9 copy-done.1
  18.1 0.0 copy-start.3
  18.1 0.9 copy-done.3
  19.0 0.5 shard_map.129
  19.4 14.7 %psum.14.refs_2_ = f32[4,128]{1,0:T(4,128)S(1)} all-reduce(f32[4,128]{1,0:T(4,128)S(1)} %shard_map.129), channel_id=1, replica_groups=mesh['vol'=8,'y_half'=2,'y_rest'=4,'z'=8] {'vol'}, use_global_device_ids=true, to_apply=%region_0.0 | all-reduce | flops 512 | bytes 4096 | tf_op jit(solution)/shard_map/psum | solution.py:373
  34.1 0.7 pad_maximum_fusion
  34.8 0.0 all-to-all-done
  34.8 0.1 broadcast_in_dim.12.refs_3_.refs_2_
  34.9 0.0 copy-start.2
  34.9 0.9 copy-done.2
  35.8 0.0 copy-start.4
  35.8 0.9 copy-done.4
  36.7 1.3 shard_map.130
  38.0 14.5 %all-to-all-start.1 = ((bf16[64,4,1536]{2,1,0:T(4,128)(2,1)}), bf16[64,4,1536]{2,1,0:T(4,128)(2,1)S(1)}, u32[]{:S(2)}, u32[]{:S(2)}) async-start(bf16[64,4,1536]{2,1,0:T(4,128)(2,1)} %get-tuple-element.26), calls=%async_computation.1 | async-start | bytes 1572864 | tf_op jit(solution)/shard_map/all_to_all | solution.py:339
  52.5 6.9 %collective-permute-start = (bf16[27,4,256]{2,1,0:T(4,128)(2,1)}, bf16[27,4,256]{2,1,0:T(4,128)(2,1)S(1)}, u32[]{:S(2)}, u32[]{:S(2)}) collective-permute-start(bf16[27,4,256]{2,1,0:T(4,128)(2,1)} %param.10), channel_id=1, source_target_pairs={{0,32},{32,0},{1,33},{33,1},{2,34},{34,2},{3,35},{35,3},{4,36},{36... | collective-permute-start | bytes 165896 | tf_op jit(solution)/shard_map/ppermute | solution.py:387
  59.5 33.3 %all-gather = bf16[216,4,256]{2,1,0:T(4,128)(2,1)S(1)} all-gather(bf16[27,4,256]{2,1,0:T(4,128)(2,1)} %bitcast.35), channel_id=2, replica_groups=mesh['vol'=8,'y_half'=2,'y_rest'=4,'z'=8] {'y_half','y_rest'}, dimensions={0}, use_global_device_ids=true | all-gather | bytes 497664 | tf_op jit(solution)/shard_map/all_gather | solution.py:386
  92.7 0.2 copy.19
  92.9 0.1 reshape.37.weight_ref
  93.1 0.1 reshape.40.acts_ref
  93.1 0.0 collective-permute-done
  93.1 0.0 copy-done.6
  93.1 0.1 maximum_bitcast_fusion.weight_ref
  93.2 0.0 all-to-all-done.1
  93.2 0.2 reshape.39.grads_ref
  93.4 5.0 %shard_map.131 = bf16[8,8,32,128]{3,2,1,0:T(8,128)(2,1)} custom-call(s32[1]{0:T(128)} %bitcast.11.base_ref, bf16[256,1536]{1,0:T(8,128)(2,1)S(1)} %reshape.39.grads_ref, bf16[32,3840]{1,0:T(8,128)(2,1)S(1)} %reshape.40.acts_ref), custom_call_target="tpu_custom_call" | custom-call | flops 1000 | bytes 1000 | tf_op jit(solution)/shard_map/pallas_call | solution.py:393
  98.4 66.3 %all-gather.3.cloned.1.call-done.cells_ref = bf16[6144,256]{1,0:T(8,128)(2,1)} async-done(((bf16[192,256]{1,0:T(8,128)(2,1)}), bf16[6144,256]{1,0:T(8,128)(2,1)}) %all-gather.3.cloned.1.call-update) | async-done | bytes 3145744 | tf_op jit(solution)/shard_map/all_gather | solution.py:368
  164.6 4.2 %shard_map.132 = bf16[8,4,3840]{2,1,0:T(4,128)(2,1)S(1)} custom-call(s32[1]{0:T(128)} %bitcast.11.base_ref, bf16[864,256]{1,0:T(8,128)(2,1)S(1)} %reshape.37.weight_ref, bf16[256,1536]{1,0:T(8,128)(2,1)S(1)} %reshape.39.grads_ref), custom_call_target="tpu_custom_call" | custom-call | flops 1000 | bytes 1000 | tf_op jit(solution)/shard_map/pallas_call | solution.py:401
  168.8 16.0 %all_to_all.20.parts_ref = bf16[8,4,3840]{2,1,0:T(4,128)(2,1)S(1)} all-to-all(bf16[8,4,3840]{2,1,0:T(4,128)(2,1)S(1)} %shard_map.132), channel_id=1, replica_groups=mesh['vol'=8,'y_half'=2,'y_rest'=4,'z'=8] {'y_half','y_rest'}, dimensions={0} | all-to-all | bytes 491520 | tf_op jit(solution)/shard_map/all_to_all | solution.py:339
  184.8 27.9 %all-to-all-start.3 = ((bf16[64,32,128]{2,1,0:T(8,128)(2,1)}), bf16[64,32,128]{2,1,0:T(8,128)(2,1)S(1)}, u32[]{:S(2)}, u32[]{:S(2)}) async-start(bf16[64,32,128]{2,1,0:T(8,128)(2,1)} %bitcast.16), calls=%async_computation.3 | async-start | bytes 1048576 | tf_op jit(solution)/shard_map/all_to_all | solution.py:339
  212.8 0.0 copy-start
  212.8 1.9 copy-done
  214.7 8.1 %shard_map.133 = (f32[4,8192]{1,0:T(4,128)S(1)}, f32[4,8192]{1,0:T(4,128)S(1)}) custom-call(bf16[216,256]{1,0:T(8,128)(2,1)S(1)} %maximum_bitcast_fusion.weight_ref, bf16[6144,256]{1,0:T(8,128)(2,1)S(1)} %copy-done), custom_call_target="tpu_custom_call" | custom-call | flops 1000 | bytes 1000 | tf_op jit(solution)/shard_map/pallas_call | solution.py:411
  222.8 7.2 %collective-permute-start.1 = (f32[4,8192]{1,0:T(4,128)S(1)}, f32[4,8192]{1,0:T(4,128)S(1)}, u32[]{:S(2)}, u32[]{:S(2)}) collective-permute-start(f32[4,8192]{1,0:T(4,128)S(1)} %get-tuple-element.37), channel_id=1, source_target_pairs={{0,32},{32,0},{1,33},{33,1},{2,34},{34,2},{3,35},{35,3},{4,36},{36... | collective-permute-start | bytes 393224 | tf_op jit(solution)/shard_map/ppermute | solution.py:417
  230.0 0.7 slice_reduce_fusion
  230.7 2.5 collective-permute-done.1.other_ref
  233.2 0.2 shard_map.134
  233.4 13.4 %psum.15.refs_1_ = f32[4,128]{1,0:T(4,128)S(1)} all-reduce(f32[4,128]{1,0:T(4,128)S(1)} %get-tuple-element.39), channel_id=1, replica_groups=mesh['vol'=8,'y_half'=2,'y_rest'=4,'z'=8] {'vol'}, use_global_device_ids=true, to_apply=%region_1.0 | all-reduce | flops 512 | bytes 4096 | tf_op jit(solution)/shard_map/psum | solution.py:424
  246.9 0.9 shard_map.135
  247.7 0.7 shard_map.136
  248.4 0.0 all-to-all-done.3
  248.4 0.1 convert_reduce_fusion
  248.5 0.1 copy.17
  248.6 0.6 reshape.42
  (1 shorter events, 0.0 us)
Async XLA Ops:
  7.2 86.0 %copy-start.6 = (bf16[27,4,256]{2,1,0:T(4,128)(2,1)S(1)}, bf16[27,4,256]{2,1,0:T(4,128)(2,1)}, u32[]{:S(2)}) copy-start(bf16[27,4,256]{2,1,0:T(4,128)(2,1)} %param.10) | copy-start | bytes 165892
  7.2 157.5 %all-gather.3.cloned.1.call-start = ((), (), s32[]{:S(2)}) async-start(), calls=%async_computation.4 | async-start | bytes 3244032 | tf_op jit(solution)/shard_map/all_gather | solution.py:368
  7.9 0.9 copy-start.5
  9.5 25.3 %all-to-all-start = ((bf16[8,4,3840]{2,1,0:T(4,128)(2,1)}), bf16[8,4,3840]{2,1,0:T(4,128)(2,1)S(1)}, u32[]{:S(2)}, u32[]{:S(2)}) async-start(bf16[8,4,3840]{2,1,0:T(4,128)(2,1)} %shard_map.128), calls=%async_computation | async-start | bytes 491520 | tf_op jit(solution)/shard_map/all_to_all | solution.py:339
  17.2 0.9 copy-start.1
  18.1 0.9 copy-start.3
  34.9 0.9 copy-start.2
  35.8 0.9 copy-start.4
  38.0 55.2 %all-to-all-start.1 = ((bf16[64,4,1536]{2,1,0:T(4,128)(2,1)}), bf16[64,4,1536]{2,1,0:T(4,128)(2,1)S(1)}, u32[]{:S(2)}, u32[]{:S(2)}) async-start(bf16[64,4,1536]{2,1,0:T(4,128)(2,1)} %get-tuple-element.26), calls=%async_computation.1 | async-start | bytes 1572864 | tf_op jit(solution)/shard_map/all_to_all | solution.py:339
  52.5 40.6 %collective-permute-start = (bf16[27,4,256]{2,1,0:T(4,128)(2,1)}, bf16[27,4,256]{2,1,0:T(4,128)(2,1)S(1)}, u32[]{:S(2)}, u32[]{:S(2)}) collective-permute-start(bf16[27,4,256]{2,1,0:T(4,128)(2,1)} %param.10), channel_id=1, source_target_pairs={{0,32},{32,0},{1,33},{33,1},{2,34},{34,2},{3,35},{35,3},{4,36},{36... | collective-permute-start | bytes 165896 | tf_op jit(solution)/shard_map/ppermute | solution.py:387
  184.8 63.6 %all-to-all-start.3 = ((bf16[64,32,128]{2,1,0:T(8,128)(2,1)}), bf16[64,32,128]{2,1,0:T(8,128)(2,1)S(1)}, u32[]{:S(2)}, u32[]{:S(2)}) async-start(bf16[64,32,128]{2,1,0:T(8,128)(2,1)} %bitcast.16), calls=%async_computation.3 | async-start | bytes 1048576 | tf_op jit(solution)/shard_map/all_to_all | solution.py:339
  212.8 1.9 copy-start
  222.8 10.4 %collective-permute-start.1 = (f32[4,8192]{1,0:T(4,128)S(1)}, f32[4,8192]{1,0:T(4,128)S(1)}, u32[]{:S(2)}, u32[]{:S(2)}) collective-permute-start(f32[4,8192]{1,0:T(4,128)S(1)} %get-tuple-element.37), channel_id=1, source_target_pairs={{0,32},{32,0},{1,33},{33,1},{2,34},{34,2},{3,35},{35,3},{4,36},{36... | collective-permute-start | bytes 393224 | tf_op jit(solution)/shard_map/ppermute | solution.py:417
Sparse Core Ops, SparseCore 0:
  10.1 154.5 all-gather.2

commit v4 on v1

--- a/solution.py
+++ b/solution.py
@@ -178,9 +178,7 @@
 
 
 def from_lanes(sums_ref, count):
-    total = sums_ref[0]
-    for vol in range(1, sums_ref.shape[0]):
-        total = total + sums_ref[vol]
+    total = sums_ref[...]
     lane = iota((OWN, 128), 1)
     return [
         jnp.sum(jnp.where(lane == index, total, 0.0), axis=1, keepdims=True)
@@ -188,29 +186,16 @@
     ]
 
 
-def to_volumes(sums_ref, values):
-    row = in_lanes(values)
-    for vol in range(sums_ref.shape[0]):
-        sums_ref[vol] = row
-
-
-def sums_kernel(saved_hbm, upstream_hbm, sums_ref, saved_ref, upstream_ref, arrived):
-    first = pltpu.make_async_copy(saved_hbm, saved_ref, arrived.at[0])
-    second = pltpu.make_async_copy(upstream_hbm, upstream_ref, arrived.at[1])
-    first.start()
-    second.start()
-    first.wait()
-    second.wait()
+def sums_kernel(saved_ref, upstream_ref, sums_ref):
     saved = saved_ref[...].astype(F32)
     upstream = upstream_ref[...].astype(F32)
-    to_volumes(
-        sums_ref,
+    sums_ref[...] = in_lanes(
         [
             lane_sum(saved),
             lane_sum(saved * saved),
             lane_sum(upstream),
             lane_sum(upstream * saved),
-        ],
+        ]
     )
 
 
@@ -265,7 +250,7 @@
         out_ref[:, block * BLOCK : (block + 1) * BLOCK] = cells
         total = total + lane_sum(cells)
         squares = squares + lane_sum(cells * cells)
-    to_volumes(sums_ref, [total, squares])
+    sums_ref[...] = in_lanes([total, squares])
 
 
 def join_kernel(parts_ref, out_ref):
@@ -302,8 +287,9 @@
     return lax.all_to_all(value, axes, 0, 0, tiled=True)
 
 
-def to_all(value, axis):
-    return exchange(jnp.broadcast_to(value[None], (lax.axis_size(axis),) + value.shape), axis)
+def gathered(filters):
+    filters = lax.all_gather(filters, "y", axis=0, tiled=False)
+    return jnp.transpose(filters, (1, 0, 2, 3)).reshape(ROWS, CH)
 
 
 def shards(
@@ -317,79 +303,65 @@
     weight_two,
     gain_two,
 ):
-    volumes = lax.axis_size("vol")
-    counted = volumes * CELLS
+    counted = lax.axis_size("vol") * CELLS
     base = (lax.axis_index("y") * BLOCK).astype(jnp.int32).reshape(1)
     params = jnp.broadcast_to(
         jnp.stack([gain_one, bias_one, gain_two])[:, :, None], (3, OWN, 128)
     )
     saved, upstream = saved_conv[0], cotangent[0]
 
-    sums_two = call(
-        sums_kernel,
-        shaped((volumes, OWN, 128), F32),
-        [pl.BlockSpec(memory_space=pl.ANY)] * 2,
-        [
-            pltpu.VMEM((OWN, CELLS), BF16),
-            pltpu.VMEM((OWN, CELLS), BF16),
-            pltpu.SemaphoreType.DMA((2,)),
-        ],
-    )(saved, upstream)
-    weight_one, sums_two = lax.optimization_barrier((weight_one, sums_two))
-    sums_two = exchange(sums_two, "vol")
-
-    cells = to_all(fwd_input[0].T, "z").reshape(BLOCK, CH)
-    rows = jnp.concatenate(
-        [jnp.transpose(weight_one, (1, 0, 2)), jnp.transpose(weight_two, (2, 0, 1))]
-    )
-    row = lax.dynamic_index_in_dim(rows, lax.axis_index("vol"), 0, keepdims=False)
-    rows = to_all(to_all(row, "y"), "vol")
-    weights = [
-        jnp.transpose(rows[first : first + OWN], (2, 1, 0, 3)).reshape(ROWS, CH)
-        for first in (0, OWN)
-    ]
+    sums_two = call(sums_kernel, shaped((OWN, 128), F32), [VMEM] * 2)(saved, upstream)
     acts = call(pack_kernel, shaped((NY, OWN, SPAN), BF16), [VMEM])(saved_input[0])
-    acts = exchange(acts, "y").reshape(GROUP, SPAN)
-
+    acts = exchange(acts, "y")
+    sums_two = lax.psum(sums_two, "vol")
+    acts, sums_two = lax.optimization_barrier((acts, sums_two))
+    acts = acts.reshape(GROUP, SPAN)
     packed, means = call(
         lambda *refs: grad_kernel(counted, *refs),
         (shaped((NY * NZ, OWN, BLOCK), BF16), shaped((OWN, 128), F32)),
         [VMEM] * 4,
     )(saved, upstream, sums_two, params)
-    grads = exchange(packed, ("y", "z")).reshape(CH, BLOCK)
-
-    cells, means = lax.optimization_barrier((cells, means))
-    conv_parts = call(
-        forward_kernel,
-        shaped((NY, OWN, SPAN), F32),
-        [SMEM, VMEM, VMEM],
-        [pltpu.VMEM((ROWS, BLOCK), F32)],
-    )(base, weights[0], cells)
-    grads, conv_parts = lax.optimization_barrier((grads, conv_parts))
-    conv_parts = exchange(conv_parts, "y")
+
+    cells, packed = lax.optimization_barrier((fwd_input[0].T, packed))
+    grads = exchange(packed, ("y", "z"))
+    cells = lax.all_gather(cells, "z", axis=0, tiled=True)
+    grads, cells = lax.optimization_barrier((grads, cells))
+    grads = grads.reshape(CH, BLOCK)
     filter_parts = call(
         filter_kernel,
         shaped((8, NY, GROUP, 128), BF16),
         [SMEM, VMEM, VMEM],
         [pltpu.VMEM((1024, BLOCK), BF16), pltpu.VMEM((CH, 1024), BF16)],
     )(base, grads, acts)
-    weight, filter_parts = lax.optimization_barrier((weights[1], filter_parts))
+
+    first, filter_parts = lax.optimization_barrier((weight_one, filter_parts))
     filter_parts = exchange(filter_parts.reshape(8 * NY, GROUP, 128), ("vol", "y"))
+    first = gathered(first)
+    conv_parts = call(
+        forward_kernel,
+        shaped((NY, OWN, SPAN), F32),
+        [SMEM, VMEM, VMEM],
+        [pltpu.VMEM((ROWS, BLOCK), F32)],
+    )(base, first, cells)
+
+    second, conv_parts, filter_parts = lax.optimization_barrier(
+        (weight_two, conv_parts, filter_parts)
+    )
+    conv_parts = exchange(conv_parts, "y")
+    second = gathered(jnp.transpose(second, (0, 2, 1)))
     input_parts = call(
         backward_kernel,
         shaped((NY, OWN, SPAN), BF16),
         [SMEM, VMEM, VMEM],
         [pltpu.VMEM((ROWS, BLOCK), F32)],
-    )(base, weight, grads)
+    )(base, second, grads)
+
     conv_parts, input_parts = lax.optimization_barrier((conv_parts, input_parts))
     input_parts = exchange(input_parts, "y")
-
     conv_out, sums_one = call(
-        join_stats_kernel,
-        (shaped((OWN, CELLS), F32), shaped((volumes, OWN, 128), F32)),
-        [VMEM],
+        join_stats_kernel, (shaped((OWN, CELLS), F32), shaped((OWN, 128), F32)), [VMEM]
     )(conv_parts)
-    sums_one = exchange(sums_one, "vol")
+    sums_one = lax.psum(sums_one, "vol")
     activation = call(
         lambda *refs: relu_kernel(counted, *refs), shaped((OWN, CELLS), BF16), [VMEM] * 3
     )(conv_out, sums_one, params)

time: 191 us -> 199 us (1.042)
  blocking collectives: 64.7 us -> 126 us
  waiting for transfers between devices: 61.3 us -> 0.01 us
  starting transfers between devices: 35.3 us -> 48 us
  local copies, waits for them, and re-layouts: 8.55 us -> 4.82 us
    all_gather x0 -> x3, blocking collectives: none -> 88.7 us  [the longest x2 54 us: gathered(): filters = lax.all_gather(filters, 'y', axis=0, tiled=False)]
    all_to_all x4 -> x0, blocking collectives: 64.7 us -> none  [exchange(): return lax.all_to_all(value, axes, 0, 0, tiled=True)]
    all_to_all x6 -> x5, waiting for transfers between devices: 61.3 us -> 0.01 us  [exchange(): return lax.all_to_all(value, axes, 0, 0, tiled=True)]
    psum x0 -> x2, blocking collectives: none -> 37.3 us  [the longest x1 22.9 us: shards(): sums_one = lax.psum(sums_one, 'vol')]
    all_to_all x6 -> x5, starting transfers between devices: 35.3 us -> 48 us  [exchange(): return lax.all_to_all(value, axes, 0, 0, tiled=True)]
    unnamed x25 -> x18, local copies, waits for them, and re-layouts: 4.21 us -> 2.4 us
  transfers between devices with their start and end apart: 6 -> 5, of which waited for: 6 -> 0; matrix products, arithmetic and copies ran while one was open for 2% -> 1% of each run, Pallas kernels for 9% -> 6%
where the time goes in v4:
time: 199 us
  blocking collectives  126 us (63%)
  starting transfers between devices  48 us (24%)
  Pallas kernels  18.8 us (9%)
  local copies, waits for them, and re-layouts  4.82 us (2%)
    all_gather x2, blocking collectives, gathered(): filters = lax.all_gather(filters, 'y', axis=0, tiled=False)  54 us
    all_to_all x5, starting transfers between devices, exchange(): return lax.all_to_all(value, axes, 0, 0, tiled=True)  48 us
    all_gather x1, blocking collectives, shards(): cells = lax.all_gather(cells, 'z', axis=0, tiled=True)  34.7 us
    psum x1, blocking collectives, shards(): sums_one = lax.psum(sums_one, 'vol')  22.9 us
    psum x1, blocking collectives, shards(): sums_two = lax.psum(sums_two, 'vol')  14.4 us
    pallas_call x1, Pallas kernels, shards(): call(forward_kernel, shaped((NY, OWN, SPAN), F32), [SMEM, VMEM, VMEM], [p...  5.22 us
    pallas_call x1, Pallas kernels, shards(): call(filter_kernel, shaped((8, NY, GROUP, 128), BF16), [SMEM, VMEM, VMEM]...  4.95 us
    pallas_call x1, Pallas kernels, shards(): call(backward_kernel, shaped((NY, OWN, SPAN), BF16), [SMEM, VMEM, VMEM],...  4.86 us
  transfers between devices with their start and end apart: 5, of which 0 were waited for; matrix products, arithmetic and copies ran while one was open for 1% of the time, Pallas kernels for 6%

profile of v4, /device:TPU:1, one launch (start us, length us, event | category | flops | bytes accessed | tf_op | source)
XLA Modules:
  0.0 198.5 jit_solution(1228374071277308397)
XLA Ops:
  0.6 0.0 copy-start.2
  0.6 0.9 copy-done.2
  1.5 0.7 shard_map.128
  2.2 0.0 copy-start
  2.2 0.0 copy-start.1
  2.2 7.8 %all-to-all-start = ((bf16[8,4,3840]{2,1,0:T(4,128)(2,1)}), bf16[8,4,3840]{2,1,0:T(4,128)(2,1)S(1)}, u32[]{:S(2)}, u32[]{:S(2)}) async-start(bf16[8,4,3840]{2,1,0:T(4,128)(2,1)} %shard_map.128), calls=%async_computation | async-start | bytes 491520 | tf_op jit(solution)/shard_map/all_to_all | solution.py:287
  10.0 0.0 copy-done
  10.0 0.0 copy-done.1
  10.0 0.2 shard_map.129
  10.3 14.4 %psum.14.refs_2_ = f32[4,128]{1,0:T(4,128)S(1)} all-reduce(f32[4,128]{1,0:T(4,128)S(1)} %shard_map.129), channel_id=1, replica_groups=mesh['vol'=8,'y'=8,'z'=8] {'vol'}, use_global_device_ids=true, to_apply=%region_0.0 | all-reduce | flops 512 | bytes 4096 | tf_op jit(solution)/shard_map/psum | solution.py:316
  24.7 0.0 copy-start.6
  24.7 0.0 copy-start.7
  24.7 0.0 copy-start.8
  24.7 0.6 copy-done.6
  25.3 0.0 copy-done.7
  25.3 0.0 copy-done.8
  25.4 0.0 all-to-all-done
  25.4 0.1 broadcast_in_dim.12.refs_3_.refs_2_
  25.4 1.1 shard_map.130
  26.6 14.7 %all-to-all-start.1 = ((bf16[64,4,1536]{2,1,0:T(4,128)(2,1)}), bf16[64,4,1536]{2,1,0:T(4,128)(2,1)S(1)}, u32[]{:S(2)}, u32[]{:S(2)}) async-start(bf16[64,4,1536]{2,1,0:T(4,128)(2,1)} %get-tuple-element.24), calls=%async_computation.1 | async-start | bytes 1572864 | tf_op jit(solution)/shard_map/all_to_all | solution.py:287
  41.3 0.0 copy-start.3
  41.3 0.1 reshape.34.acts_ref
  41.4 0.8 copy-done.3
  42.2 34.7 %all_gather.15.cells_ref = bf16[1536,256]{1,0:T(8,128)(2,1)S(1)} all-gather(bf16[192,256]{1,0:T(8,128)(2,1)S(1)} %bitcast.34), channel_id=1, replica_groups=mesh['vol'=8,'y'=8,'z'=8] {'z'}, dimensions={0}, use_global_device_ids=true | all-gather | bytes 884736 | tf_op jit(solution)/shard_map/all_gather | solution.py:327
  76.9 0.0 all-to-all-done.1
  76.9 0.2 reshape.33.grads_ref
  77.1 5.0 %shard_map.131 = bf16[8,8,32,128]{3,2,1,0:T(8,128)(2,1)} custom-call(s32[1]{0:T(128)} %bitcast.base_ref, bf16[256,1536]{1,0:T(8,128)(2,1)S(1)} %reshape.33.grads_ref, bf16[32,3840]{1,0:T(8,128)(2,1)S(1)} %reshape.34.acts_ref), custom_call_target="tpu_custom_call" | custom-call | flops 1000 | bytes 1000 | tf_op jit(solution)/shard_map/pallas_call | solution.py:330
  82.0 0.0 copy-start.4
  82.0 14.9 %all-to-all-start.2 = ((bf16[64,32,128]{2,1,0:T(8,128)(2,1)}), bf16[64,32,128]{2,1,0:T(8,128)(2,1)S(1)}, u32[]{:S(2)}, u32[]{:S(2)}) async-start(bf16[64,32,128]{2,1,0:T(8,128)(2,1)} %bitcast.11), calls=%async_computation.2 | async-start | bytes 1048576 | tf_op jit(solution)/shard_map/all_to_all | solution.py:287
  97.0 0.0 copy-done.4
  97.0 29.0 %all-gather = bf16[216,4,256]{2,1,0:T(4,128)(2,1)S(1)} all-gather(bf16[27,4,256]{2,1,0:T(4,128)(2,1)S(1)} %copy-done.4), channel_id=2, replica_groups=mesh['vol'=8,'y'=8,'z'=8] {'y'}, dimensions={0}, use_global_device_ids=true | all-gather | bytes 497664 | tf_op jit(solution)/shard_map/all_gather | solution.py:291
  126.0 0.2 copy.24
  126.2 0.1 reshape.35.weight_ref
  126.4 5.2 %shard_map.132 = f32[8,4,3840]{2,1,0:T(4,128)} custom-call(s32[1]{0:T(128)} %bitcast.base_ref, bf16[864,256]{1,0:T(8,128)(2,1)S(1)} %reshape.35.weight_ref, bf16[1536,256]{1,0:T(8,128)(2,1)S(1)} %all_gather.15.cells_ref), custom_call_target="tpu_custom_call" | custom-call | flops 1000 | bytes 1000 | tf_op jit(solution)/shard_map/pallas_call | solution.py:340
  131.6 0.0 copy-start.5
  131.6 0.0 all-to-all-done.2
  131.6 5.4 %all-to-all-start.3 = ((f32[8,4,3840]{2,1,0:T(4,128)}), f32[8,4,3840]{2,1,0:T(4,128)S(1)}, u32[]{:S(2)}, u32[]{:S(2)}) async-start(f32[8,4,3840]{2,1,0:T(4,128)} %shard_map.132), calls=%async_computation.3 | async-start | bytes 983040 | tf_op jit(solution)/shard_map/all_to_all | solution.py:287
  137.0 0.0 copy-done.5
  137.0 25.0 %all-gather.1 = bf16[216,4,256]{2,1,0:T(4,128)(2,1)S(1)} all-gather(bf16[27,4,256]{2,1,0:T(4,128)(2,1)S(1)} %bitcast.38), channel_id=3, replica_groups=mesh['vol'=8,'y'=8,'z'=8] {'y'}, dimensions={0}, use_global_device_ids=true | all-gather | bytes 497664 | tf_op jit(solution)/shard_map/all_gather | solution.py:291
  162.0 0.2 copy.23
  162.2 0.1 reshape.37.weight_ref
  162.3 4.9 %shard_map.133 = bf16[8,4,3840]{2,1,0:T(4,128)(2,1)} custom-call(s32[1]{0:T(128)} %bitcast.base_ref, bf16[864,256]{1,0:T(8,128)(2,1)S(1)} %reshape.37.weight_ref, bf16[256,1536]{1,0:T(8,128)(2,1)S(1)} %reshape.33.grads_ref), custom_call_target="tpu_custom_call" | custom-call | flops 1000 | bytes 1000 | tf_op jit(solution)/shard_map/pallas_call | solution.py:352
  167.2 0.0 all-to-all-done.3.parts_ref
  167.2 5.1 %all-to-all-start.4 = ((bf16[8,4,3840]{2,1,0:T(4,128)(2,1)}), bf16[8,4,3840]{2,1,0:T(4,128)(2,1)S(1)}, u32[]{:S(2)}, u32[]{:S(2)}) async-start(bf16[8,4,3840]{2,1,0:T(4,128)(2,1)} %shard_map.133), calls=%async_computation.4 | async-start | bytes 491520 | tf_op jit(solution)/shard_map/all_to_all | solution.py:287
  172.3 0.7 slice_reduce_fusion
  173.0 0.1 convert_reduce_fusion
  173.1 0.1 copy.20
  173.3 0.6 reshape.38
  173.9 0.2 shard_map.134
  174.1 22.9 %psum.15.refs_1_ = f32[4,128]{1,0:T(4,128)S(1)} all-reduce(f32[4,128]{1,0:T(4,128)S(1)} %get-tuple-element.35), channel_id=1, replica_groups=mesh['vol'=8,'y'=8,'z'=8] {'vol'}, use_global_device_ids=true, to_apply=%region_1.0 | all-reduce | flops 512 | bytes 4096 | tf_op jit(solution)/shard_map/psum | solution.py:364
  196.9 0.9 shard_map.135
  197.8 0.0 all-to-all-done.4.parts_ref
  197.8 0.7 shard_map.136
  (2 shorter events, 0.0 us)
Async XLA Ops:
  0.6 0.9 copy-start.2
  2.2 7.8 %copy-start = (bf16[1,4,12288]{2,1,0:T(4,128)(2,1)S(1)}, bf16[1,4,12288]{2,1,0:T(4,128)(2,1)}, u32[]{:S(2)}) copy-start(bf16[1,4,12288]{2,1,0:T(4,128)(2,1)} %param.13) | copy-start | bytes 294916
  2.2 7.8 %copy-start.1 = (bf16[1,4,12288]{2,1,0:T(4,128)(2,1)S(1)}, bf16[1,4,12288]{2,1,0:T(4,128)(2,1)}, u32[]{:S(2)}) copy-start(bf16[1,4,12288]{2,1,0:T(4,128)(2,1)} %param.14) | copy-start | bytes 294916
  2.2 23.1 %all-to-all-start = ((bf16[8,4,3840]{2,1,0:T(4,128)(2,1)}), bf16[8,4,3840]{2,1,0:T(4,128)(2,1)S(1)}, u32[]{:S(2)}, u32[]{:S(2)}) async-start(bf16[8,4,3840]{2,1,0:T(4,128)(2,1)} %shard_map.128), calls=%async_computation | async-start | bytes 491520 | tf_op jit(solution)/shard_map/all_to_all | solution.py:287
  24.7 0.7 copy-start.6
  24.7 0.7 copy-start.7
  24.7 0.7 copy-start.8
  26.6 50.3 %all-to-all-start.1 = ((bf16[64,4,1536]{2,1,0:T(4,128)(2,1)}), bf16[64,4,1536]{2,1,0:T(4,128)(2,1)S(1)}, u32[]{:S(2)}, u32[]{:S(2)}) async-start(bf16[64,4,1536]{2,1,0:T(4,128)(2,1)} %get-tuple-element.24), calls=%async_computation.1 | async-start | bytes 1572864 | tf_op jit(solution)/shard_map/all_to_all | solution.py:287
  41.3 0.9 copy-start.3
  82.0 14.9 %copy-start.4 = (bf16[27,4,256]{2,1,0:T(4,128)(2,1)S(1)}, bf16[27,4,256]{2,1,0:T(4,128)(2,1)}, u32[]{:S(2)}) copy-start(bf16[27,4,256]{2,1,0:T(4,128)(2,1)} %param.10) | copy-start | bytes 165892
  82.0 49.5 %all-to-all-start.2 = ((bf16[64,32,128]{2,1,0:T(8,128)(2,1)}), bf16[64,32,128]{2,1,0:T(8,128)(2,1)S(1)}, u32[]{:S(2)}, u32[]{:S(2)}) async-start(bf16[64,32,128]{2,1,0:T(8,128)(2,1)} %bitcast.11), calls=%async_computation.2 | async-start | bytes 1048576 | tf_op jit(solution)/shard_map/all_to_all | solution.py:287
  131.6 5.4 %copy-start.5 = (bf16[27,256,4]{1,2,0:T(4,128)(2,1)S(1)}, bf16[27,256,4]{1,2,0:T(4,128)(2,1)}, u32[]{:S(2)}) copy-start(bf16[27,256,4]{1,2,0:T(4,128)(2,1)} %param.16) | copy-start | bytes 165892
  131.6 35.6 %all-to-all-start.3 = ((f32[8,4,3840]{2,1,0:T(4,128)}), f32[8,4,3840]{2,1,0:T(4,128)S(1)}, u32[]{:S(2)}, u32[]{:S(2)}) async-start(f32[8,4,3840]{2,1,0:T(4,128)} %shard_map.132), calls=%async_computation.3 | async-start | bytes 983040 | tf_op jit(solution)/shard_map/all_to_all | solution.py:287
  167.2 30.6 %all-to-all-start.4 = ((bf16[8,4,3840]{2,1,0:T(4,128)(2,1)}), bf16[8,4,3840]{2,1,0:T(4,128)(2,1)S(1)}, u32[]{:S(2)}, u32[]{:S(2)}) async-start(bf16[8,4,3840]{2,1,0:T(4,128)(2,1)} %shard_map.133), calls=%async_computation.4 | async-start | bytes 491520 | tf_op jit(solution)/shard_map/all_to_all | solution.py:287

commit v5 on v4

--- a/solution.py
+++ b/solution.py
@@ -14,6 +14,7 @@
 REACH = PLANE + EDGE
 SPAN = BLOCK + 2 * REACH
 CELLS = 12288
+HALF = 6
 NY = 8
 NZ = 8
 OWN = 4
@@ -85,14 +86,56 @@
     lax.fori_loop(0, GROUP // 8, rows, 0)
 
 
-def forward_kernel(base_ref, weight_ref, cells_ref, out_ref, terms):
+def forward_kernel(low_ref, high_ref, lower_ref, upper_ref, out_ref, sums_ref, terms, held):
+    at = pl.program_id(0)
+
+    @pl.when(at == 0)
+    def _():
+        held[...] = jnp.zeros_like(held)
+
     def columns(step, carry):
         part = pl.ds(pl.multiple_of(step * 256, 256), 256)
-        terms[:, part] = nt_dot(weight_ref[...], cells_ref[part, :])
-        return carry
-
-    lax.fori_loop(0, BLOCK // 256, columns, 0)
-    spread(base_ref[0], terms, out_ref, 1)
+        terms[:, part] = nt_dot(low_ref[...], lower_ref[part, :]) + nt_dot(
+            high_ref[...], upper_ref[part, :]
+        )
+        return carry
+
+    lax.fori_loop(0, PLANE // 256, columns, 0)
+    lane = iota((8, PLANE), 1)
+    along_x, along_y = lane & 31, lax.shift_right_logical(lane, 5)
+    ends = {1: along_x >= 1, -1: along_x <= 30}
+    sides = {1: along_y >= 1, -1: along_y <= 30}
+    for a in (-1, 0, 1):
+        total = None
+        for b in (-1, 0, 1):
+            line = None
+            for c in (-1, 0, 1):
+                index = 9 * (a + 1) + 3 * (b + 1) + (c + 1)
+                term = terms[8 * index : 8 * index + 8, :]
+                if c != 0:
+                    term = shift(jnp.where(ends[c], term, 0.0), c)
+                line = term if line is None else line + term
+            if b != 0:
+                line = shift(jnp.where(sides[b], line, 0.0), 32 * b)
+            total = line if total is None else total + line
+        goal = pl.ds(pl.multiple_of((at + 1 - a) * PLANE, PLANE), PLANE)
+        held[:, goal] += total
+
+    @pl.when(at == HALF - 1)
+    def _():
+        total = jnp.zeros((OWN, 128), F32)
+        squares = jnp.zeros((OWN, 128), F32)
+        for z in range(2 * HALF):
+            side, own = divmod(z, HALF)
+            cells = held[OWN * side : OWN * side + OWN, (own + 1) * PLANE : (own + 2) * PLANE]
+            if z == HALF - 1:
+                cells = cells + held[OWN:, :PLANE]
+            if z == HALF:
+                cells = cells + held[:OWN, (HALF + 1) * PLANE :]
+            out_ref[:, z * PLANE : (z + 1) * PLANE] = cells
+            total = total + lane_sum(cells)
+            squares = squares + lane_sum(cells * cells)
+        sums_ref[...] = in_lanes([total, squares])
 
 
 def backward_kernel(base_ref, weight_ref, grads_ref, out_ref, terms):
@@ -242,17 +285,6 @@
     return jnp.concatenate(pieces, axis=1)
 
 
-def join_stats_kernel(parts_ref, out_ref, sums_ref):
-    total = jnp.zeros((OWN, 128), F32)
-    squares = jnp.zeros((OWN, 128), F32)
-    for block in range(NY):
-        cells = joined(parts_ref, block)
-        out_ref[:, block * BLOCK : (block + 1) * BLOCK] = cells
-        total = total + lane_sum(cells)
-        squares = squares + lane_sum(cells * cells)
-    sums_ref[...] = in_lanes([total, squares])
-
-
 def join_kernel(parts_ref, out_ref):
     for block in range(NY):
         out_ref[:, block * BLOCK : (block + 1) * BLOCK] = joined(parts_ref, block).astype(BF16)
@@ -310,6 +342,10 @@
     )
     saved, upstream = saved_conv[0], cotangent[0]
 
+    cells = lax.all_gather(fwd_input[0].T, ("y", "z"), axis=0, tiled=True)
+    low = jnp.pad(weight_one, ((0, 0), (0, OWN), (0, 0))).reshape(27 * 2 * OWN, CH)
+    high = jnp.pad(weight_one, ((0, 0), (OWN, 0), (0, 0))).reshape(27 * 2 * OWN, CH)
+
     sums_two = call(sums_kernel, shaped((OWN, 128), F32), [VMEM] * 2)(saved, upstream)
     acts = call(pack_kernel, shaped((NY, OWN, SPAN), BF16), [VMEM])(saved_input[0])
     acts = exchange(acts, "y")
@@ -322,10 +358,10 @@
         [VMEM] * 4,
     )(saved, upstream, sums_two, params)
 
-    cells, packed = lax.optimization_barrier((fwd_input[0].T, packed))
+    second, packed = lax.optimization_barrier((weight_two, packed))
     grads = exchange(packed, ("y", "z"))
-    cells = lax.all_gather(cells, "z", axis=0, tiled=True)
-    grads, cells = lax.optimization_barrier((grads, cells))
+    second = gathered(jnp.transpose(second, (0, 2, 1)))
+    grads, second = lax.optimization_barrier((grads, second))
     grads = grads.reshape(CH, BLOCK)
     filter_parts = call(
         filter_kernel,
@@ -333,22 +369,8 @@
         [SMEM, VMEM, VMEM],
         [pltpu.VMEM((1024, BLOCK), BF16), pltpu.VMEM((CH, 1024), BF16)],
     )(base, grads, acts)
-
-    first, filter_parts = lax.optimization_barrier((weight_one, filter_parts))
+    second, filter_parts = lax.optimization_barrier((second, filter_parts))
     filter_parts = exchange(filter_parts.reshape(8 * NY, GROUP, 128), ("vol", "y"))
-    first = gathered(first)
-    conv_parts = call(
-        forward_kernel,
-        shaped((NY, OWN, SPAN), F32),
-        [SMEM, VMEM, VMEM],
-        [pltpu.VMEM((ROWS, BLOCK), F32)],
-    )(base, first, cells)
-
-    second, conv_parts, filter_parts = lax.optimization_barrier(
-        (weight_two, conv_parts, filter_parts)
-    )
-    conv_parts = exchange(conv_parts, "y")
-    second = gathered(jnp.transpose(second, (0, 2, 1)))
     input_parts = call(
         backward_kernel,
         shaped((NY, OWN, SPAN), BF16),
@@ -356,11 +378,29 @@
         [pltpu.VMEM((ROWS, BLOCK), F32)],
     )(base, second, grads)
 
-    conv_parts, input_parts = lax.optimization_barrier((conv_parts, input_parts))
+    cells, input_parts = lax.optimization_barrier((cells, input_parts))
     input_parts = exchange(input_parts, "y")
-    conv_out, sums_one = call(
-        join_stats_kernel, (shaped((OWN, CELLS), F32), shaped((OWN, 128), F32)), [VMEM]
-    )(conv_parts)
+    conv_out, sums_one = pl.pallas_call(
+        forward_kernel,
+        out_shape=(shaped((OWN, CELLS), F32), shaped((OWN, 128), F32)),
+        grid=(HALF,),
+        in_specs=[
+            pl.BlockSpec((27 * 2 * OWN, CH), lambda at: (0, 0)),
+            pl.BlockSpec((27 * 2 * OWN, CH), lambda at: (0, 0)),
+            pl.BlockSpec((PLANE, CH), lambda at: (at, 0)),
+            pl.BlockSpec((PLANE, CH), lambda at: (at + HALF, 0)),
+        ],
+        out_specs=(
+            pl.BlockSpec((OWN, CELLS), lambda at: (0, 0)),
+            pl.BlockSpec((OWN, 128), lambda at: (0, 0)),
+        ),
+        scratch_shapes=[
+            pltpu.VMEM((27 * 2 * OWN, PLANE), F32),
+            pltpu.VMEM((2 * OWN, (HALF + 2) * PLANE), F32),
+        ],
+        compiler_params=PARAMS,
+        cost_estimate=pl.CostEstimate(flops=1000, bytes_accessed=1000, transcendentals=0),
+    )(low, high, cells, cells)
     sums_one = lax.psum(sums_one, "vol")
     activation = call(
         lambda *refs: relu_kernel(counted, *refs), shaped((OWN, CELLS), BF16), [VMEM] * 3

time: 199 us -> 172 us (0.86)
  blocking collectives: 126 us -> 61.1 us
  waiting for transfers between devices: 0.01 us -> 21 us
  between operations: 0.77 us -> 14.1 us
  starting transfers between devices: 48 us -> 41.7 us
  local copies, waits for them, and re-layouts: 4.82 us -> 9.38 us
  Pallas kernels: 18.8 us -> 22.6 us
    all_gather x1 -> x0, blocking collectives: 34.7 us -> none  [shards(): cells = lax.all_gather(cells, 'z', axis=0, tiled=True)]
    all_gather x2 -> x1, blocking collectives: 54 us -> 33.1 us  [gathered(): filters = lax.all_gather(filters, 'y', axis=0, tiled=False)]
    all_gather x0 -> x1, waiting for transfers between devices: none -> 20.3 us  [shards(): cells = lax.all_gather(fwd_input[0].T, ('y', 'z'), axis=0, tiled=True)]
    psum x1, blocking collectives: 22.9 us -> 13.3 us  [shards(): sums_one = lax.psum(sums_one, 'vol')]
    all_to_all x5 -> x4, starting transfers between devices: 48 us -> 41.6 us  [exchange(): return lax.all_to_all(value, axes, 0, 0, tiled=True)]
    unnamed x18 -> x14, local copies, waits for them, and re-layouts: 2.4 us -> 7.24 us
    pallas_call x2 -> x1, Pallas kernels: 5.37 us -> 9.14 us  [shards(): pl.pallas_call(forward_kernel, out_shape=(shaped((OWN, CELLS), F32), shap...]
  transfers between devices with their start and end apart: 5 -> 5, of which waited for: 0 -> 1; matrix products, arithmetic and copies ran while one was open for 1% -> 2% of each run, Pallas kernels for 6% -> 13%
where the time goes in v5:
time: 172 us; the launch traced here: 171 us
  blocking collectives  61.1 us (36%)
  starting transfers between devices  41.7 us (24%)
  Pallas kernels  22.6 us (13%)
  waiting for transfers between devices  21 us (12%)
  between operations  14.1 us (8%)
  local copies, waits for them, and re-layouts  9.38 us (5%)
    all_to_all x4, starting transfers between devices, exchange(): return lax.all_to_all(value, axes, 0, 0, tiled=True)  41.6 us
    all_gather x1, blocking collectives, gathered(): filters = lax.all_gather(filters, 'y', axis=0, tiled=False)  33.1 us
    all_gather x1, waiting for transfers between devices, shards(): cells = lax.all_gather(fwd_input[0].T, ('y', 'z'), axis=0, tiled=True)  20.3 us
    psum x1, blocking collectives, shards(): sums_two = lax.psum(sums_two, 'vol')  14.7 us
    psum x1, blocking collectives, shards(): sums_one = lax.psum(sums_one, 'vol')  13.3 us
    pallas_call x1, Pallas kernels, shards(): pl.pallas_call(forward_kernel, out_shape=(shaped((OWN, CELLS), F32), shap...  9.14 us
    unnamed x14, local copies, waits for them, and re-layouts  7.24 us
    pallas_call x1, Pallas kernels, shards(): call(filter_kernel, shaped((8, NY, GROUP, 128), BF16), [SMEM, VMEM, VMEM]...  4.98 us
  transfers between devices with their start and end apart: 5, of which 1 were waited for; matrix products, arithmetic and copies ran while one was open for 2% of the time, Pallas kernels for 13%

profile of v5, /device:TPU:1, one launch (start us, length us, event | category | flops | bytes accessed | tf_op | source)
XLA Modules:
  0.0 170.7 jit_solution(11901030542944396830)
XLA Ops:
  7.2 0.0 copy-start.6
  7.2 0.0 all-gather.3.cloned.1.call-start
  7.2 0.7 all-gather.3.cloned.1.call-update
  7.9 0.0 copy-start.5
  7.9 0.9 copy-done.5
  8.8 0.7 shard_map.128
  9.5 7.7 %all-to-all-start = ((bf16[8,4,3840]{2,1,0:T(4,128)(2,1)}), bf16[8,4,3840]{2,1,0:T(4,128)(2,1)S(1)}, u32[]{:S(2)}, u32[]{:S(2)}) async-start(bf16[8,4,3840]{2,1,0:T(4,128)(2,1)} %shard_map.128), calls=%async_computation | async-start | bytes 491520 | tf_op jit(solution)/shard_map/all_to_all | solution.py:319
  17.2 0.0 copy-start.1
  17.2 0.9 copy-done.1
  18.1 0.0 copy-start.3
  18.1 0.9 copy-done.3
  18.9 0.2 shard_map.129
  19.2 14.7 %psum.14.refs_2_ = f32[4,128]{1,0:T(4,128)S(1)} all-reduce(f32[4,128]{1,0:T(4,128)S(1)} %shard_map.129), channel_id=1, replica_groups=mesh['vol'=8,'y'=8,'z'=8] {'vol'}, use_global_device_ids=true, to_apply=%region_0.1 | all-reduce | flops 512 | bytes 4096 | tf_op jit(solution)/shard_map/psum | solution.py:352
  33.9 0.7 pad_maximum_fusion
  34.6 0.0 all-to-all-done
  34.6 0.1 broadcast_in_dim.12.refs_3_.refs_2_
  34.6 0.0 copy-start.2
  34.6 0.9 copy-done.2
  35.5 0.0 copy-start.4
  35.5 0.9 copy-done.4
  36.4 1.1 shard_map.130
  37.5 14.4 %all-to-all-start.1 = ((bf16[64,4,1536]{2,1,0:T(4,128)(2,1)}), bf16[64,4,1536]{2,1,0:T(4,128)(2,1)S(1)}, u32[]{:S(2)}, u32[]{:S(2)}) async-start(bf16[64,4,1536]{2,1,0:T(4,128)(2,1)} %get-tuple-element.21), calls=%async_computation.1 | async-start | bytes 1572864 | tf_op jit(solution)/shard_map/all_to_all | solution.py:319
  52.0 33.1 %all-gather = bf16[216,4,256]{2,1,0:T(4,128)(2,1)S(1)} all-gather(bf16[27,4,256]{2,1,0:T(4,128)(2,1)} %bitcast.36), channel_id=2, replica_groups=mesh['vol'=8,'y'=8,'z'=8] {'y'}, dimensions={0}, use_global_device_ids=true | all-gather | bytes 497664 | tf_op jit(solution)/shard_map/all_gather | solution.py:323
  85.1 0.2 copy.19
  85.4 0.1 reshape.38.weight_ref
  85.5 0.1 reshape.40.acts_ref
  85.5 0.0 all-to-all-done.1
  85.5 0.2 reshape.39.grads_ref
  85.7 5.0 %shard_map.131 = bf16[8,8,32,128]{3,2,1,0:T(8,128)(2,1)} custom-call(s32[1]{0:T(128)} %bitcast.4.base_ref, bf16[256,1536]{1,0:T(8,128)(2,1)S(1)} %reshape.39.grads_ref, bf16[32,3840]{1,0:T(8,128)(2,1)S(1)} %reshape.40.acts_ref), custom_call_target="tpu_custom_call" | custom-call | flops 1000 | bytes 1000 | tf_op jit(solution)/shard_map/pallas_call | solution.py:366
  90.7 15.3 %all-to-all-start.3 = ((bf16[64,32,128]{2,1,0:T(8,128)(2,1)}), bf16[64,32,128]{2,1,0:T(8,128)(2,1)S(1)}, u32[]{:S(2)}, u32[]{:S(2)}) async-start(bf16[64,32,128]{2,1,0:T(8,128)(2,1)} %bitcast.16), calls=%async_computation.3 | async-start | bytes 1048576 | tf_op jit(solution)/shard_map/all_to_all | solution.py:319
  106.0 0.0 copy-done.6
  106.1 4.8 %shard_map.132 = bf16[8,4,3840]{2,1,0:T(4,128)(2,1)} custom-call(s32[1]{0:T(128)} %bitcast.4.base_ref, bf16[864,256]{1,0:T(8,128)(2,1)S(1)} %reshape.38.weight_ref, bf16[256,1536]{1,0:T(8,128)(2,1)S(1)} %reshape.39.grads_ref), custom_call_target="tpu_custom_call" | custom-call | flops 1000 | bytes 1000 | tf_op jit(solution)/shard_map/pallas_call | solution.py:374
  110.9 20.3 %all-gather.3.cloned.1.call-done.lower_ref.upper_ref = bf16[12288,256]{1,0:T(8,128)(2,1)} async-done(((bf16[192,256]{1,0:T(8,128)(2,1)}), bf16[12288,256]{1,0:T(8,128)(2,1)}) %all-gather.3.cloned.1.call-update) | async-done | bytes 6291472 | tf_op jit(solution)/shard_map/all_gather | solution.py:345
  131.3 0.0 all-to-all-done.3
  131.3 4.3 %all-to-all-start.2 = ((bf16[8,4,3840]{2,1,0:T(4,128)(2,1)}), bf16[8,4,3840]{2,1,0:T(4,128)(2,1)S(1)}, u32[]{:S(2)}, u32[]{:S(2)}) async-start(bf16[8,4,3840]{2,1,0:T(4,128)(2,1)} %shard_map.132), calls=%async_computation.2 | async-start | bytes 491520 | tf_op jit(solution)/shard_map/all_to_all | solution.py:319
  135.5 0.7 slice_reduce_fusion
  136.2 0.1 convert_reduce_fusion
  136.3 0.1 copy.17
  136.4 0.6 reshape.42
  137.1 0.0 copy-start
  137.1 2.8 %copy-done = bf16[12288,256]{1,0:T(8,128)(2,1)S(1)} copy-done((bf16[12288,256]{1,0:T(8,128)(2,1)S(1)}, bf16[12288,256]{1,0:T(8,128)(2,1)}, u32[]{:S(2)}) %copy-start) | copy-done | bytes 6291480
  139.9 9.1 %shard_map.133 = (f32[4,12288]{1,0:T(4,128)S(1)}, f32[4,128]{1,0:T(4,128)S(1)}) custom-call(bf16[216,256]{1,0:T(8,128)(2,1)S(1)} %get-tuple-element.36.low_ref, bf16[216,256]{1,0:T(8,128)(2,1)S(1)} %get-tuple-element.35.high_ref, bf16[12288,256]{1,0:T(8,128)(2,1)S(1)} %copy-done, bf16[12288,256]{1,0:T(8,128)(2,1)S(1)} %copy-done), custom_call_target="tpu_custom_call" | custom-call | flops 1000 | bytes 1000 | tf_op jit(solution)/shard_map/pallas_call | solution.py:383
  149.0 13.3 %psum.15.refs_1_ = f32[4,128]{1,0:T(4,128)S(1)} all-reduce(f32[4,128]{1,0:T(4,128)S(1)} %get-tuple-element.29), channel_id=1, replica_groups=mesh['vol'=8,'y'=8,'z'=8] {'vol'}, use_global_device_ids=true, to_apply=%region_1.2 | all-reduce | flops 512 | bytes 4096 | tf_op jit(solution)/shard_map/psum | solution.py:404
  162.3 0.9 shard_map.134
  163.2 0.0 all-to-all-done.2.parts_ref
  163.2 0.7 shard_map.135
  (2 shorter events, 0.1 us)
Async XLA Ops:
  7.2 98.8 %copy-start.6 = (bf16[27,4,256]{2,1,0:T(4,128)(2,1)S(1)}, bf16[27,4,256]{2,1,0:T(4,128)(2,1)}, u32[]{:S(2)}) copy-start(bf16[27,4,256]{2,1,0:T(4,128)(2,1)} %param.10) | copy-start | bytes 165892
  7.2 124.1 %all-gather.3.cloned.1.call-start = ((), (), s32[]{:S(2)}) async-start(), calls=%async_computation.4 | async-start | bytes 6389760 | tf_op jit(solution)/shard_map/all_gather | solution.py:345
  7.9 0.9 copy-start.5
  9.5 25.1 %all-to-all-start = ((bf16[8,4,3840]{2,1,0:T(4,128)(2,1)}), bf16[8,4,3840]{2,1,0:T(4,128)(2,1)S(1)}, u32[]{:S(2)}, u32[]{:S(2)}) async-start(bf16[8,4,3840]{2,1,0:T(4,128)(2,1)} %shard_map.128), calls=%async_computation | async-start | bytes 491520 | tf_op jit(solution)/shard_map/all_to_all | solution.py:319
  17.2 0.9 copy-start.1
  18.1 0.9 copy-start.3
  34.6 0.9 copy-start.2
  35.5 0.9 copy-start.4
  37.5 48.0 %all-to-all-start.1 = ((bf16[64,4,1536]{2,1,0:T(4,128)(2,1)}), bf16[64,4,1536]{2,1,0:T(4,128)(2,1)S(1)}, u32[]{:S(2)}, u32[]{:S(2)}) async-start(bf16[64,4,1536]{2,1,0:T(4,128)(2,1)} %get-tuple-element.21), calls=%async_computation.1 | async-start | bytes 1572864 | tf_op jit(solution)/shard_map/all_to_all | solution.py:319
  90.7 40.6 %all-to-all-start.3 = ((bf16[64,32,128]{2,1,0:T(8,128)(2,1)}), bf16[64,32,128]{2,1,0:T(8,128)(2,1)S(1)}, u32[]{:S(2)}, u32[]{:S(2)}) async-start(bf16[64,32,128]{2,1,0:T(8,128)(2,1)} %bitcast.16), calls=%async_computation.3 | async-start | bytes 1048576 | tf_op jit(solution)/shard_map/all_to_all | solution.py:319
  131.3 31.9 %all-to-all-start.2 = ((bf16[8,4,3840]{2,1,0:T(4,128)(2,1)}), bf16[8,4,3840]{2,1,0:T(4,128)(2,1)S(1)}, u32[]{:S(2)}, u32[]{:S(2)}) async-start(bf16[8,4,3840]{2,1,0:T(4,128)(2,1)} %shard_map.132), calls=%async_computation.2 | async-start | bytes 491520 | tf_op jit(solution)/shard_map/all_to_all | solution.py:319
  137.1 2.8 %copy-start = (bf16[12288,256]{1,0:T(8,128)(2,1)S(1)}, bf16[12288,256]{1,0:T(8,128)(2,1)}, u32[]{:S(2)}) copy-start(bf16[12288,256]{1,0:T(8,128)(2,1)} %all-gather.3.cloned.1.call-done.lower_ref.upper_ref) | copy-start | bytes 18874372
Sparse Core Ops, SparseCore 0:
  11.1 120.1 all-gather.2

commit v6 on v5

--- a/solution.py
+++ b/solution.py
@@ -135,7 +135,9 @@
             out_ref[:, z * PLANE : (z + 1) * PLANE] = cells
             total = total + lane_sum(cells)
             squares = squares + lane_sum(cells * cells)
-        sums_ref[...] = in_lanes([total, squares])
+        row = in_lanes([total, squares])
+        for vol in range(sums_ref.shape[0]):
+            sums_ref[vol] = row
 
 
 def backward_kernel(base_ref, weight_ref, grads_ref, out_ref, terms):
@@ -220,8 +222,7 @@
     return row
 
 
-def from_lanes(sums_ref, count):
-    total = sums_ref[...]
+def from_lanes(total, count):
     lane = iota((OWN, 128), 1)
     return [
         jnp.sum(jnp.where(lane == index, total, 0.0), axis=1, keepdims=True)
@@ -254,7 +255,7 @@
 
 
 def grad_kernel(counted, saved_ref, upstream_ref, sums_ref, params_ref, packed_ref, means_ref):
-    saved_sum, square_sum, upstream_sum, product_sum = from_lanes(sums_ref, 4)
+    saved_sum, square_sum, upstream_sum, product_sum = from_lanes(sums_ref[...], 4)
     mean = saved_sum / counted
     var = square_sum / counted - mean * mean
     inverse = lax.rsqrt(var + EPSILON)
@@ -291,7 +292,10 @@
 
 
 def relu_kernel(counted, conv_ref, sums_ref, params_ref, out_ref):
-    first_sum, square_sum = from_lanes(sums_ref, 2)
+    total = sums_ref[0]
+    for vol in range(1, sums_ref.shape[0]):
+        total = total + sums_ref[vol]
+    first_sum, square_sum = from_lanes(total, 2)
     mean = first_sum / counted
     var = square_sum / counted - mean * mean
     scale = params_ref[0][:, :1] * lax.rsqrt(var + EPSILON)
@@ -335,7 +339,8 @@
     weight_two,
     gain_two,
 ):
-    counted = lax.axis_size("vol") * CELLS
+    volumes = lax.axis_size("vol")
+    counted = volumes * CELLS
     base = (lax.axis_index("y") * BLOCK).astype(jnp.int32).reshape(1)
     params = jnp.broadcast_to(
         jnp.stack([gain_one, bias_one, gain_two])[:, :, None], (3, OWN, 128)
@@ -378,11 +383,12 @@
         [pltpu.VMEM((ROWS, BLOCK), F32)],
     )(base, second, grads)
 
-    cells, input_parts = lax.optimization_barrier((cells, input_parts))
+    after = input_parts, filter_parts
+    cells, after = lax.optimization_barrier((cells, after))
     input_parts = exchange(input_parts, "y")
     conv_out, sums_one = pl.pallas_call(
         forward_kernel,
-        out_shape=(shaped((OWN, CELLS), F32), shaped((OWN, 128), F32)),
+        out_shape=(shaped((OWN, CELLS), F32), shaped((volumes, OWN, 128), F32)),
         grid=(HALF,),
         in_specs=[
             pl.BlockSpec((27 * 2 * OWN, CH), lambda at: (0, 0)),
@@ -392,16 +398,16 @@
         ],
         out_specs=(
             pl.BlockSpec((OWN, CELLS), lambda at: (0, 0)),
-            pl.BlockSpec((OWN, 128), lambda at: (0, 0)),
+            pl.BlockSpec((volumes, OWN, 128), lambda at: (0, 0, 0)),
         ),
         scratch_shapes=[
             pltpu.VMEM((27 * 2 * OWN, PLANE), F32),
             pltpu.VMEM((2 * OWN, (HALF + 2) * PLANE), F32),
         ],
-        compiler_params=PARAMS,
+        compiler_params=pltpu.CompilerParams(vmem_limit_bytes=58 * 1024 * 1024),
         cost_estimate=pl.CostEstimate(flops=1000, bytes_accessed=1000, transcendentals=0),
     )(low, high, cells, cells)
-    sums_one = lax.psum(sums_one, "vol")
+    sums_one = exchange(sums_one, "vol")
     activation = call(
         lambda *refs: relu_kernel(counted, *refs), shaped((OWN, CELLS), BF16), [VMEM] * 3
     )(conv_out, sums_one, params)

time: 172 us -> 173 us (level)
  blocking collectives: 61.1 us -> 64.2 us
    all_gather x1, waiting for transfers between devices: 20.3 us -> 0.01 us  [shards(): cells = lax.all_gather(fwd_input[0].T, ('y', 'z'), axis=0, tiled=True)]
    all_to_all x4, waiting for transfers between devices: 0.01 us -> 18.9 us  [exchange(): return lax.all_to_all(value, axes, 0, 0, tiled=True)]
    all_to_all x0 -> x1, blocking collectives: none -> 15.9 us  [exchange(): return lax.all_to_all(value, axes, 0, 0, tiled=True)]
    psum x1 -> x0, blocking collectives: 13.3 us -> none  [shards(): sums_one = lax.psum(sums_one, 'vol')]
    pallas_call x1, Pallas kernels: 9.14 us -> 11.2 us  [shards(): pl.pallas_call(forward_kernel, out_shape=(shaped((OWN, CELLS), F32), shap...]
    unnamed x14, local copies, waits for them, and re-layouts: 7.24 us -> 5.38 us
  transfers between devices with their start and end apart: 5 -> 5, of which waited for: 1 -> 2; matrix products, arithmetic and copies ran while one was open for 2% -> 2% of each run, Pallas kernels for 13% -> 7%
where the time goes in v6:
time: 173 us; the launch traced here: 172 us
  blocking collectives  64.2 us (37%)
  starting transfers between devices  41.4 us (24%)
  Pallas kernels  23.9 us (14%)
  waiting for transfers between devices  19.6 us (11%)
  between operations  14.1 us (8%)
  local copies, waits for them, and re-layouts  8.22 us (5%)
    all_to_all x4, starting transfers between devices, exchange(): return lax.all_to_all(value, axes, 0, 0, tiled=True)  41.4 us
    all_gather x1, blocking collectives, gathered(): filters = lax.all_gather(filters, 'y', axis=0, tiled=False)  33.5 us
    all_to_all x4, waiting for transfers between devices, exchange(): return lax.all_to_all(value, axes, 0, 0, tiled=True)  18.9 us
    all_to_all x1, blocking collectives, exchange(): return lax.all_to_all(value, axes, 0, 0, tiled=True)  15.9 us
    psum x1, blocking collectives, shards(): sums_two = lax.psum(sums_two, 'vol')  14.7 us
    pallas_call x1, Pallas kernels, shards(): pl.pallas_call(forward_kernel, out_shape=(shaped((OWN, CELLS), F32), shap...  11.2 us
    unnamed x14, local copies, waits for them, and re-layouts  5.38 us
    pallas_call x1, Pallas kernels, shards(): call(filter_kernel, shaped((8, NY, GROUP, 128), BF16), [SMEM, VMEM, VMEM]...  4.98 us
  transfers between devices with their start and end apart: 5, of which 2 were waited for; matrix products, arithmetic and copies ran while one was open for 2% of the time, Pallas kernels for 7%

profile of v6, /device:TPU:1, one launch (start us, length us, event | category | flops | bytes accessed | tf_op | source)
XLA Modules:
  0.0 172.3 jit_solution(2310477256991862761)
XLA Ops:
  7.2 0.0 copy-start.6
  7.2 0.0 all-gather.3.cloned.1.call-start
  7.2 0.7 all-gather.3.cloned.1.call-update
  7.9 0.0 copy-start.5
  7.9 0.9 copy-done.5
  8.8 0.7 shard_map.128
  9.5 7.7 %all-to-all-start = ((bf16[8,4,3840]{2,1,0:T(4,128)(2,1)}), bf16[8,4,3840]{2,1,0:T(4,128)(2,1)S(1)}, u32[]{:S(2)}, u32[]{:S(2)}) async-start(bf16[8,4,3840]{2,1,0:T(4,128)(2,1)} %shard_map.128), calls=%async_computation | async-start | bytes 491520 | tf_op jit(solution)/shard_map/all_to_all | solution.py:323
  17.2 0.0 copy-start
  17.2 0.9 copy-done
  18.1 0.0 copy-start.2
  18.1 0.9 copy-done.2
  19.0 0.2 shard_map.129
  19.2 14.7 %psum.7.refs_2_ = f32[4,128]{1,0:T(4,128)S(1)} all-reduce(f32[4,128]{1,0:T(4,128)S(1)} %shard_map.129), channel_id=1, replica_groups=mesh['vol'=8,'y'=8,'z'=8] {'vol'}, use_global_device_ids=true, to_apply=%region_0.1 | all-reduce | flops 512 | bytes 4096 | tf_op jit(solution)/shard_map/psum | solution.py:357
  33.9 0.7 pad_maximum_fusion
  34.6 0.0 all-to-all-done
  34.6 0.1 broadcast_in_dim.12.refs_3_.refs_2_
  34.7 0.0 copy-start.1
  34.7 0.9 copy-done.1
  35.5 0.0 copy-start.3
  35.5 0.9 copy-done.3
  36.4 1.1 shard_map.130
  37.6 14.4 %all-to-all-start.1 = ((bf16[64,4,1536]{2,1,0:T(4,128)(2,1)}), bf16[64,4,1536]{2,1,0:T(4,128)(2,1)S(1)}, u32[]{:S(2)}, u32[]{:S(2)}) async-start(bf16[64,4,1536]{2,1,0:T(4,128)(2,1)} %get-tuple-element.20), calls=%async_computation.1 | async-start | bytes 1572864 | tf_op jit(solution)/shard_map/all_to_all | solution.py:323
  52.0 33.5 %all-gather = bf16[216,4,256]{2,1,0:T(4,128)(2,1)S(1)} all-gather(bf16[27,4,256]{2,1,0:T(4,128)(2,1)} %bitcast.36), channel_id=2, replica_groups=mesh['vol'=8,'y'=8,'z'=8] {'y'}, dimensions={0}, use_global_device_ids=true | all-gather | bytes 497664 | tf_op jit(solution)/shard_map/all_gather | solution.py:327
  85.6 0.2 copy.19
  85.8 0.1 reshape.38.weight_ref
  85.9 0.1 reshape.40.acts_ref
  86.0 0.0 all-to-all-done.1
  86.0 0.2 reshape.39.grads_ref
  86.2 5.0 %shard_map.131 = bf16[8,8,32,128]{3,2,1,0:T(8,128)(2,1)} custom-call(s32[1]{0:T(128)} %bitcast.4.base_ref, bf16[256,1536]{1,0:T(8,128)(2,1)S(1)} %reshape.39.grads_ref, bf16[32,3840]{1,0:T(8,128)(2,1)S(1)} %reshape.40.acts_ref), custom_call_target="tpu_custom_call" | custom-call | flops 1000 | bytes 1000 | tf_op jit(solution)/shard_map/pallas_call | solution.py:371
  91.2 4.2 %shard_map.132 = bf16[8,4,3840]{2,1,0:T(4,128)(2,1)S(1)} custom-call(s32[1]{0:T(128)} %bitcast.4.base_ref, bf16[864,256]{1,0:T(8,128)(2,1)S(1)} %reshape.38.weight_ref, bf16[256,1536]{1,0:T(8,128)(2,1)S(1)} %reshape.39.grads_ref), custom_call_target="tpu_custom_call" | custom-call | flops 1000 | bytes 1000 | tf_op jit(solution)/shard_map/pallas_call | solution.py:379
  95.3 15.9 %all_to_all.25.parts_ref = bf16[8,4,3840]{2,1,0:T(4,128)(2,1)S(1)} all-to-all(bf16[8,4,3840]{2,1,0:T(4,128)(2,1)S(1)} %shard_map.132), channel_id=1, replica_groups=mesh['vol'=8,'y'=8,'z'=8] {'y'}, dimensions={0} | all-to-all | bytes 491520 | tf_op jit(solution)/shard_map/all_to_all | solution.py:323
  111.3 13.8 %all-to-all-start.2 = ((bf16[64,32,128]{2,1,0:T(8,128)(2,1)}), bf16[64,32,128]{2,1,0:T(8,128)(2,1)S(1)}, u32[]{:S(2)}, u32[]{:S(2)}) async-start(bf16[64,32,128]{2,1,0:T(8,128)(2,1)} %bitcast.14), calls=%async_computation.2 | async-start | bytes 1048576 | tf_op jit(solution)/shard_map/all_to_all | solution.py:323
  125.0 0.0 copy-done.6
  125.0 0.7 pad_bitcast_fusion
  125.8 0.7 slice_reduce_fusion
  126.5 0.7 shard_map.135
  127.2 15.0 %all-to-all-done.2 = bf16[64,32,128]{2,1,0:T(8,128)(2,1)S(1)} async-done(((bf16[64,32,128]{2,1,0:T(8,128)(2,1)}), bf16[64,32,128]{2,1,0:T(8,128)(2,1)S(1)}, u32[]{:S(2)}, u32[]{:S(2)}) %all-to-all-start.2) | async-done | bytes 524320 | tf_op jit(solution)/shard_map/all_to_all | solution.py:323
  142.2 0.1 convert_reduce_fusion
  142.3 0.0 all-gather.3.cloned.1.call-done.lower_ref.upper_ref
  142.3 11.2 %shard_map.133 = (f32[4,12288]{1,0:T(4,128)}, f32[8,4,128]{2,1,0:T(4,128)}) custom-call(bf16[216,256]{1,0:T(8,128)(2,1)} %get-tuple-element.34.low_ref, bf16[216,256]{1,0:T(8,128)(2,1)} %get-tuple-element.33.high_ref, bf16[12288,256]{1,0:T(8,128)(2,1)} %all-gather.3.cloned.1.call-done.lower_ref.upper_ref, ...), custom_call_target="tpu_custom_call" | custom-call | flops 1000 | bytes 1000 | tf_op jit(solution)/shard_map/pallas_call | solution.py:389
  153.5 5.6 %all-to-all-start.3 = ((f32[8,4,128]{2,1,0:T(4,128)}), f32[8,4,128]{2,1,0:T(4,128)S(1)}, u32[]{:S(2)}, u32[]{:S(2)}) async-start(f32[8,4,128]{2,1,0:T(4,128)} %get-tuple-element.29), calls=%async_computation.3 | async-start | bytes 32768 | tf_op jit(solution)/shard_map/all_to_all | solution.py:323
  159.1 0.1 copy.17
  159.2 0.6 reshape.42
  159.8 3.9 %all-to-all-done.3.refs_1_ = f32[8,4,128]{2,1,0:T(4,128)S(1)} async-done(((f32[8,4,128]{2,1,0:T(4,128)}), f32[8,4,128]{2,1,0:T(4,128)S(1)}, u32[]{:S(2)}, u32[]{:S(2)}) %all-to-all-start.3) | async-done | bytes 16416 | tf_op jit(solution)/shard_map/all_to_all | solution.py:323
  163.7 0.0 copy-start.4
  163.7 0.9 copy-done.4
  164.6 0.9 shard_map.134
  (1 shorter events, 0.0 us)
Async XLA Ops:
  7.2 117.9 %copy-start.6 = (bf16[27,4,256]{2,1,0:T(4,128)(2,1)S(1)}, bf16[27,4,256]{2,1,0:T(4,128)(2,1)}, u32[]{:S(2)}) copy-start(bf16[27,4,256]{2,1,0:T(4,128)(2,1)} %param.10) | copy-start | bytes 165892
  7.2 135.1 %all-gather.3.cloned.1.call-start = ((), (), s32[]{:S(2)}) async-start(), calls=%async_computation.5 | async-start | bytes 6389760 | tf_op jit(solution)/shard_map/all_gather | solution.py:350
  7.9 0.9 copy-start.5
  9.5 25.1 %all-to-all-start = ((bf16[8,4,3840]{2,1,0:T(4,128)(2,1)}), bf16[8,4,3840]{2,1,0:T(4,128)(2,1)S(1)}, u32[]{:S(2)}, u32[]{:S(2)}) async-start(bf16[8,4,3840]{2,1,0:T(4,128)(2,1)} %shard_map.128), calls=%async_computation | async-start | bytes 491520 | tf_op jit(solution)/shard_map/all_to_all | solution.py:323
  17.2 0.9 copy-start
  18.1 0.9 copy-start.2
  34.7 0.9 copy-start.1
  35.5 0.9 copy-start.3
  37.6 48.4 %all-to-all-start.1 = ((bf16[64,4,1536]{2,1,0:T(4,128)(2,1)}), bf16[64,4,1536]{2,1,0:T(4,128)(2,1)S(1)}, u32[]{:S(2)}, u32[]{:S(2)}) async-start(bf16[64,4,1536]{2,1,0:T(4,128)(2,1)} %get-tuple-element.20), calls=%async_computation.1 | async-start | bytes 1572864 | tf_op jit(solution)/shard_map/all_to_all | solution.py:323
  111.3 30.9 %all-to-all-start.2 = ((bf16[64,32,128]{2,1,0:T(8,128)(2,1)}), bf16[64,32,128]{2,1,0:T(8,128)(2,1)S(1)}, u32[]{:S(2)}, u32[]{:S(2)}) async-start(bf16[64,32,128]{2,1,0:T(8,128)(2,1)} %bitcast.14), calls=%async_computation.2 | async-start | bytes 1048576 | tf_op jit(solution)/shard_map/all_to_all | solution.py:323
  153.5 10.2 %all-to-all-start.3 = ((f32[8,4,128]{2,1,0:T(4,128)}), f32[8,4,128]{2,1,0:T(4,128)S(1)}, u32[]{:S(2)}, u32[]{:S(2)}) async-start(f32[8,4,128]{2,1,0:T(4,128)} %get-tuple-element.29), calls=%async_computation.3 | async-start | bytes 32768 | tf_op jit(solution)/shard_map/all_to_all | solution.py:323
  163.7 0.9 copy-start.4
Sparse Core Ops, SparseCore 0:
  11.1 113.8 all-gather.2

commit v7 on v6

--- a/solution.py
+++ b/solution.py
@@ -375,7 +375,6 @@
         [pltpu.VMEM((1024, BLOCK), BF16), pltpu.VMEM((CH, 1024), BF16)],
     )(base, grads, acts)
     second, filter_parts = lax.optimization_barrier((second, filter_parts))
-    filter_parts = exchange(filter_parts.reshape(8 * NY, GROUP, 128), ("vol", "y"))
     input_parts = call(
         backward_kernel,
         shaped((NY, OWN, SPAN), BF16),
@@ -383,9 +382,11 @@
         [pltpu.VMEM((ROWS, BLOCK), F32)],
     )(base, second, grads)
 
-    after = input_parts, filter_parts
-    cells, after = lax.optimization_barrier((cells, after))
     input_parts = exchange(input_parts, "y")
+
+    filter_parts, _ = lax.optimization_barrier((filter_parts, input_parts))
+    filter_parts = exchange(filter_parts.reshape(8 * NY, GROUP, 128), ("vol", "y"))
+    cells, _ = lax.optimization_barrier((cells, input_parts))
     conv_out, sums_one = pl.pallas_call(
         forward_kernel,
         out_shape=(shaped((OWN, CELLS), F32), shaped((volumes, OWN, 128), F32)),

time: 173 us -> 173 us (level)
  no operation moved by 1% of the time
where the time goes in v7:
time: 173 us; the launch traced here: 172 us
  blocking collectives  64.2 us (37%)
  starting transfers between devices  41.4 us (24%)
  Pallas kernels  23.9 us (14%)
  waiting for transfers between devices  19.6 us (11%)
  between operations  14.1 us (8%)
  local copies, waits for them, and re-layouts  8.22 us (5%)
    all_to_all x4, starting transfers between devices, exchange(): return lax.all_to_all(value, axes, 0, 0, tiled=True)  41.4 us
    all_gather x1, blocking collectives, gathered(): filters = lax.all_gather(filters, 'y', axis=0, tiled=False)  33.5 us
    all_to_all x4, waiting for transfers between devices, exchange(): return lax.all_to_all(value, axes, 0, 0, tiled=True)  18.9 us
    all_to_all x1, blocking collectives, exchange(): return lax.all_to_all(value, axes, 0, 0, tiled=True)  15.9 us
    psum x1, blocking collectives, shards(): sums_two = lax.psum(sums_two, 'vol')  14.7 us
    pallas_call x1, Pallas kernels, shards(): pl.pallas_call(forward_kernel, out_shape=(shaped((OWN, CELLS), F32), shap...  11.2 us
    unnamed x14, local copies, waits for them, and re-layouts  5.38 us
    pallas_call x1, Pallas kernels, shards(): call(filter_kernel, shaped((8, NY, GROUP, 128), BF16), [SMEM, VMEM, VMEM]...  4.98 us
  transfers between devices with their start and end apart: 5, of which 2 were waited for; matrix products, arithmetic and copies ran while one was open for 2% of the time, Pallas kernels for 7%

profile of v7, /device:TPU:1, one launch (start us, length us, event | category | flops | bytes accessed | tf_op | source)
XLA Modules:
  0.0 172.3 jit_solution(2310477256991862761)
XLA Ops:
  7.2 0.0 copy-start.6
  7.2 0.0 all-gather.3.cloned.1.call-start
  7.2 0.7 all-gather.3.cloned.1.call-update
  7.9 0.0 copy-start.5
  7.9 0.9 copy-done.5
  8.8 0.7 shard_map.128
  9.5 7.7 %all-to-all-start = ((bf16[8,4,3840]{2,1,0:T(4,128)(2,1)}), bf16[8,4,3840]{2,1,0:T(4,128)(2,1)S(1)}, u32[]{:S(2)}, u32[]{:S(2)}) async-start(bf16[8,4,3840]{2,1,0:T(4,128)(2,1)} %shard_map.128), calls=%async_computation | async-start | bytes 491520 | tf_op jit(solution)/shard_map/all_to_all | solution.py:323
  17.2 0.0 copy-start
  17.2 0.9 copy-done
  18.1 0.0 copy-start.2
  18.1 0.9 copy-done.2
  19.0 0.2 shard_map.129
  19.2 14.7 %psum.7.refs_2_ = f32[4,128]{1,0:T(4,128)S(1)} all-reduce(f32[4,128]{1,0:T(4,128)S(1)} %shard_map.129), channel_id=1, replica_groups=mesh['vol'=8,'y'=8,'z'=8] {'vol'}, use_global_device_ids=true, to_apply=%region_0.1 | all-reduce | flops 512 | bytes 4096 | tf_op jit(solution)/shard_map/psum | solution.py:357
  33.9 0.7 pad_maximum_fusion
  34.6 0.0 all-to-all-done
  34.6 0.1 broadcast_in_dim.12.refs_3_.refs_2_
  34.7 0.0 copy-start.1
  34.7 0.9 copy-done.1
  35.5 0.0 copy-start.3
  35.5 0.9 copy-done.3
  36.4 1.1 shard_map.130
  37.6 14.4 %all-to-all-start.1 = ((bf16[64,4,1536]{2,1,0:T(4,128)(2,1)}), bf16[64,4,1536]{2,1,0:T(4,128)(2,1)S(1)}, u32[]{:S(2)}, u32[]{:S(2)}) async-start(bf16[64,4,1536]{2,1,0:T(4,128)(2,1)} %get-tuple-element.21), calls=%async_computation.1 | async-start | bytes 1572864 | tf_op jit(solution)/shard_map/all_to_all | solution.py:323
  52.0 33.5 %all-gather = bf16[216,4,256]{2,1,0:T(4,128)(2,1)S(1)} all-gather(bf16[27,4,256]{2,1,0:T(4,128)(2,1)} %bitcast.36), channel_id=2, replica_groups=mesh['vol'=8,'y'=8,'z'=8] {'y'}, dimensions={0}, use_global_device_ids=true | all-gather | bytes 497664 | tf_op jit(solution)/shard_map/all_gather | solution.py:327
  85.6 0.2 copy.19
  85.8 0.1 reshape.38.weight_ref
  85.9 0.1 reshape.40.acts_ref
  86.0 0.0 all-to-all-done.1
  86.0 0.2 reshape.39.grads_ref
  86.2 5.0 %shard_map.131 = bf16[8,8,32,128]{3,2,1,0:T(8,128)(2,1)} custom-call(s32[1]{0:T(128)} %bitcast.4.base_ref, bf16[256,1536]{1,0:T(8,128)(2,1)S(1)} %reshape.39.grads_ref, bf16[32,3840]{1,0:T(8,128)(2,1)S(1)} %reshape.40.acts_ref), custom_call_target="tpu_custom_call" | custom-call | flops 1000 | bytes 1000 | tf_op jit(solution)/shard_map/pallas_call | solution.py:371
  91.2 4.2 %shard_map.132 = bf16[8,4,3840]{2,1,0:T(4,128)(2,1)S(1)} custom-call(s32[1]{0:T(128)} %bitcast.4.base_ref, bf16[864,256]{1,0:T(8,128)(2,1)S(1)} %reshape.38.weight_ref, bf16[256,1536]{1,0:T(8,128)(2,1)S(1)} %reshape.39.grads_ref), custom_call_target="tpu_custom_call" | custom-call | flops 1000 | bytes 1000 | tf_op jit(solution)/shard_map/pallas_call | solution.py:378
  95.3 15.9 %all_to_all.25.parts_ref = bf16[8,4,3840]{2,1,0:T(4,128)(2,1)S(1)} all-to-all(bf16[8,4,3840]{2,1,0:T(4,128)(2,1)S(1)} %shard_map.132), channel_id=1, replica_groups=mesh['vol'=8,'y'=8,'z'=8] {'y'}, dimensions={0} | all-to-all | bytes 491520 | tf_op jit(solution)/shard_map/all_to_all | solution.py:323
  111.3 13.8 %all-to-all-start.4 = ((bf16[64,32,128]{2,1,0:T(8,128)(2,1)}), bf16[64,32,128]{2,1,0:T(8,128)(2,1)S(1)}, u32[]{:S(2)}, u32[]{:S(2)}) async-start(bf16[64,32,128]{2,1,0:T(8,128)(2,1)} %bitcast.16), calls=%async_computation.4 | async-start | bytes 1048576 | tf_op jit(solution)/shard_map/all_to_all | solution.py:323
  125.0 0.0 copy-done.6
  125.0 0.7 pad_bitcast_fusion
  125.8 0.7 slice_reduce_fusion
  126.5 0.7 shard_map.135
  127.2 15.0 %all-to-all-done.4 = bf16[64,32,128]{2,1,0:T(8,128)(2,1)S(1)} async-done(((bf16[64,32,128]{2,1,0:T(8,128)(2,1)}), bf16[64,32,128]{2,1,0:T(8,128)(2,1)S(1)}, u32[]{:S(2)}, u32[]{:S(2)}) %all-to-all-start.4) | async-done | bytes 524320 | tf_op jit(solution)/shard_map/all_to_all | solution.py:323
  142.2 0.1 convert_reduce_fusion
  142.3 0.0 all-gather.3.cloned.1.call-done.lower_ref.upper_ref
  142.3 11.2 %shard_map.133 = (f32[4,12288]{1,0:T(4,128)}, f32[8,4,128]{2,1,0:T(4,128)}) custom-call(bf16[216,256]{1,0:T(8,128)(2,1)} %get-tuple-element.36.low_ref, bf16[216,256]{1,0:T(8,128)(2,1)} %get-tuple-element.35.high_ref, bf16[12288,256]{1,0:T(8,128)(2,1)} %all-gather.3.cloned.1.call-done.lower_ref.upper_ref, ...), custom_call_target="tpu_custom_call" | custom-call | flops 1000 | bytes 1000 | tf_op jit(solution)/shard_map/pallas_call | solution.py:390
  153.5 5.6 %all-to-all-start.3 = ((f32[8,4,128]{2,1,0:T(4,128)}), f32[8,4,128]{2,1,0:T(4,128)S(1)}, u32[]{:S(2)}, u32[]{:S(2)}) async-start(f32[8,4,128]{2,1,0:T(4,128)} %get-tuple-element.29), calls=%async_computation.3 | async-start | bytes 32768 | tf_op jit(solution)/shard_map/all_to_all | solution.py:323
  159.1 0.1 copy.17
  159.2 0.6 reshape.42
  159.8 3.9 %all-to-all-done.3.refs_1_ = f32[8,4,128]{2,1,0:T(4,128)S(1)} async-done(((f32[8,4,128]{2,1,0:T(4,128)}), f32[8,4,128]{2,1,0:T(4,128)S(1)}, u32[]{:S(2)}, u32[]{:S(2)}) %all-to-all-start.3) | async-done | bytes 16416 | tf_op jit(solution)/shard_map/all_to_all | solution.py:323
  163.7 0.0 copy-start.4
  163.7 0.9 copy-done.4
  164.6 0.9 shard_map.134
  (1 shorter events, 0.0 us)
Async XLA Ops:
  7.2 117.9 %copy-start.6 = (bf16[27,4,256]{2,1,0:T(4,128)(2,1)S(1)}, bf16[27,4,256]{2,1,0:T(4,128)(2,1)}, u32[]{:S(2)}) copy-start(bf16[27,4,256]{2,1,0:T(4,128)(2,1)} %param.10) | copy-start | bytes 165892
  7.2 135.1 %all-gather.3.cloned.1.call-start = ((), (), s32[]{:S(2)}) async-start(), calls=%async_computation.5 | async-start | bytes 6389760 | tf_op jit(solution)/shard_map/all_gather | solution.py:350
  7.9 0.9 copy-start.5
  9.5 25.1 %all-to-all-start = ((bf16[8,4,3840]{2,1,0:T(4,128)(2,1)}), bf16[8,4,3840]{2,1,0:T(4,128)(2,1)S(1)}, u32[]{:S(2)}, u32[]{:S(2)}) async-start(bf16[8,4,3840]{2,1,0:T(4,128)(2,1)} %shard_map.128), calls=%async_computation | async-start | bytes 491520 | tf_op jit(solution)/shard_map/all_to_all | solution.py:323
  17.2 0.9 copy-start
  18.1 0.9 copy-start.2
  34.7 0.9 copy-start.1
  35.5 0.9 copy-start.3
  37.6 48.4 %all-to-all-start.1 = ((bf16[64,4,1536]{2,1,0:T(4,128)(2,1)}), bf16[64,4,1536]{2,1,0:T(4,128)(2,1)S(1)}, u32[]{:S(2)}, u32[]{:S(2)}) async-start(bf16[64,4,1536]{2,1,0:T(4,128)(2,1)} %get-tuple-element.21), calls=%async_computation.1 | async-start | bytes 1572864 | tf_op jit(solution)/shard_map/all_to_all | solution.py:323
  111.3 30.9 %all-to-all-start.4 = ((bf16[64,32,128]{2,1,0:T(8,128)(2,1)}), bf16[64,32,128]{2,1,0:T(8,128)(2,1)S(1)}, u32[]{:S(2)}, u32[]{:S(2)}) async-start(bf16[64,32,128]{2,1,0:T(8,128)(2,1)} %bitcast.16), calls=%async_computation.4 | async-start | bytes 1048576 | tf_op jit(solution)/shard_map/all_to_all | solution.py:323
  153.5 10.2 %all-to-all-start.3 = ((f32[8,4,128]{2,1,0:T(4,128)}), f32[8,4,128]{2,1,0:T(4,128)S(1)}, u32[]{:S(2)}, u32[]{:S(2)}) async-start(f32[8,4,128]{2,1,0:T(4,128)} %get-tuple-element.29), calls=%async_computation.3 | async-start | bytes 32768 | tf_op jit(solution)/shard_map/all_to_all | solution.py:323
  163.7 0.9 copy-start.4
Sparse Core Ops, SparseCore 0:
  11.1 113.8 all-gather.2

commit v8 on v5

--- a/solution.py
+++ b/solution.py
@@ -378,7 +378,8 @@
         [pltpu.VMEM((ROWS, BLOCK), F32)],
     )(base, second, grads)
 
-    cells, input_parts = lax.optimization_barrier((cells, input_parts))
+    cells, _ = lax.optimization_barrier((cells, (input_parts, filter_parts)))
+    input_parts, _ = lax.optimization_barrier((input_parts, filter_parts))
     input_parts = exchange(input_parts, "y")
     conv_out, sums_one = pl.pallas_call(
         forward_kernel,

time: 172 us -> 178 us (1.035)
  waiting for transfers between devices: 21 us -> 27.5 us
    all_to_all x4, waiting for transfers between devices: 0.01 us -> 26.8 us  [exchange(): return lax.all_to_all(value, axes, 0, 0, tiled=True)]
    all_gather x1, waiting for transfers between devices: 20.3 us -> 0.01 us  [shards(): cells = lax.all_gather(fwd_input[0].T, ('y', 'z'), axis=0, tiled=True)]
  transfers between devices with their start and end apart: 5 -> 5, of which waited for: 1 -> 2; matrix products, arithmetic and copies ran while one was open for 2% -> 2% of each run, Pallas kernels for 13% -> 7%
where the time goes in v8:
time: 178 us; the launch traced here: 177 us
  blocking collectives  61.8 us (35%)
  starting transfers between devices  41.2 us (23%)
  waiting for transfers between devices  27.5 us (15%)
  Pallas kernels  22.6 us (13%)
  between operations  14.1 us (8%)
  local copies, waits for them, and re-layouts  9.38 us (5%)
    all_to_all x4, starting transfers between devices, exchange(): return lax.all_to_all(value, axes, 0, 0, tiled=True)  41.1 us
    all_gather x1, blocking collectives, gathered(): filters = lax.all_gather(filters, 'y', axis=0, tiled=False)  33.1 us
    all_to_all x4, waiting for transfers between devices, exchange(): return lax.all_to_all(value, axes, 0, 0, tiled=True)  26.8 us
    psum x1, blocking collectives, shards(): sums_two = lax.psum(sums_two, 'vol')  14.7 us
    psum x1, blocking collectives, shards(): sums_one = lax.psum(sums_one, 'vol')  14 us
    pallas_call x1, Pallas kernels, shards(): pl.pallas_call(forward_kernel, out_shape=(shaped((OWN, CELLS), F32), shap...  9.13 us
    unnamed x14, local copies, waits for them, and re-layouts  7.24 us
    pallas_call x1, Pallas kernels, shards(): call(filter_kernel, shaped((8, NY, GROUP, 128), BF16), [SMEM, VMEM, VMEM]...  4.98 us
  transfers between devices with their start and end apart: 5, of which 2 were waited for; matrix products, arithmetic and copies ran while one was open for 2% of the time, Pallas kernels for 7%

profile of v8, /device:TPU:1, one launch (start us, length us, event | category | flops | bytes accessed | tf_op | source)
XLA Modules:
  0.0 177.4 jit_solution(15113405130783750911)
XLA Ops:
  7.2 0.0 copy-start.6
  7.2 0.0 all-gather.3.cloned.1.call-start
  7.2 0.7 all-gather.3.cloned.1.call-update
  7.9 0.0 copy-start.5
  7.9 0.9 copy-done.5
  8.8 0.7 shard_map.128
  9.5 7.7 %all-to-all-start = ((bf16[8,4,3840]{2,1,0:T(4,128)(2,1)}), bf16[8,4,3840]{2,1,0:T(4,128)(2,1)S(1)}, u32[]{:S(2)}, u32[]{:S(2)}) async-start(bf16[8,4,3840]{2,1,0:T(4,128)(2,1)} %shard_map.128), calls=%async_computation | async-start | bytes 491520 | tf_op jit(solution)/shard_map/all_to_all | solution.py:319
  17.2 0.0 copy-start.1
  17.2 0.9 copy-done.1
  18.1 0.0 copy-start.3
  18.1 0.9 copy-done.3
  18.9 0.2 shard_map.129
  19.2 14.7 %psum.14.refs_2_ = f32[4,128]{1,0:T(4,128)S(1)} all-reduce(f32[4,128]{1,0:T(4,128)S(1)} %shard_map.129), channel_id=1, replica_groups=mesh['vol'=8,'y'=8,'z'=8] {'vol'}, use_global_device_ids=true, to_apply=%region_0.1 | all-reduce | flops 512 | bytes 4096 | tf_op jit(solution)/shard_map/psum | solution.py:352
  33.9 0.7 pad_maximum_fusion
  34.6 0.0 all-to-all-done
  34.6 0.1 broadcast_in_dim.12.refs_3_.refs_2_
  34.6 0.0 copy-start.2
  34.6 0.9 copy-done.2
  35.5 0.0 copy-start.4
  35.5 0.9 copy-done.4
  36.4 1.1 shard_map.130
  37.5 14.4 %all-to-all-start.1 = ((bf16[64,4,1536]{2,1,0:T(4,128)(2,1)}), bf16[64,4,1536]{2,1,0:T(4,128)(2,1)S(1)}, u32[]{:S(2)}, u32[]{:S(2)}) async-start(bf16[64,4,1536]{2,1,0:T(4,128)(2,1)} %get-tuple-element.21), calls=%async_computation.1 | async-start | bytes 1572864 | tf_op jit(solution)/shard_map/all_to_all | solution.py:319
  52.0 33.1 %all-gather = bf16[216,4,256]{2,1,0:T(4,128)(2,1)S(1)} all-gather(bf16[27,4,256]{2,1,0:T(4,128)(2,1)} %bitcast.36), channel_id=2, replica_groups=mesh['vol'=8,'y'=8,'z'=8] {'y'}, dimensions={0}, use_global_device_ids=true | all-gather | bytes 497664 | tf_op jit(solution)/shard_map/all_gather | solution.py:323
  85.1 0.2 copy.19
  85.4 0.1 reshape.38.weight_ref
  85.5 0.1 reshape.40.acts_ref
  85.5 0.0 all-to-all-done.1
  85.5 0.2 reshape.39.grads_ref
  85.7 5.0 %shard_map.131 = bf16[8,8,32,128]{3,2,1,0:T(8,128)(2,1)} custom-call(s32[1]{0:T(128)} %bitcast.4.base_ref, bf16[256,1536]{1,0:T(8,128)(2,1)S(1)} %reshape.39.grads_ref, bf16[32,3840]{1,0:T(8,128)(2,1)S(1)} %reshape.40.acts_ref), custom_call_target="tpu_custom_call" | custom-call | flops 1000 | bytes 1000 | tf_op jit(solution)/shard_map/pallas_call | solution.py:366
  90.7 15.3 %all-to-all-start.2 = ((bf16[64,32,128]{2,1,0:T(8,128)(2,1)}), bf16[64,32,128]{2,1,0:T(8,128)(2,1)S(1)}, u32[]{:S(2)}, u32[]{:S(2)}) async-start(bf16[64,32,128]{2,1,0:T(8,128)(2,1)} %bitcast.14), calls=%async_computation.2 | async-start | bytes 1048576 | tf_op jit(solution)/shard_map/all_to_all | solution.py:319
  106.0 0.0 copy-done.6
  106.1 4.8 %shard_map.132 = bf16[8,4,3840]{2,1,0:T(4,128)(2,1)} custom-call(s32[1]{0:T(128)} %bitcast.4.base_ref, bf16[864,256]{1,0:T(8,128)(2,1)S(1)} %reshape.38.weight_ref, bf16[256,1536]{1,0:T(8,128)(2,1)S(1)} %reshape.39.grads_ref), custom_call_target="tpu_custom_call" | custom-call | flops 1000 | bytes 1000 | tf_op jit(solution)/shard_map/pallas_call | solution.py:374
  110.9 18.1 %all-to-all-done.2 = bf16[64,32,128]{2,1,0:T(8,128)(2,1)S(1)} async-done(((bf16[64,32,128]{2,1,0:T(8,128)(2,1)}), bf16[64,32,128]{2,1,0:T(8,128)(2,1)S(1)}, u32[]{:S(2)}, u32[]{:S(2)}) %all-to-all-start.2) | async-done | bytes 524320 | tf_op jit(solution)/shard_map/all_to_all | solution.py:319
  129.0 3.8 %all-to-all-start.3 = ((bf16[8,4,3840]{2,1,0:T(4,128)(2,1)}), bf16[8,4,3840]{2,1,0:T(4,128)(2,1)S(1)}, u32[]{:S(2)}, u32[]{:S(2)}) async-start(bf16[8,4,3840]{2,1,0:T(4,128)(2,1)} %shard_map.132), calls=%async_computation.3 | async-start | bytes 491520 | tf_op jit(solution)/shard_map/all_to_all | solution.py:319
  132.8 0.7 slice_reduce_fusion
  133.5 0.1 convert_reduce_fusion
  133.6 0.1 copy.17
  133.7 0.6 reshape.42
  134.3 8.7 %all-to-all-done.3.parts_ref = bf16[8,4,3840]{2,1,0:T(4,128)(2,1)S(1)} async-done(((bf16[8,4,3840]{2,1,0:T(4,128)(2,1)}), bf16[8,4,3840]{2,1,0:T(4,128)(2,1)S(1)}, u32[]{:S(2)}, u32[]{:S(2)}) %all-to-all-start.3) | async-done | bytes 245792 | tf_op jit(solution)/shard_map/all_to_all | solution.py:319
  143.0 0.7 shard_map.135
  143.7 0.0 all-gather.3.cloned.1.call-done.lower_ref.upper_ref
  143.7 0.0 copy-start
  143.7 2.8 %copy-done = bf16[12288,256]{1,0:T(8,128)(2,1)S(1)} copy-done((bf16[12288,256]{1,0:T(8,128)(2,1)S(1)}, bf16[12288,256]{1,0:T(8,128)(2,1)}, u32[]{:S(2)}) %copy-start) | copy-done | bytes 6291480
  146.5 9.1 %shard_map.133 = (f32[4,12288]{1,0:T(4,128)S(1)}, f32[4,128]{1,0:T(4,128)S(1)}) custom-call(bf16[216,256]{1,0:T(8,128)(2,1)S(1)} %get-tuple-element.36.low_ref, bf16[216,256]{1,0:T(8,128)(2,1)S(1)} %get-tuple-element.35.high_ref, bf16[12288,256]{1,0:T(8,128)(2,1)S(1)} %copy-done, bf16[12288,256]{1,0:T(8,128)(2,1)S(1)} %copy-done), custom_call_target="tpu_custom_call" | custom-call | flops 1000 | bytes 1000 | tf_op jit(solution)/shard_map/pallas_call | solution.py:384
  155.7 14.0 %psum.15.refs_1_ = f32[4,128]{1,0:T(4,128)S(1)} all-reduce(f32[4,128]{1,0:T(4,128)S(1)} %get-tuple-element.30), channel_id=1, replica_groups=mesh['vol'=8,'y'=8,'z'=8] {'vol'}, use_global_device_ids=true, to_apply=%region_1.2 | all-reduce | flops 512 | bytes 4096 | tf_op jit(solution)/shard_map/psum | solution.py:405
  169.7 0.9 shard_map.134
  (2 shorter events, 0.1 us)
Async XLA Ops:
  7.2 98.8 %copy-start.6 = (bf16[27,4,256]{2,1,0:T(4,128)(2,1)S(1)}, bf16[27,4,256]{2,1,0:T(4,128)(2,1)}, u32[]{:S(2)}) copy-start(bf16[27,4,256]{2,1,0:T(4,128)(2,1)} %param.10) | copy-start | bytes 165892
  7.2 136.6 %all-gather.3.cloned.1.call-start = ((), (), s32[]{:S(2)}) async-start(), calls=%async_computation.4 | async-start | bytes 6389760 | tf_op jit(solution)/shard_map/all_gather | solution.py:345
  7.9 0.9 copy-start.5
  9.5 25.1 %all-to-all-start = ((bf16[8,4,3840]{2,1,0:T(4,128)(2,1)}), bf16[8,4,3840]{2,1,0:T(4,128)(2,1)S(1)}, u32[]{:S(2)}, u32[]{:S(2)}) async-start(bf16[8,4,3840]{2,1,0:T(4,128)(2,1)} %shard_map.128), calls=%async_computation | async-start | bytes 491520 | tf_op jit(solution)/shard_map/all_to_all | solution.py:319
  17.2 0.9 copy-start.1
  18.1 0.9 copy-start.3
  34.6 0.9 copy-start.2
  35.5 0.9 copy-start.4
  37.5 48.0 %all-to-all-start.1 = ((bf16[64,4,1536]{2,1,0:T(4,128)(2,1)}), bf16[64,4,1536]{2,1,0:T(4,128)(2,1)S(1)}, u32[]{:S(2)}, u32[]{:S(2)}) async-start(bf16[64,4,1536]{2,1,0:T(4,128)(2,1)} %get-tuple-element.21), calls=%async_computation.1 | async-start | bytes 1572864 | tf_op jit(solution)/shard_map/all_to_all | solution.py:319
  90.7 38.3 %all-to-all-start.2 = ((bf16[64,32,128]{2,1,0:T(8,128)(2,1)}), bf16[64,32,128]{2,1,0:T(8,128)(2,1)S(1)}, u32[]{:S(2)}, u32[]{:S(2)}) async-start(bf16[64,32,128]{2,1,0:T(8,128)(2,1)} %bitcast.14), calls=%async_computation.2 | async-start | bytes 1048576 | tf_op jit(solution)/shard_map/all_to_all | solution.py:319
  129.0 14.0 %all-to-all-start.3 = ((bf16[8,4,3840]{2,1,0:T(4,128)(2,1)}), bf16[8,4,3840]{2,1,0:T(4,128)(2,1)S(1)}, u32[]{:S(2)}, u32[]{:S(2)}) async-start(bf16[8,4,3840]{2,1,0:T(4,128)(2,1)} %shard_map.132), calls=%async_computation.3 | async-start | bytes 491520 | tf_op jit(solution)/shard_map/all_to_all | solution.py:319
  143.7 2.8 %copy-start = (bf16[12288,256]{1,0:T(8,128)(2,1)S(1)}, bf16[12288,256]{1,0:T(8,128)(2,1)}, u32[]{:S(2)}) copy-start(bf16[12288,256]{1,0:T(8,128)(2,1)} %all-gather.3.cloned.1.call-done.lower_ref.upper_ref) | copy-start | bytes 18874372
Sparse Core Ops, SparseCore 0:
  11.1 120.1 all-gather.2
